TPU v7x, 32 devices: a whole 2x2x4 slice. The times are simulated.
32 devices in a mesh: dp: 4 (over z), ctx: 2 (over x), head: 4 (over y, core).
Axes of the slice: x: 2, y: 2, z: 4, core: 2. Of those that a mesh axis runs over, the one named last changes fastest.
Arguments:
- tokens: bfloat16 [8, 1024, 1024], P('dp', ('ctx', 'head')), may hold values from -6 to 6
- cotangent: bfloat16 [8, 1024, 1024], P('dp', ('ctx', 'head')), may hold values from -6 to 6
- w_qkv: bfloat16 [1024, 3072], P(('dp', 'ctx')), may hold values from -0.1875 to 0.1875
- w_attn_out: bfloat16 [1024, 1024], P(('dp', 'ctx')), may hold values from -3 to 3
- w_in: bfloat16 [1024, 5248], P(('dp', 'ctx')), may hold values from -0.1875 to 0.1875
- w_mlp_out: bfloat16 [2624, 1024], P(('dp', 'ctx')), may hold values from -0.125 to 0.125
- norm_gain1: bfloat16 [1024], P(('dp', 'ctx')), may hold values from 0.5 to 1.5
- norm_gain2: bfloat16 [1024], P(('dp', 'ctx')), may hold values from 0.5 to 1.5
Outputs:
- out: bfloat16 [8, 1024, 1024], P('dp', ('ctx', 'head'))
- grad_tokens: float32 [8, 1024, 1024], P('dp', ('ctx', 'head'))
- grad_qkv: float32 [1024, 3072], P(('dp', 'ctx'), 'head')
- grad_attn_out: float32 [1024, 1024], P(('dp', 'ctx'), 'head')
- grad_in: float32 [1024, 5248], P(('dp', 'ctx'), 'head')
- grad_mlp_out: float32 [2624, 1024], P(('dp', 'ctx'), 'head')
- grad_gain1: float32 [1024], P(('dp', 'ctx', 'head'))
- grad_gain2: float32 [1024], P(('dp', 'ctx', 'head'))
All inputs are finite; a program needn't handle non-finite values.
Results may differ from a plain program's by a relative error of at most 0.023.
Values may be sent and summed in bfloat16 or wider, within the bound.
No kernel may reach another device: no remote copies, remote signals or barrier semaphores. Data moves between devices by JAX's collectives and lax.ppermute only.
A program may use at most 192 MiB of HBM per device.

v0:
```python
import math

import jax
import jax.numpy as jnp
from jax import lax
from jax.sharding import PartitionSpec as P

HD = 64


EPSILON = 1e-05
ROPE_BASE = 160000.0


def normalize(values):
    centre = jnp.mean(values, axis=-1, keepdims=True)
    shifted = values - centre
    spread = jnp.mean(shifted * shifted, axis=-1, keepdims=True)
    factor = lax.rsqrt(spread + EPSILON)
    return (shifted * factor, factor)


def norm_back(grad_normed, normed, factor):
    grad_centre = jnp.mean(grad_normed, axis=-1, keepdims=True)
    grad_along = jnp.mean(grad_normed * normed, axis=-1, keepdims=True)
    return (grad_normed - grad_centre - normed * grad_along) * factor


def rope_tables(positions, half_size):
    frequency = jnp.exp(
        jnp.arange(half_size, dtype=jnp.float32) * (-math.log(ROPE_BASE) / half_size)
    )
    angles = positions[:, None] * frequency[None, :]
    return (jnp.cos(angles), jnp.sin(angles))


def rotate(values, cosine, sine_table, direction):
    half_size = cosine.shape[-1]
    first_half = values[..., :half_size]
    second_half = values[..., half_size:]
    cos_part = cosine[:, None, :]
    sin_part = sine_table[:, None, :] * direction
    return jnp.concatenate(
        [
            first_half * cos_part - second_half * sin_part,
            second_half * cos_part + first_half * sin_part,
        ],
        axis=-1,
    )


def block_scores(queries4, keys_block, scale):
    keys4 = keys_block.reshape(
        keys_block.shape[0], keys_block.shape[1], queries4.shape[2], queries4.shape[3]
    )
    return (
        jnp.einsum("sqgd,skgd->sgqk", queries4, keys4, preferred_element_type=jnp.float32) * scale
    )


def attend_forward(queries4, keys_all, values_all, key_rows, scale):
    seqs_here, query_rows, groups, head_size = queries4.shape
    turns = keys_all.shape[1] // key_rows

    def statistics(turn, carry):
        row_peak, row_total = carry
        keys_block = lax.dynamic_slice_in_dim(keys_all, turn * key_rows, key_rows, 1)
        scores = block_scores(queries4, keys_block, scale)
        new_peak = jnp.maximum(row_peak, jnp.max(scores, axis=-1))
        row_total = row_total * jnp.exp(row_peak - new_peak) + jnp.sum(
            jnp.exp(scores - new_peak[..., None]), axis=-1
        )
        return (new_peak, row_total)

    start_peak = jnp.full((seqs_here, groups, query_rows), -1e30, jnp.float32)
    row_peak, row_total = lax.fori_loop(
        0, turns, statistics, (start_peak, jnp.zeros_like(start_peak))
    )
    log_total = row_peak + jnp.log(row_total)

    def accumulate(turn, running):
        keys_block = lax.dynamic_slice_in_dim(keys_all, turn * key_rows, key_rows, 1)
        values_block = lax.dynamic_slice_in_dim(values_all, turn * key_rows, key_rows, 1).reshape(
            seqs_here, key_rows, groups, head_size
        )
        weights = jnp.exp(block_scores(queries4, keys_block, scale) - log_total[..., None]).astype(
            jnp.bfloat16
        )
        return running + jnp.einsum(
            "sgqk,skgd->sqgd", weights, values_block, preferred_element_type=jnp.float32
        )

    attended = lax.fori_loop(
        0, turns, accumulate, jnp.zeros((seqs_here, query_rows, groups, head_size), jnp.float32)
    )
    return (attended, log_total)


def attend_backward(queries4, keys_all, values_all, grad_out4, log_total, along, key_rows, scale):
    seqs_here, query_rows, groups, head_size = queries4.shape
    length = keys_all.shape[1]
    width_group = groups * head_size
    turns = length // key_rows

    def step_back(turn, carry):
        grad_queries, grad_keys, grad_values = carry
        keys_block = lax.dynamic_slice_in_dim(keys_all, turn * key_rows, key_rows, 1)
        keys4 = keys_block.reshape(seqs_here, key_rows, groups, head_size)
        values4 = lax.dynamic_slice_in_dim(values_all, turn * key_rows, key_rows, 1).reshape(
            seqs_here, key_rows, groups, head_size
        )
        weights = jnp.exp(block_scores(queries4, keys_block, scale) - log_total[..., None])
        grad_weights = jnp.einsum(
            "sqgd,skgd->sgqk", grad_out4, values4, preferred_element_type=jnp.float32
        )
        grad_scores = (weights * (grad_weights - along[..., None])).astype(jnp.bfloat16)
        grad_queries = grad_queries + jnp.einsum(
            "sgqk,skgd->sqgd", grad_scores, keys4, preferred_element_type=jnp.float32
        )
        key_part = (
            jnp.einsum("sgqk,sqgd->skgd", grad_scores, queries4, preferred_element_type=jnp.float32)
            * scale
        )
        value_part = jnp.einsum(
            "sgqk,sqgd->skgd",
            weights.astype(jnp.bfloat16),
            grad_out4,
            preferred_element_type=jnp.float32,
        )
        grad_keys = lax.dynamic_update_slice_in_dim(
            grad_keys, key_part.reshape(seqs_here, key_rows, width_group), turn * key_rows, 1
        )
        grad_values = lax.dynamic_update_slice_in_dim(
            grad_values, value_part.reshape(seqs_here, key_rows, width_group), turn * key_rows, 1
        )
        return (grad_queries, grad_keys, grad_values)

    start = (
        jnp.zeros((seqs_here, query_rows, groups, head_size), jnp.float32),
        jnp.zeros((seqs_here, length, width_group), jnp.float32),
        jnp.zeros((seqs_here, length, width_group), jnp.float32),
    )
    grad_queries, grad_keys, grad_values = lax.fori_loop(0, turns, step_back, start)
    return (grad_queries * scale, grad_keys, grad_values)


def local(tokens, cotangent, w_qkv, w_attn_out, w_in, w_mlp_out, norm_gain1, norm_gain2):
    seqs_here, block_rows, width = tokens.shape
    count_rows = seqs_here * block_rows
    heads_all = width // HD
    head_devices = lax.axis_size("head")
    group_devices = lax.axis_size(("dp", "ctx"))
    groups = heads_all // head_devices
    width_group = groups * HD
    scale = HD ** (-0.5)
    ff_width = w_in.shape[1] // 2
    full_qkv, full_out, full_in, full_mlp, gain_one, gain_two = (
        lax.all_gather(w_qkv, ("dp", "ctx"), axis=0, tiled=True),
        lax.all_gather(w_attn_out, ("dp", "ctx"), axis=0, tiled=True),
        lax.all_gather(w_in, ("dp", "ctx"), axis=0, tiled=True),
        lax.all_gather(w_mlp_out, ("dp", "ctx"), axis=0, tiled=True),
        lax.all_gather(norm_gain1, ("dp", "ctx"), axis=0, tiled=True),
        lax.all_gather(norm_gain2, ("dp", "ctx"), axis=0, tiled=True),
    )
    x_in = tokens.astype(jnp.float32).reshape(count_rows, width)
    normed1, factor1 = normalize(x_in)
    lowered1 = (normed1 * gain_one.astype(jnp.float32)).astype(jnp.bfloat16)
    projected = jnp.dot(lowered1, full_qkv, preferred_element_type=jnp.float32).reshape(
        seqs_here, block_rows, 3, heads_all, HD
    )
    first_pos = (lax.axis_index("ctx") * head_devices + lax.axis_index("head")) * block_rows
    positions = (first_pos + jnp.arange(block_rows, dtype=jnp.int32)).astype(jnp.float32)
    cosine, sine_table = rope_tables(positions, HD // 2)
    queries = (
        rotate(projected[:, :, 0], cosine, sine_table, 1.0)
        .astype(jnp.bfloat16)
        .reshape(seqs_here, block_rows, width)
    )
    keys_local = (
        rotate(projected[:, :, 1], cosine, sine_table, 1.0)
        .astype(jnp.bfloat16)
        .reshape(seqs_here, block_rows, width)
    )
    values_local = projected[:, :, 2].astype(jnp.bfloat16).reshape(seqs_here, block_rows, width)
    queries_h, keys_h, values_h = (
        lax.all_to_all(queries, "head", split_axis=2, concat_axis=1, tiled=True),
        lax.all_to_all(keys_local, "head", split_axis=2, concat_axis=1, tiled=True),
        lax.all_to_all(values_local, "head", split_axis=2, concat_axis=1, tiled=True),
    )
    query_rows = queries_h.shape[1]
    queries4 = queries_h.reshape(seqs_here, query_rows, groups, HD)
    keys_all, values_all = (
        lax.all_gather(keys_h, "ctx", axis=1, tiled=True),
        lax.all_gather(values_h, "ctx", axis=1, tiled=True),
    )
    key_rows = math.gcd(keys_all.shape[1], 1024)
    attended, log_total = attend_forward(queries4, keys_all, values_all, key_rows, scale)
    attended_low = attended.astype(jnp.bfloat16).reshape(seqs_here, query_rows, width_group)
    back_rows = lax.all_to_all(
        attended_low, "head", split_axis=1, concat_axis=2, tiled=True
    ).reshape(count_rows, width)
    residual = x_in + jnp.dot(back_rows, full_out, preferred_element_type=jnp.float32)
    normed2, factor2 = normalize(residual)
    lowered2 = (normed2 * gain_two.astype(jnp.float32)).astype(jnp.bfloat16)
    lifted = jnp.dot(lowered2, full_in, preferred_element_type=jnp.float32)
    first_part = lifted[:, :ff_width]
    second_part = lifted[:, ff_width:]
    activated, gelu_pullback = jax.vjp(
        lambda entries: jax.nn.gelu(entries, approximate=False), first_part
    )
    mixed = (activated * second_part).astype(jnp.bfloat16)
    result = (residual + jnp.dot(mixed, full_mlp, preferred_element_type=jnp.float32)).astype(
        jnp.bfloat16
    )
    full_qkv, full_out, full_in, full_mlp, gain_one, gain_two = (
        lax.all_gather(w_qkv, ("dp", "ctx"), axis=0, tiled=True),
        lax.all_gather(w_attn_out, ("dp", "ctx"), axis=0, tiled=True),
        lax.all_gather(w_in, ("dp", "ctx"), axis=0, tiled=True),
        lax.all_gather(w_mlp_out, ("dp", "ctx"), axis=0, tiled=True),
        lax.all_gather(norm_gain1, ("dp", "ctx"), axis=0, tiled=True),
        lax.all_gather(norm_gain2, ("dp", "ctx"), axis=0, tiled=True),
    )
    keys_all, values_all = (
        lax.all_gather(keys_h, "ctx", axis=1, tiled=True),
        lax.all_gather(values_h, "ctx", axis=1, tiled=True),
    )
    grad_top = cotangent.reshape(count_rows, width)
    grad_mlp = jnp.einsum("nf,nd->fd", mixed, grad_top, preferred_element_type=jnp.float32)
    grad_mixed = jnp.einsum("nd,fd->nf", grad_top, full_mlp, preferred_element_type=jnp.float32)
    grad_first = gelu_pullback(grad_mixed * second_part)[0]
    grad_lifted = jnp.concatenate([grad_first, grad_mixed * activated], axis=-1).astype(
        jnp.bfloat16
    )
    grad_inner = jnp.einsum("nd,nf->df", lowered2, grad_lifted, preferred_element_type=jnp.float32)
    grad_lowered2 = jnp.einsum(
        "nf,df->nd", grad_lifted, full_in, preferred_element_type=jnp.float32
    )
    grad_two = jnp.sum(grad_lowered2 * normed2, axis=0)
    grad_residual = grad_top.astype(jnp.float32) + norm_back(
        grad_lowered2 * gain_two.astype(jnp.float32), normed2, factor2
    )
    grad_branch = grad_residual.astype(jnp.bfloat16)
    grad_outproj = jnp.einsum(
        "nd,ne->de", back_rows, grad_branch, preferred_element_type=jnp.float32
    )
    grad_attended = jnp.einsum(
        "ne,de->nd", grad_branch, full_out, preferred_element_type=jnp.float32
    ).astype(jnp.bfloat16)
    grad_attended_h = lax.all_to_all(
        grad_attended.reshape(seqs_here, block_rows, width),
        "head",
        split_axis=2,
        concat_axis=1,
        tiled=True,
    )
    grad_out4 = grad_attended_h.reshape(seqs_here, query_rows, groups, HD)
    along = jnp.transpose(jnp.sum(grad_out4.astype(jnp.float32) * attended, axis=-1), (0, 2, 1))
    grad_queries, grad_keys_all, grad_values_all = attend_backward(
        queries4, keys_all, values_all, grad_out4, log_total, along, key_rows, scale
    )
    grad_keys_sum, grad_values_sum = (
        lax.psum_scatter(
            grad_keys_all.astype(jnp.bfloat16), "ctx", scatter_dimension=1, tiled=True
        ).astype(jnp.float32),
        lax.psum_scatter(
            grad_values_all.astype(jnp.bfloat16), "ctx", scatter_dimension=1, tiled=True
        ).astype(jnp.float32),
    )
    grad_q_low = grad_queries.astype(jnp.bfloat16).reshape(seqs_here, query_rows, width_group)
    grad_q_tok, grad_k_tok, grad_v_tok = (
        lax.all_to_all(grad_q_low, "head", split_axis=1, concat_axis=2, tiled=True),
        lax.all_to_all(
            grad_keys_sum.astype(jnp.bfloat16), "head", split_axis=1, concat_axis=2, tiled=True
        ),
        lax.all_to_all(
            grad_values_sum.astype(jnp.bfloat16), "head", split_axis=1, concat_axis=2, tiled=True
        ),
    )
    unrot_q = rotate(
        grad_q_tok.astype(jnp.float32).reshape(seqs_here, block_rows, heads_all, HD),
        cosine,
        sine_table,
        -1.0,
    )
    unrot_k = rotate(
        grad_k_tok.astype(jnp.float32).reshape(seqs_here, block_rows, heads_all, HD),
        cosine,
        sine_table,
        -1.0,
    )
    grad_projected = jnp.concatenate(
        [
            unrot_q.reshape(count_rows, width),
            unrot_k.reshape(count_rows, width),
            grad_v_tok.astype(jnp.float32).reshape(count_rows, width),
        ],
        axis=-1,
    ).astype(jnp.bfloat16)
    grad_project = jnp.einsum(
        "nd,nf->df", lowered1, grad_projected, preferred_element_type=jnp.float32
    )
    grad_lowered1 = jnp.einsum(
        "nf,df->nd", grad_projected, full_qkv, preferred_element_type=jnp.float32
    )
    grad_one = jnp.sum(grad_lowered1 * normed1, axis=0)
    grad_input = grad_residual + norm_back(
        grad_lowered1 * gain_one.astype(jnp.float32), normed1, factor1
    )
    pieces_one = grad_one.reshape(group_devices, head_devices, -1)
    pieces_two = grad_two.reshape(group_devices, head_devices, -1)
    part_qkv, part_out, part_in, part_mlp, part_one, part_two = (
        lax.psum_scatter(
            grad_project.astype(jnp.bfloat16), ("dp", "ctx"), scatter_dimension=0, tiled=True
        ).astype(jnp.float32),
        lax.psum_scatter(
            grad_outproj.astype(jnp.bfloat16), ("dp", "ctx"), scatter_dimension=0, tiled=True
        ).astype(jnp.float32),
        lax.psum_scatter(
            grad_inner.astype(jnp.bfloat16), ("dp", "ctx"), scatter_dimension=0, tiled=True
        ).astype(jnp.float32),
        lax.psum_scatter(
            grad_mlp.astype(jnp.bfloat16), ("dp", "ctx"), scatter_dimension=0, tiled=True
        ).astype(jnp.float32),
        lax.psum_scatter(
            pieces_one.astype(jnp.bfloat16), ("dp", "ctx"), scatter_dimension=0, tiled=True
        ).astype(jnp.float32),
        lax.psum_scatter(
            pieces_two.astype(jnp.bfloat16), ("dp", "ctx"), scatter_dimension=0, tiled=True
        ).astype(jnp.float32),
    )
    final_qkv, final_out, final_in, final_mlp, final_one, final_two = (
        lax.psum_scatter(
            part_qkv.astype(jnp.bfloat16), "head", scatter_dimension=1, tiled=True
        ).astype(jnp.float32),
        lax.psum_scatter(
            part_out.astype(jnp.bfloat16), "head", scatter_dimension=1, tiled=True
        ).astype(jnp.float32),
        lax.psum_scatter(
            part_in.astype(jnp.bfloat16), "head", scatter_dimension=1, tiled=True
        ).astype(jnp.float32),
        lax.psum_scatter(
            part_mlp.astype(jnp.bfloat16), "head", scatter_dimension=1, tiled=True
        ).astype(jnp.float32),
        lax.psum_scatter(
            part_one.astype(jnp.bfloat16), "head", scatter_dimension=1, tiled=True
        ).astype(jnp.float32),
        lax.psum_scatter(
            part_two.astype(jnp.bfloat16), "head", scatter_dimension=1, tiled=True
        ).astype(jnp.float32),
    )
    return (
        result.reshape(seqs_here, block_rows, width),
        grad_input.reshape(seqs_here, block_rows, width),
        final_qkv,
        final_out,
        final_in,
        final_mlp,
        final_one.reshape(-1),
        final_two.reshape(-1),
    )


def solution(mesh):
    in_specs = (
        P("dp", ("ctx", "head"), None),
        P("dp", ("ctx", "head"), None),
        P(("dp", "ctx"), None),
        P(("dp", "ctx"), None),
        P(("dp", "ctx"), None),
        P(("dp", "ctx"), None),
        P(("dp", "ctx")),
        P(("dp", "ctx")),
    )
    out_specs = (
        P("dp", ("ctx", "head"), None),
        P("dp", ("ctx", "head"), None),
        P(("dp", "ctx"), "head"),
        P(("dp", "ctx"), "head"),
        P(("dp", "ctx"), "head"),
        P(("dp", "ctx"), "head"),
        P(("dp", "ctx", "head")),
        P(("dp", "ctx", "head")),
    )
    return jax.shard_map(local, mesh=mesh, in_specs=in_specs, out_specs=out_specs, check_vma=False)
```

profile of v0, /device:TPU:0, one launch (start us, length us, event | category | flops | bytes accessed | tf_op | source)
XLA Modules:
  0.0 1207.7 jit_solution(1914630628178082951)
XLA Ops:
  8.0 22.5 %all-gather = bf16[8,1,128]{2,1,0:T(2,128)(2,1)S(1)} all-gather(bf16[1,1,128]{2,1,0:T(2,128)(2,1)} %bitcast.210), channel_id=1, replica_groups=mesh['dp'=4,'ctx'=2,'head'=4] {'dp','ctx'}, dimensions={0}, use_global_device_ids=true | all-gather | bytes 2304 | tf_op jit(solution)/shard_map/all_gather | solution.py:162
  31.7 1.3 multiply_reduce_fusion.7
  33.2 78.8 %all-gather.9.cloned.1.call-done = bf16[1024,3072]{1,0:T(8,128)(2,1)} async-done(((bf16[128,3072]{1,0:T(8,128)(2,1)}), bf16[1024,3072]{1,0:T(8,128)(2,1)}) %all-gather.9.cloned.1.call-update) | async-done | bytes 6291472 | tf_op jit(solution)/shard_map/all_gather | solution.py:158
  111.9 8.7 copy.91
  120.7 4.8 fusion.15
  127.7 11.4 all_to_all.108
  142.5 11.2 all_to_all.109
  157.4 11.7 all_to_all.110
  169.8 3.9 multiply_reduce_fusion
  173.7 3.7 exponential_reduce_fusion
  177.3 2.1 copy-done
  179.4 3.3 all-gather.11.cloned.1.call-done
  182.8 8.5 fusion.34
  192.4 3.5 all-to-all-start.3
  195.9 19.6 %all-gather.1 = bf16[8,1,128]{2,1,0:T(2,128)(2,1)S(1)} all-gather(bf16[1,1,128]{2,1,0:T(2,128)(2,1)S(1)} %bitcast.211), channel_id=1, replica_groups=mesh['dp'=4,'ctx'=2,'head'=4] {'dp','ctx'}, dimensions={0}, use_global_device_ids=true | all-gather | bytes 2304 | tf_op jit(solution)/shard_map/all_gather | solution.py:163
  216.2 17.9 %all-gather.15.cloned.1.call-done = bf16[1024,1024]{1,0:T(8,128)(2,1)} async-done(((bf16[128,1024]{1,0:T(8,128)(2,1)}), bf16[1024,1024]{1,0:T(8,128)(2,1)}) %all-gather.15.cloned.1.call-update) | async-done | bytes 2097168 | tf_op jit(solution)/shard_map/all_gather | solution.py:159
  234.1 2.4 fusion.35
  236.7 151.9 %all-gather.17.cloned.1.call-done = bf16[1024,5248]{1,0:T(8,128)(2,1)} async-done(((bf16[128,5248]{1,0:T(8,128)(2,1)}), bf16[1024,5248]{1,0:T(8,128)(2,1)}) %all-gather.17.cloned.1.call-update) | async-done | bytes 10747920 | tf_op jit(solution)/shard_map/all_gather | solution.py:160
  388.7 9.1 fusion.32
  397.8 79.0 %all-gather.19.cloned.1.call-done = bf16[2624,1024]{1,0:T(8,128)(2,1)} async-done(((bf16[328,1024]{1,0:T(8,128)(2,1)}), bf16[2624,1024]{1,0:T(8,128)(2,1)}) %all-gather.19.cloned.1.call-update) | async-done | bytes 5373968 | tf_op jit(solution)/shard_map/all_gather | solution.py:161
  476.8 12.1 add_convert_fusion
  488.9 2.4 multiply_convert_fusion.1
  491.2 2.7 copy-done.1
  493.9 5.8 multiply_reduce_fusion.1
  499.8 1.8 multiply_add_fusion.1
  503.6 12.7 %all_to_all.111 = bf16[2,128,1024]{1,0,2:T(2,128)(2,1)S(1)} all-to-all(bf16[2,128,1024]{1,0,2:T(2,128)(2,1)} %copy.104), channel_id=1, replica_groups=mesh['dp'=4,'ctx'=2,'head'=4] {'head'}, dimensions={2} | all-to-all | bytes 1048576 | tf_op jit(solution)/shard_map/all_to_all | solution.py:249
  518.8 8.8 convolution_convert_fusion.4
  527.7 10.1 multiply_convert_fusion
  537.8 3.6 copy.115
  541.5 6.1 multiply_convert_fusion.3
  547.6 3.7 copy.111
  551.4 2.1 convolution_convert_fusion.3
  553.6 5.8 convolution_convert_fusion.1
  559.5 6.4 fusion.10
  566.9 3.5 all-to-all-start.5
  571.7 40.2 %all-reduce.11.cloned.1.call-done = (bf16[2,1024,256]{2,0,1:T(2,128)(2,1)}, bf16[2,1024,256]{2,0,1:T(2,128)(2,1)}) async-done(((bf16[2,1024,256]{2,0,1:T(2,128)(2,1)}, bf16[2,1024,256]{2,0,1:T(2,128)(2,1)}), (bf16[2,1024,256]{2,0,1:T(2,128)(2,1)}, bf16[2,1024,256]{2,0,1:T(2,128)(2,1)})) %all-reduce.11.cloned.1.call-update) | async-done | bytes 2097168
  611.8 2.2 constant_dynamic-slice_fusion.5
  614.0 4.2 all-to-all-start.6
  619.3 2.6 copy.109
  621.9 2.2 constant_dynamic-slice_fusion.4
  624.2 2.9 all-to-all-done.6
  627.1 3.6 all-to-all-start.7
  633.0 2.6 copy.113
  635.6 1.9 subtract_convert_fusion
  637.5 1.3 copy.114
  638.9 1.3 copy.110
  641.1 1.3 copy.122
  644.7 6.0 multiply_reduce_fusion.2
  650.7 4.5 convolution_convert_fusion.2
  655.3 9.1 convolution_convert_fusion
  664.4 19.2 %reduce-scatter.17.cloned.1.call-done = bf16[128,1024]{1,0:T(8,128)(2,1)} async-done(((bf16[1024,1024]{1,0:T(8,128)(2,1)}), bf16[128,1024]{1,0:T(8,128)(2,1)}) %reduce-scatter.17.cloned.1.call-update) | async-done | bytes 262160 | tf_op jit(solution)/shard_map/reduce_scatter | solution.py:315
  683.8 107.4 %reduce-scatter.23.cloned.1.call-done = bf16[328,1024]{1,0:T(8,128)(2,1)} async-done(((bf16[2624,1024]{1,0:T(8,128)(2,1)}), bf16[328,1024]{1,0:T(8,128)(2,1)}) %reduce-scatter.23.cloned.1.call-update) | async-done | bytes 671760 | tf_op jit(solution)/shard_map/reduce_scatter | solution.py:321
  791.2 121.1 %reduce-scatter.13.cloned.1.call-done = bf16[128,3072]{1,0:T(8,128)(2,1)} async-done(((bf16[1024,3072]{1,0:T(8,128)(2,1)}), bf16[128,3072]{1,0:T(8,128)(2,1)}) %reduce-scatter.13.cloned.1.call-update) | async-done | bytes 786448 | tf_op jit(solution)/shard_map/reduce_scatter | solution.py:312
  912.4 184.5 %reduce-scatter.21.cloned.1.call-done = bf16[128,5248]{1,0:T(8,128)(2,1)} async-done(((bf16[1024,5248]{1,0:T(8,128)(2,1)}), bf16[128,5248]{1,0:T(8,128)(2,1)}) %reduce-scatter.21.cloned.1.call-update) | async-done | bytes 1343504 | tf_op jit(solution)/shard_map/reduce_scatter | solution.py:318
  1096.9 2.5 copy.123
  1100.7 5.4 fusion.9
  1106.2 35.2 %all-reduce.6 = (bf16[8,4,32]{2,1,0:T(4,128)(2,1)S(1)}, bf16[8,4,32]{2,1,0:T(4,128)(2,1)S(1)}) all-reduce(bf16[8,4,32]{2,1,0:T(4,128)(2,1)S(1)} %convert_element_type.237, bf16[8,4,32]{2,1,0:T(4,128)(2,1)S(1)} %convert_element_type.239), channel_id=12, replica_groups=mesh['dp'=4,'ctx'=2,'head'=4] {'dp','ctx'}, use_global_device_ids=true, to_apply=%region_22.0.clone | all-reduce | flops 2048 | bytes 8192
  1142.7 5.7 all-reduce.7
  1150.7 2.7 multiply_add_fusion
  1153.4 1.5 convert_element_type.231
  1154.9 1.7 convert_element_type.235
  1156.5 12.9 %reduce-scatter.15.cloned.1.call-done = bf16[128,768]{1,0:T(8,128)(2,1)} async-done(((bf16[128,3072]{1,0:T(8,128)(2,1)}), bf16[128,768]{1,0:T(8,128)(2,1)}) %reduce-scatter.15.cloned.1.call-update) | async-done | bytes 196624 | tf_op jit(solution)/shard_map/reduce_scatter | solution.py:332
  1169.5 1.7 convert_element_type.229
  1171.2 27.6 %reduce-scatter.27.cloned.1.call-done = bf16[1312,128]{1,0:T(8,128)(2,1)} async-done(((bf16[5248,128]{1,0:T(8,128)(2,1)}), bf16[1312,128]{1,0:T(8,128)(2,1)}) %reduce-scatter.27.cloned.1.call-update) | async-done | bytes 335888
  (131 shorter events, 34.7 us)
Async XLA Ops:
  7.2 104.8 %all-gather.9.cloned.1.call-start = ((), (), s32[]{:S(2)}) async-start(), calls=%async_computation.16 | async-start | bytes 7077888 | tf_op jit(solution)/shard_map/all_gather | solution.py:158
  7.9 161.9 %all-gather.13.cloned.1.call-start = ((), (), s32[]{:S(2)}) async-start(), calls=%async_computation.18 | async-start | bytes 1572864 | tf_op jit(solution)/shard_map/all_gather | solution.py:193
  111.9 8.7 copy-start.3
  125.4 1.6 copy-start.9
  140.6 42.2 %all-gather.11.cloned.1.call-start = ((), (), s32[]{:S(2)}) async-start(), calls=%async_computation.17 | async-start | bytes 1572864 | tf_op jit(solution)/shard_map/all_gather | solution.py:194
  155.1 78.9 %all-gather.15.cloned.1.call-start = ((), (), s32[]{:S(2)}) async-start(), calls=%async_computation.19 | async-start | bytes 2359296 | tf_op jit(solution)/shard_map/all_gather | solution.py:159
  155.7 233.0 %all-gather.17.cloned.1.call-start = ((), (), s32[]{:S(2)}) async-start(), calls=%async_computation.20 | async-start | bytes 12091392 | tf_op jit(solution)/shard_map/all_gather | solution.py:160
  156.3 320.5 %all-gather.19.cloned.1.call-start = ((), (), s32[]{:S(2)}) async-start(), calls=%async_computation.21 | async-start | bytes 6045696 | tf_op jit(solution)/shard_map/all_gather | solution.py:161
  169.8 3.9 copy-start.4
  173.7 5.7 copy-start
  182.8 13.2 %copy-start.11 = (bf16[128]{0:T(256)(128)(2,1)S(1)}, bf16[128]{0:T(256)(128)(2,1)}, u32[]{:S(2)}) copy-start(bf16[128]{0:T(256)(128)(2,1)} %param.15) | copy-start | bytes 772
  192.4 23.1 %all-to-all-start.3 = ((bf16[2,512,256]{2,0,1:T(2,128)(2,1)}), bf16[2,512,256]{2,0,1:T(2,128)(2,1)S(1)}, u32[]{:S(2)}, u32[]{:S(2)}) async-start(bf16[2,512,256]{2,0,1:T(2,128)(2,1)} %copy.99), calls=%async_computation.3 | async-start | bytes 1048576 | tf_op jit(solution)/shard_map/all_to_all | solution.py:199
  195.9 416.0 %all-reduce.11.cloned.1.call-start = ((), (), s32[]{:S(2)}) async-start(), calls=%async_computation.30 | async-start | bytes 4194304
  216.2 181.6 %copy-start.5 = (bf16[32,8,4,256]{3,1,2,0:T(8,128)(2,1)}, bf16[32,8,4,256]{3,1,2,0:T(8,128)(2,1)S(1)}, u32[]{:S(2)}) copy-start(bf16[32,8,4,256]{3,1,2,0:T(8,128)(2,1)S(1)} %copy.131) | copy-start | bytes 1572868
  388.7 88.1 %copy-start.10 = (bf16[2,128,1024]{2,1,0:T(8,128)(2,1)S(1)}, bf16[2,128,1024]{2,1,0:T(8,128)(2,1)}, u32[]{:S(2)}) copy-start(bf16[2,128,1024]{2,1,0:T(8,128)(2,1)} %param.9) | copy-start | bytes 1572868
  476.8 12.1 slice-start
  476.8 12.1 slice-start.1
  488.9 5.0 copy-start.1
  499.8 1.9 copy-start.2
  518.8 8.8 copy-start.8
  518.8 9.0 copy-start.7
  547.6 3.8 copy-start.6
  551.3 132.3 %reduce-scatter.17.cloned.1.call-start = ((), (), s32[]{:S(2)}) async-start(), calls=%async_computation.24 | async-start | bytes 2359296 | tf_op jit(solution)/shard_map/reduce_scatter | solution.py:315
  553.5 237.6 %reduce-scatter.23.cloned.1.call-start = ((), (), s32[]{:S(2)}) async-start(), calls=%async_computation.27 | async-start | bytes 6045696 | tf_op jit(solution)/shard_map/reduce_scatter | solution.py:321
  559.4 11.0 copy-start.14
  566.9 47.1 %all-to-all-start.5 = ((bf16[2,512,256]{2,0,1:T(2,128)(2,1)}), bf16[2,512,256]{2,0,1:T(2,128)(2,1)S(1)}, u32[]{:S(2)}, u32[]{:S(2)}) async-start(bf16[2,512,256]{2,0,1:T(2,128)(2,1)} %copy.107), calls=%async_computation.5 | async-start | bytes 1048576 | tf_op jit(solution)/shard_map/all_to_all | solution.py:271
  614.0 13.1 %all-to-all-start.6 = ((bf16[2,512,256]{2,0,1:T(2,128)(2,1)}), bf16[2,512,256]{2,0,1:T(2,128)(2,1)}, u32[]{:S(2)}, u32[]{:S(2)}) async-start(bf16[2,512,256]{2,0,1:T(2,128)(2,1)} %constant_dynamic-slice_fusion.5), calls=%async_computation.6 | async-start | bytes 1048576 | tf_op jit(solution)/shard_map/all_to_all | solution.py:272
  627.1 13.1 %all-to-all-start.7 = ((bf16[2,512,256]{2,0,1:T(2,128)(2,1)}), bf16[2,512,256]{2,0,1:T(2,128)(2,1)S(1)}, u32[]{:S(2)}, u32[]{:S(2)}) async-start(bf16[2,512,256]{2,0,1:T(2,128)(2,1)} %constant_dynamic-slice_fusion.4), calls=%async_computation.7 | async-start | bytes 1048576 | tf_op jit(solution)/shard_map/all_to_all | solution.py:275
  630.8 281.6 %reduce-scatter.13.cloned.1.call-start = ((), (), s32[]{:S(2)}) async-start(), calls=%async_computation.22 | async-start | bytes 7077888 | tf_op jit(solution)/shard_map/reduce_scatter | solution.py:312
  655.2 441.7 %reduce-scatter.21.cloned.1.call-start = ((), (), s32[]{:S(2)}) async-start(), calls=%async_computation.26 | async-start | bytes 12091392 | tf_op jit(solution)/shard_map/reduce_scatter | solution.py:318
  664.4 489.0 %reduce-scatter.19.cloned.1.call-start = ((), (), s32[]{:S(2)}) async-start(), calls=%async_computation.25 | async-start | bytes 327680 | tf_op jit(solution)/shard_map/reduce_scatter | solution.py:335
  683.7 415.8 %copy-start.13 = (u32[32]{0:T(128)S(1)}, u32[32]{0:T(128)}, u32[]{:S(2)}) copy-start(u32[32]{0:T(128)} %constant.146) | copy-start | bytes 388
  683.7 416.4 %copy-start.12 = (u32[32]{0:T(128)S(1)}, u32[32]{0:T(128)}, u32[]{:S(2)}) copy-start(u32[32]{0:T(128)} %constant.150) | copy-start | bytes 388
  683.7 471.2 %reduce-scatter.25.cloned.1.call-start = ((), (), s32[]{:S(2)}) async-start(), calls=%async_computation.28 | async-start | bytes 839680 | tf_op jit(solution)/shard_map/reduce_scatter | solution.py:341
  791.2 378.3 %reduce-scatter.15.cloned.1.call-start = ((), (), s32[]{:S(2)}) async-start(), calls=%async_computation.23 | async-start | bytes 983040 | tf_op jit(solution)/shard_map/reduce_scatter | solution.py:332
  912.4 286.4 %reduce-scatter.27.cloned.1.call-start = ((), (), s32[]{:S(2)}) async-start(), calls=%async_computation.29 | async-start | bytes 1679360
Sparse Core Ops, SparseCore 0:
  10.2 101.7 all-gather.8
  140.7 18.5 all-gather.12
  161.4 21.3 all-gather.10
  184.8 49.2 all-gather.14
  236.1 152.5 all-gather.16
  390.7 86.0 all-gather.18
  551.4 60.3 all-reduce.10
  615.8 67.8 reduce-scatter.16
  687.7 103.4 reduce-scatter.22
  794.6 117.7 reduce-scatter.12
  916.0 180.8 reduce-scatter.20
  1099.4 19.1 reduce-scatter.18
  1121.1 22.5 reduce-scatter.24
  1146.1 23.3 reduce-scatter.14
  1172.0 26.7 reduce-scatter.26
where the time goes:
time: 1210 us
  waiting for transfers between devices  849 us (70%)
  blocking collectives  130 us (11%)
  matrix products  112 us (9%)
  local copies, waits for them, and re-layouts  60.9 us (5%)
  other arithmetic  25.3 us (2%)
  starting transfers between devices  15.3 us (1%)
  between operations  15.2 us (1%)
    reduce_scatter x1, waiting for transfers between devices, local(): lax.psum_scatter(grad_inner.astype(jnp.bfloat16), ('dp', 'ctx'), scatter_...  184 us
    all_gather x1, waiting for transfers between devices, local(): lax.all_gather(w_in, ('dp', 'ctx'), axis=0, tiled=True)  152 us
    reduce_scatter x1, waiting for transfers between devices, local(): lax.psum_scatter(grad_project.astype(jnp.bfloat16), ('dp', 'ctx'), scatte...  121 us
    reduce_scatter x1, waiting for transfers between devices, local(): lax.psum_scatter(grad_mlp.astype(jnp.bfloat16), ('dp', 'ctx'), scatter_di...  107 us
    all_gather x1, waiting for transfers between devices, local(): lax.all_gather(w_mlp_out, ('dp', 'ctx'), axis=0, tiled=True)  79 us
    all_gather x1, waiting for transfers between devices, local(): lax.all_gather(w_qkv, ('dp', 'ctx'), axis=0, tiled=True)  78.8 us
    unnamed x17, waiting for transfers between devices  70.3 us
    unnamed x2, blocking collectives  40.8 us
  transfers between devices with their start and end apart: 19, of which 13 were waited for; matrix products, arithmetic and copies ran while one was open for 9% of the time, Pallas kernels for 0%

commit v1 on v0

--- a/solution.py
+++ b/solution.py
@@ -3,6 +3,8 @@
 import jax
 import jax.numpy as jnp
 from jax import lax
+from jax.experimental import pallas as pl
+from jax.experimental.pallas import tpu as pltpu
 from jax.sharding import PartitionSpec as P
 
 HD = 64
@@ -144,7 +146,7 @@
     return (grad_queries * scale, grad_keys, grad_values)
 
 
-def local(tokens, cotangent, w_qkv, w_attn_out, w_in, w_mlp_out, norm_gain1, norm_gain2):
+def local_general(tokens, cotangent, w_qkv, w_attn_out, w_in, w_mlp_out, norm_gain1, norm_gain2):
     seqs_here, block_rows, width = tokens.shape
     count_rows = seqs_here * block_rows
     heads_all = width // HD
@@ -360,6 +362,438 @@
     )
 
 
+F32 = jnp.float32
+BF16 = jnp.bfloat16
+VMEM_BYTES = 56 * 1024 * 1024
+
+
+def dot(left, right, dims=((1,), (0,))):
+    return lax.dot_general(left, right, (dims, ((), ())), preferred_element_type=F32)
+
+
+def lane_rotate(values, cosine, sine_signed):
+    lane = lax.broadcasted_iota(jnp.int32, values.shape, 1)
+    width = values.shape[1]
+    partner = jnp.where(
+        lane % HD < HD // 2,
+        pltpu.roll(values, width - HD // 2, 1),
+        pltpu.roll(values, HD // 2, 1),
+    )
+    return values * cosine + partner * sine_signed
+
+
+def project_kernel(*refs):
+    blocks = refs[:-6]
+    gain_ref, w_ref, cos_ref, sin_ref, low_ref, qkv_ref = refs[-6:]
+    rows = blocks[0].shape[0]
+    for place, block in enumerate(blocks):
+        normed, _ = normalize(block[...].astype(F32))
+        low_ref[place * rows : (place + 1) * rows, :] = (normed * gain_ref[...]).astype(BF16)
+    projected = dot(low_ref[...], w_ref[...])
+    part = w_ref.shape[1] // 3
+    cosine, sine = cos_ref[...], sin_ref[...]
+    qkv_ref[:, :part] = (lane_rotate(projected[:, :part], cosine, sine) * HD**-0.5).astype(BF16)
+    qkv_ref[:, part : 2 * part] = lane_rotate(
+        projected[:, part : 2 * part], cosine, sine
+    ).astype(BF16)
+    qkv_ref[:, 2 * part :] = projected[:, 2 * part :].astype(BF16)
+
+
+def project(blocks, gain, w, cosine, sine):
+    tokens = len(blocks) * blocks[0].shape[0]
+    return pl.pallas_call(
+        project_kernel,
+        out_shape=(
+            jax.ShapeDtypeStruct((tokens, w.shape[0]), BF16),
+            jax.ShapeDtypeStruct((tokens, w.shape[1]), BF16),
+        ),
+        compiler_params=pltpu.CompilerParams(vmem_limit_bytes=VMEM_BYTES),
+        name="project",
+    )(*blocks, gain, w, cosine, sine)
+
+
+def head_masks(shape):
+    lane = lax.broadcasted_iota(jnp.int32, shape, 1)
+    return [lane // HD == head for head in range(shape[1] // HD)]
+
+
+def attend_kernel(q_ref, k_ref, v_ref, w_ref, att_ref, low_ref, log_ref, even_ref, odd_ref):
+    queries = q_ref[...]
+    keys, values = k_ref[...], v_ref[...]
+    attended = jnp.zeros(queries.shape, F32)
+    logs = jnp.zeros(queries.shape, F32)
+    for mask in head_masks(queries.shape):
+        scores = dot(jnp.where(mask, queries, 0), keys, ((1,), (1,)))
+        peak = jnp.max(scores, axis=1, keepdims=True)
+        weights = jnp.exp(scores - peak)
+        total = jnp.sum(weights, axis=1, keepdims=True)
+        mixed = dot(weights.astype(BF16), values) * (1.0 / total)
+        attended = jnp.where(mask, mixed, attended)
+        logs = jnp.where(mask, peak + jnp.log(total), logs)
+    att_ref[...] = attended
+    log_ref[...] = logs
+    low = attended.astype(BF16)
+    low_ref[...] = low
+    half = queries.shape[0] // 2
+    part = dot(low, w_ref[...]).astype(BF16)
+    even_ref[0] = part[:half]
+    odd_ref[0] = part[half:]
+
+
+def attend(qkv, w, block):
+    tokens, width = qkv.shape[0], qkv.shape[1] // 3
+    steps = tokens // (2 * block)
+    rows = pl.BlockSpec((2 * block, width), lambda i: (i, 0))
+    part = pl.BlockSpec((1, block, w.shape[1]), lambda i: (i, 0, 0))
+    part_shape = jax.ShapeDtypeStruct((steps, block, w.shape[1]), BF16)
+    return pl.pallas_call(
+        attend_kernel,
+        grid=(steps,),
+        in_specs=[
+            rows,
+            pl.BlockSpec((tokens, width), lambda i: (0, 1)),
+            pl.BlockSpec((tokens, width), lambda i: (0, 2)),
+            pl.BlockSpec(w.shape, lambda i: (0, 0)),
+        ],
+        out_specs=(rows, rows, rows, part, part),
+        out_shape=(
+            jax.ShapeDtypeStruct((tokens, width), F32),
+            jax.ShapeDtypeStruct((tokens, width), BF16),
+            jax.ShapeDtypeStruct((tokens, width), F32),
+            part_shape,
+            part_shape,
+        ),
+        compiler_params=pltpu.CompilerParams(vmem_limit_bytes=VMEM_BYTES),
+        name="attend",
+    )(qkv, qkv, qkv, w)
+
+
+def attend_back_kernel(
+    q_ref, k_ref, v_ref, grad_ref, att_ref, log_ref, cosq_ref, sinq_ref, cos_ref, sin_ref,
+    gq_ref, gk_ref, gv_ref, sum_k, sum_v,
+):
+    step = pl.program_id(0)
+
+    @pl.when(step == 0)
+    def _():
+        sum_k[...] = jnp.zeros_like(sum_k)
+        sum_v[...] = jnp.zeros_like(sum_v)
+
+    queries, grads = q_ref[...], grad_ref[...]
+    keys, values = k_ref[...], v_ref[...]
+    along = (grads.astype(F32) * att_ref[...]).T
+    logs = log_ref[...].T
+    grad_queries = jnp.zeros(queries.shape, F32)
+    for head, mask in enumerate(head_masks(queries.shape)):
+        own_q = jnp.where(mask, queries, 0)
+        own_g = jnp.where(mask, grads, 0)
+        scores = dot(keys, own_q, ((1,), (1,)))
+        weights = jnp.exp(scores - logs[head * HD : head * HD + 1])
+        lifted = dot(values, own_g, ((1,), (1,)))
+        row = jnp.sum(along[head * HD : (head + 1) * HD], axis=0, keepdims=True)
+        grad_scores = (weights * (lifted - row)).astype(BF16)
+        sum_k[...] += dot(grad_scores, own_q)
+        sum_v[...] += dot(weights.astype(BF16), own_g)
+        grad_queries = jnp.where(mask, dot(grad_scores, keys, ((0,), (0,))), grad_queries)
+    gq_ref[...] = lane_rotate(grad_queries * HD**-0.5, cosq_ref[...], -sinq_ref[...]).astype(BF16)
+
+    @pl.when(step == pl.num_programs(0) - 1)
+    def _():
+        gk_ref[...] = lane_rotate(sum_k[...], cos_ref[...], -sin_ref[...]).astype(BF16)
+        gv_ref[...] = sum_v[...].astype(BF16)
+
+
+def attend_back(qkv, grads, attended, logs, cosine, sine, query_rows):
+    tokens, width = qkv.shape[0], qkv.shape[1] // 3
+    rows = pl.BlockSpec((query_rows, width), lambda i: (i, 0))
+    whole = pl.BlockSpec((tokens, width), lambda i: (0, 0))
+    shape = jax.ShapeDtypeStruct((tokens, width), BF16)
+    return pl.pallas_call(
+        attend_back_kernel,
+        grid=(tokens // query_rows,),
+        in_specs=[
+            rows,
+            pl.BlockSpec((tokens, width), lambda i: (0, 1)),
+            pl.BlockSpec((tokens, width), lambda i: (0, 2)),
+            rows,
+            rows,
+            rows,
+            rows,
+            rows,
+            whole,
+            whole,
+        ],
+        out_specs=(rows, whole, whole),
+        out_shape=(shape, shape, shape),
+        scratch_shapes=[pltpu.VMEM((tokens, width), F32), pltpu.VMEM((tokens, width), F32)],
+        compiler_params=pltpu.CompilerParams(vmem_limit_bytes=VMEM_BYTES),
+        name="attend_back",
+    )(qkv, qkv, qkv, grads, attended, logs, cosine, sine, cosine, sine)
+
+
+class Group:
+    def __init__(self):
+        self.heads = lax.axis_size("head")
+        self.dp = lax.axis_size("dp")
+        self.ctx_at = lax.axis_index("ctx")
+        self.head_at = lax.axis_index("head")
+        self.dp_at = lax.axis_index("dp")
+
+    def swap(self, values, bit):
+        if bit == 4:
+            return lax.ppermute(values, "ctx", [(0, 1), (1, 0)])
+        return lax.ppermute(values, "head", [(i, i ^ bit) for i in range(self.heads)])
+
+    def gather(self, own, first, second):
+        blocks = {0: own, first: self.swap(own, first), second: self.swap(own, second)}
+        blocks[6] = self.swap(blocks[first], second)
+        for place in (0, 2, 4, 6):
+            blocks[place + 1] = self.swap(blocks[place], 1)
+        return [blocks[place] for place in range(8)]
+
+    def reduce(self, even, odd, first, second):
+        met = even.astype(F32) + self.swap(odd, 1).astype(F32)
+        at = {2 * place: met[place] for place in range(4)}
+        other = first ^ second
+        far = self.swap(at[other].astype(BF16), first)
+        near = self.swap(at[first].astype(BF16), first)
+        last = self.swap((at[second] + far.astype(F32)).astype(BF16), second)
+        return at[0] + near.astype(F32) + last.astype(F32)
+
+    def rows_in(self, values, place):
+        pairs = [
+            (place[h] * self.heads + d, d * self.heads + h)
+            for d in range(self.dp)
+            for h in range(self.heads)
+        ]
+        return lax.ppermute(values, ("dp", "head"), pairs)
+
+    def rows_back(self, values, place):
+        pairs = [
+            (d * self.heads + h, place[h] * self.heads + d)
+            for d in range(self.dp)
+            for h in range(self.heads)
+        ]
+        return lax.ppermute(values, ("dp", "head"), pairs)
+
+    def total(self, values):
+        for bit in (1, 2, 4):
+            values = values + self.swap(values, bit)
+        step = 1
+        while step < self.dp:
+            values = values + lax.ppermute(
+                values, "dp", [(i, i ^ step) for i in range(self.dp)]
+            )
+            step *= 2
+        return values
+
+
+def table(choices, index):
+    return jnp.asarray(choices, jnp.int32)[index]
+
+
+def pick(array, index, axis):
+    return lax.dynamic_index_in_dim(array, index, axis, keepdims=False)
+
+
+def split_places(partial):
+    rows = partial.shape[0] // 8
+    blocks = partial.astype(BF16).reshape(4, 2, rows, partial.shape[1])
+    return blocks[:, 0], blocks[:, 1]
+
+
+def local_split(tokens, cotangent, w_qkv, w_attn_out, w_in, w_mlp_out, norm_gain1, norm_gain2):
+    seqs, block, width = tokens.shape
+    group = Group()
+    heads, dp = group.heads, group.dp
+    at_c, at_h = group.ctx_at, group.head_at
+    parts = 2 * heads
+    hidden = w_in.shape[1] // 2 // parts
+    own_width = width // parts
+    half = heads // 2
+    place = [2 * h if h < half else 2 * (h - half) + 1 for h in range(heads)]
+    straight = list(range(heads))
+    way = [(4, 2) if s % 2 == 0 else (2, 4) for s in range(seqs)]
+
+    x_blocks = [group.gather(tokens[s], *way[s]) for s in range(seqs)]
+
+    gains = jnp.concatenate([norm_gain1, norm_gain2]).reshape(2, 1, -1)
+    rows_here = w_qkv.shape[0]
+    qkv_view = w_qkv.reshape(rows_here, 3, heads, 2, own_width)
+    qkv_view = pick(qkv_view, at_h, 2)
+    in_view = w_in.reshape(rows_here, 2, heads, 2, hidden)
+    in_view = pick(in_view, table(place, at_h), 2)
+
+    def in_order(own, other):
+        return jnp.where(at_c == 0, jnp.stack([own, other]), jnp.stack([other, own]))
+
+    def own_columns(view):
+        own = pick(view, at_c, 2)
+        other = group.swap(pick(view, 1 - at_c, 2), 4)
+        return in_order(own, other)
+
+    gain_rows = jnp.pad(
+        gains.reshape(2, -1), ((0, 14), (0, 3 * own_width - rows_here))
+    )
+    qkv_pair = own_columns(qkv_view).reshape(2, rows_here, 3 * own_width)
+    gain_pair = in_order(gain_rows, group.swap(gain_rows, 4))
+    qkv_all = lax.all_gather(jnp.concatenate([qkv_pair, gain_pair], axis=1), "dp", axis=0)
+    weight_qkv = qkv_all[:, :, :rows_here].reshape(width, 3 * own_width)
+    gain_one = qkv_all[:, :, rows_here, :rows_here].reshape(1, width).astype(F32)
+    gain_two = qkv_all[:, :, rows_here + 1, :rows_here].reshape(1, width).astype(F32)
+    in_pair = jnp.moveaxis(own_columns(in_view), 2, 0)
+    in_all = lax.all_gather(in_pair, "dp", axis=1)
+    weight_first = in_all[0].reshape(width, hidden)
+    weight_second = in_all[1].reshape(width, hidden)
+    weight_out = group.rows_in(w_attn_out, straight)
+    weight_mlp = group.rows_in(w_mlp_out, place)
+
+    me = at_c * heads + at_h
+    relative = jnp.arange(8 * block, dtype=jnp.int32)
+    positions = ((relative // block) ^ me) * block + relative % block
+    lane = jnp.arange(own_width, dtype=jnp.int32)
+    frequency = jnp.exp(
+        (lane % (HD // 2)).astype(F32) * (-math.log(ROPE_BASE) / (HD // 2))
+    )
+    angles = positions.astype(F32)[:, None] * frequency[None, :]
+    cosine = jnp.cos(angles)
+    sine = jnp.sin(angles) * jnp.where(lane % HD < HD // 2, -1.0, 1.0)[None, :]
+
+    low1, qkv, att, att_low, logs, residual, back2 = [], [], [], [], [], [], []
+    low2_all = []
+    for s in range(seqs):
+        low, rotated = project(x_blocks[s], gain_one, weight_qkv, cosine, sine)
+        low1.append(low)
+        qkv.append(rotated)
+        attended, attended_low, log_total, even, odd = attend(rotated, weight_out, block)
+        att.append(attended)
+        att_low.append(attended_low)
+        logs.append(log_total)
+        branch = group.reduce(even, odd, *way[s])
+        resid = tokens[s].astype(F32) + branch
+        normed2, factor2 = normalize(resid)
+        residual.append(resid)
+        back2.append((normed2, factor2))
+        low2_all.append(
+            jnp.concatenate(group.gather((normed2 * gain_two).astype(BF16), *way[s]))
+        )
+
+    cot_all = [jnp.concatenate(group.gather(cotangent[s], *way[s])) for s in range(seqs)]
+
+    results, grad_inputs = [], []
+    mixed_all, first_all, second_all, branch_all, proj_all = [], [], [], [], []
+    grad_res = []
+    gain2_sum = 0.0
+    for s in range(seqs):
+        first = dot(low2_all[s], weight_first)
+        second = dot(low2_all[s], weight_second)
+        activated, pullback = jax.vjp(
+            lambda entries: jax.nn.gelu(entries, approximate=False), first
+        )
+        mixed = (activated * second).astype(BF16)
+        grad_mixed = dot(cot_all[s], weight_mlp, ((1,), (1,)))
+        grad_first = pullback(grad_mixed * second)[0].astype(BF16)
+        grad_second = (grad_mixed * activated).astype(BF16)
+        mixed_all.append(mixed)
+        first_all.append(grad_first)
+        second_all.append(grad_second)
+        partial = dot(grad_first, weight_first, ((1,), (1,))) + dot(
+            grad_second, weight_second, ((1,), (1,))
+        )
+        grad_low2 = group.reduce(*split_places(partial), *way[s])
+        normed2, factor2 = back2[s]
+        gain2_sum = gain2_sum + jnp.sum(grad_low2 * normed2, axis=0)
+        grad_residual = cotangent[s].astype(F32) + norm_back(
+            grad_low2 * gain_two, normed2, factor2
+        )
+        grad_res.append(grad_residual)
+        gathered = jnp.concatenate(group.gather(grad_residual.astype(BF16), *way[s]))
+        branch_all.append(gathered)
+        grad_att = dot(gathered, weight_out, ((1,), (1,))).astype(BF16)
+        gq, gk, gv = attend_back(qkv[s], grad_att, att[s], logs[s], cosine, sine, 2 * block)
+        proj = jnp.concatenate([gq, gk, gv], axis=1)
+        proj_all.append(proj)
+        grad_low1 = group.reduce(
+            *split_places(dot(proj, weight_qkv, ((1,), (1,)))), *way[s]
+        )
+        normed1, factor1 = normalize(tokens[s].astype(F32))
+        grad_inputs.append(
+            grad_residual + norm_back(grad_low1 * gain_one, normed1, factor1)
+        )
+        out_sum = group.reduce(*split_places(dot(mixed, weight_mlp)), *way[s])
+        results.append((residual[s] + out_sum).astype(BF16))
+
+    def over_tokens(left, right):
+        return sum(dot(a, b, ((0,), (0,))) for a, b in zip(left, right))
+
+    def scatter(values, axis):
+        return lax.psum_scatter(values.astype(BF16), "dp", scatter_dimension=axis, tiled=True)
+
+    def columns_first(values):
+        return jnp.moveaxis(values.reshape(values.shape[0], dp, -1), 1, 0)
+
+    grad_mlp = scatter(columns_first(over_tokens(mixed_all, cot_all)), 0)[0]
+    grad_mlp = group.rows_back(grad_mlp, place).astype(F32)
+    grad_out = scatter(columns_first(over_tokens(att_low, branch_all)), 0)[0]
+    grad_out = group.rows_back(grad_out, straight).astype(F32)
+
+    def rows_here_of(values):
+        pair = values.reshape(2, rows_here, -1)
+        own = pick(pair, at_c, 0)
+        other = group.swap(pick(pair, 1 - at_c, 0), 4)
+        return in_order(own, other)
+
+    grad_in = scatter(
+        jnp.stack([over_tokens(low2_all, first_all), over_tokens(low2_all, second_all)]), 1
+    )
+    grad_in = jnp.stack([rows_here_of(grad_in[0]), rows_here_of(grad_in[1])])
+    keep = (at_h >= half).astype(jnp.int32)
+    stays = pick(grad_in, keep, 0)
+    comes = group.swap(pick(grad_in, 1 - keep, 0), half)
+    grad_in = jnp.where(
+        keep == 0, jnp.concatenate([stays, comes]), jnp.concatenate([comes, stays])
+    )
+    grad_in = jnp.moveaxis(grad_in, 0, 1).reshape(rows_here, -1).astype(F32)
+
+    grad_qkv = over_tokens(low1, proj_all)
+    gain1_sum = jnp.sum(grad_qkv * weight_qkv.astype(F32), axis=1) / gain_one[0]
+    sums = group.total(jnp.stack([gain1_sum, gain2_sum]).reshape(-1, 128))
+    sums = sums.reshape(2, -1)
+    per_device = width // (dp * parts)
+    start = ((group.dp_at * 2 + at_c) * heads + at_h) * per_device
+    grad_gain1, grad_gain2 = (
+        lax.dynamic_slice_in_dim(sums[i], start, per_device, 0) for i in range(2)
+    )
+    grad_qkv = rows_here_of(scatter(grad_qkv, 0)).reshape(2, rows_here, 3, own_width)
+    grad_qkv = jnp.moveaxis(grad_qkv, 2, 0)
+    stays = pick(grad_qkv, table([0, 1, 1, 2], at_h), 0)
+    core = group.swap(pick(grad_qkv, table([1, 0, 2, 1], at_h), 0), 1)
+    chip = group.swap(pick(grad_qkv, table([2, 2, 0, 0], at_h), 0), 2)
+    grad_qkv = jnp.where(
+        at_h % 2 == 0, jnp.concatenate([stays, core, chip]), jnp.concatenate([chip, core, stays])
+    )
+    grad_qkv = jnp.moveaxis(grad_qkv, 0, 1).reshape(rows_here, -1).astype(F32)
+
+    return (
+        jnp.stack(results),
+        jnp.stack(grad_inputs),
+        grad_qkv,
+        grad_out,
+        grad_in,
+        grad_mlp,
+        grad_gain1,
+        grad_gain2,
+    )
+
+
+def local(tokens, cotangent, w_qkv, w_attn_out, w_in, w_mlp_out, norm_gain1, norm_gain2):
+    args = (tokens, cotangent, w_qkv, w_attn_out, w_in, w_mlp_out, norm_gain1, norm_gain2)
+    sizes = [lax.axis_size(axis) for axis in ("dp", "ctx", "head")]
+    if sizes == [4, 2, 4] and tokens.shape[2] == 8 * 2 * HD and tokens.shape[1] % 16 == 0:
+        return local_split(*args)
+    return local_general(*args)
+
+
 def solution(mesh):
     in_specs = (
         P("dp", ("ctx", "head"), None),

time: 1210 us -> 454 us (0.38)
  waiting for transfers between devices: 849 us -> 100 us
  blocking collectives: 130 us -> 18.8 us
  starting transfers between devices: 15.3 us -> 108 us
  matrix products: 112 us -> 50.1 us
  Pallas kernels: 0 us -> 44.9 us
    reduce_scatter x7 -> x4, waiting for transfers between devices: 445 us -> 2.97 us  [scatter(): lax.psum_scatter(values.astype(BF16), 'dp', scatter_dimension=axis, tiled...]
    all_gather x6 -> x1, waiting for transfers between devices: 331 us -> 0.01 us  [local_split(): in_all = lax.all_gather(in_pair, 'dp', axis=1)]
    ppermute x0 -> x106, starting transfers between devices: none -> 107 us  [the longest x69 64.1 us: swap(): lax.ppermute(values, 'head', [(i, i ^ bit) for i in range(self.heads)])]
    ppermute x0 -> x106, waiting for transfers between devices: none -> 97.1 us  [the longest x69 49.6 us: swap(): lax.ppermute(values, 'head', [(i, i ^ bit) for i in range(self.heads)])]
    unnamed x17 -> x5, waiting for transfers between devices: 70.3 us -> 0.08 us
    dot_general x18 -> x26, matrix products: 112 us -> 50.1 us  [dot(): lax.dot_general(left, right, (dims, ((), ())), preferred_element_type=F32)]
    all_to_all x4 -> x0, blocking collectives: 47 us -> none  [the longest x1 12.7 us: local(): lax.all_to_all(grad_attended.reshape(seqs_here, block_rows, width), 'head...]
    pallas_call x0 -> x6, Pallas kernels: none -> 44.9 us  [the longest x2 19.4 us: attend_back(): pl.pallas_call(attend_back_kernel, grid=(tokens // query_rows,), in_specs...]
  transfers between devices with their start and end apart: 19 -> 111, of which waited for: 13 -> 35; matrix products, arithmetic and copies ran while one was open for 9% -> 29% of each run, Pallas kernels for 0% -> 10%
where the time goes in v1:
time: 454 us; the launch traced here: 447 us
  starting transfers between devices  108 us (24%)
  waiting for transfers between devices  100 us (22%)
  local copies, waits for them, and re-layouts  64.6 us (14%)
  matrix products  50.1 us (11%)
  Pallas kernels  44.9 us (10%)
  other arithmetic  36.7 us (8%)
  between operations  23.7 us (5%)
  blocking collectives  18.8 us (4%)
    ppermute x69, starting transfers between devices, swap(): lax.ppermute(values, 'head', [(i, i ^ bit) for i in range(self.heads)])  64.1 us
    dot_general x26, matrix products, dot(): lax.dot_general(left, right, (dims, ((), ())), preferred_element_type=F32)  50.1 us
    ppermute x69, waiting for transfers between devices, swap(): lax.ppermute(values, 'head', [(i, i ^ bit) for i in range(self.heads)])  49.6 us
    ppermute x31, waiting for transfers between devices, swap(): return lax.ppermute(values, 'ctx', [(0, 1), (1, 0)])  43.3 us
    unnamed x202, local copies, waits for them, and re-layouts  36 us
    ppermute x31, starting transfers between devices, swap(): return lax.ppermute(values, 'ctx', [(0, 1), (1, 0)])  35.6 us
    pallas_call x2, Pallas kernels, attend_back(): pl.pallas_call(attend_back_kernel, grid=(tokens // query_rows,), in_specs...  19.4 us
    all_gather x1, blocking collectives, local_split(): lax.all_gather(jnp.concatenate([qkv_pair, gain_pair], axis=1), 'dp', axis=0)  18.8 us
  transfers between devices with their start and end apart: 111, of which 35 were waited for; matrix products, arithmetic and copies ran while one was open for 29% of the time, Pallas kernels for 10%

profile of v1, /device:TPU:0, one launch (start us, length us, event | category | flops | bytes accessed | tf_op | source)
XLA Modules:
  0.0 446.6 jit_solution(17114402193068744949)
XLA Ops:
  7.2 1.9 slice_bitcast_fusion.45
  9.2 3.0 collective-permute-start.50
  23.7 2.0 copy.94
  25.8 3.1 fusion.52
  42.2 2.0 collective-permute-done.7
  46.1 5.1 %collective-permute-done.21 = bf16[128,2,328]{0,2,1:T(8,128)(2,1)S(1)} collective-permute-done((bf16[128,2,328]{0,2,1:T(8,128)(2,1)S(1)}, bf16[128,2,328]{0,2,1:T(8,128)(2,1)S(1)}, u32[]{:S(2)}, u32[]{:S(2)}) %collective-permute-start.21) | collective-permute-done | bytes 167968 | tf_op jit(solution)/shard_map/ppermute | solution.py:544
  51.2 4.5 %collective-permute-start.72 = (bf16[128,1024]{1,0:T(8,128)(2,1)}, bf16[128,1024]{1,0:T(8,128)(2,1)S(1)}, u32[]{:S(2)}, u32[]{:S(2)}) collective-permute-start(bf16[128,1024]{1,0:T(8,128)(2,1)} %get-tuple-element.164), channel_id=1, source_target_pairs={{0,2},{1,3},{2,0},{3,1},{4,6},{5,7},{6,4},{7,5},{8,10},{9,11},{10,... | collective-permute-start | bytes 786440 | tf_op jit(solution)/shard_map/ppermute | solution.py:545
  58.0 18.8 %all-gather = bf16[8,144,384]{2,1,0:T(8,128)(2,1)S(1)} all-gather(bf16[2,144,384]{2,1,0:T(8,128)(2,1)S(1)} %copy.92), channel_id=2, replica_groups=mesh['dp'=4,'ctx'=2,'head'=4] {'dp'}, dimensions={0}, use_global_device_ids=true | all-gather | bytes 1105920 | tf_op jit(solution)/shard_map/all_gather | solution.py:640
  78.4 1.7 collective-permute-start.28
  85.5 6.9 %collective-permute-done.5.refs_6_ = bf16[128,1024]{1,0:T(8,128)(2,1)} collective-permute-done((bf16[128,1024]{1,0:T(8,128)(2,1)}, bf16[128,1024]{1,0:T(8,128)(2,1)}, u32[]{:S(2)}, u32[]{:S(2)}) %collective-permute-start.5) | collective-permute-done | bytes 262176 | tf_op jit(solution)/shard_map/ppermute | solution.py:545
  94.7 1.7 collective-permute-start.54
  102.7 5.4 %project.2 = (bf16[1024,1024]{1,0:T(8,128)(2,1)}, bf16[1024,384]{1,0:T(8,128)(2,1)}) custom-call(bf16[128,1024]{1,0:T(8,128)(2,1)} %copy-done.25, bf16[128,1024]{1,0:T(8,128)(2,1)} %collective-permute-done.refs_1_, bf16[128,1024]{1,0:T(8,128)(2,1)} %copy-done.38, bf16[128,1024]{1,0:T(8,128)(2,1)} %copy-done.42, ...), custom_call_target="tpu_custom_call" | custom-call | tf_op jit(solution)/shard_map/project/pallas_call | solution.py:404
  108.1 7.4 %attend.2 = (f32[1024,128]{1,0:T(8,128)}, bf16[1024,128]{1,0:T(8,128)(2,1)}, f32[1024,128]{1,0:T(8,128)}, bf16[4,128,1024]{2,1,0:T(8,128)(2,1)}, bf16[4,128,1024]{2,1,0:T(8,128)(2,1)}) custom-call(bf16[1024,384]{1,0:T(8,128)(2,1)} %get-tuple-element.28.q_ref.k_ref.v_ref, bf16[1024,384]{1,0:T(8,128)(2,1)} %get-tuple-element.28.q_ref.k_ref.v_ref, ...), custom_call_target="tpu_custom_call" | custom-call | tf_op jit(solution)/shard_map/attend/pallas_call | solution.py:449
  123.2 5.4 %project.3 = (bf16[1024,1024]{1,0:T(8,128)(2,1)}, bf16[1024,384]{1,0:T(8,128)(2,1)}) custom-call(bf16[128,1024]{1,0:T(8,128)(2,1)} %copy-done.24, bf16[128,1024]{1,0:T(8,128)(2,1)} %copy-done.37, bf16[128,1024]{1,0:T(8,128)(2,1)} %copy-done.36, bf16[128,1024]{1,0:T(8,128)(2,1)} %copy-done.44, bf16[128,1024]{1,0:T(8,128)(2,1)} %copy-done.35, ...), custom_call_target="tpu_custom_call" | custom-call | tf_op jit(solution)/shard_map/project/pallas_call | solution.py:404
  128.7 7.3 %attend.3 = (f32[1024,128]{1,0:T(8,128)}, bf16[1024,128]{1,0:T(8,128)(2,1)}, f32[1024,128]{1,0:T(8,128)}, bf16[4,128,1024]{2,1,0:T(8,128)(2,1)}, bf16[4,128,1024]{2,1,0:T(8,128)(2,1)}) custom-call(bf16[1024,384]{1,0:T(8,128)(2,1)} %get-tuple-element.31.q_ref.k_ref.v_ref, bf16[1024,384]{1,0:T(8,128)(2,1)} %get-tuple-element.31.q_ref.k_ref.v_ref, ...), custom_call_target="tpu_custom_call" | custom-call | tf_op jit(solution)/shard_map/attend/pallas_call | solution.py:449
  145.8 1.7 collective-permute-start.35
  147.6 3.1 collective-permute-done.12
  156.4 1.9 collective-permute-done.35
  158.3 4.4 collective-permute-done.13
  162.7 1.9 fusion.51
  167.2 1.7 collective-permute-start.39
  169.1 3.4 collective-permute-done.17
  174.0 2.1 collective-permute-done.15
  176.2 5.5 %collective-permute-done.39 = bf16[128,1024]{1,0:T(8,128)(2,1)S(1)} collective-permute-done((bf16[128,1024]{1,0:T(8,128)(2,1)S(1)}, bf16[128,1024]{1,0:T(8,128)(2,1)S(1)}, u32[]{:S(2)}, u32[]{:S(2)}) %collective-permute-start.39) | collective-permute-done | bytes 262176 | tf_op jit(solution)/shard_map/ppermute | solution.py:545
  185.5 4.9 %collective-permute-done.43 = bf16[128,1024]{1,0:T(8,128)(2,1)S(1)} collective-permute-done((bf16[128,1024]{1,0:T(8,128)(2,1)S(1)}, bf16[128,1024]{1,0:T(8,128)(2,1)S(1)}, u32[]{:S(2)}, u32[]{:S(2)}) %collective-permute-start.43) | collective-permute-done | bytes 262176 | tf_op jit(solution)/shard_map/ppermute | solution.py:544
  194.4 4.8 %multiply_convert_fusion = (bf16[1024,328]{0,1:T(8,128)(2,1)}, f32[1024,328]{0,1:T(8,128)S(1)}, f32[1024,328]{0,1:T(8,128)S(1)}) fusion(f32[1024,328]{0,1:T(8,128)S(1)} %fusion.28, bf16[1024,1024]{1,0:T(8,128)(2,1)S(1)} %copy-done.66, bf16[328,1024]{1,0:T(8,128)(2,1)S(1)} %collective-permute-done.22), kind=kOutput, calls=%fused_computation.27 | convolution fusion | flops 710033408 | bytes 7471104 | tf_op jit(solution)/shard_map/dot_general | solution.py:371
  200.7 3.4 fusion.24
  204.1 2.0 fusion.148
  208.4 4.4 multiply_convert_fusion.1
  212.8 2.4 add_convert_fusion.3
  217.7 21.4 %collective-permute-start.23 = (bf16[4,128,1024]{2,1,0:T(8,128)(2,1)}, bf16[4,128,1024]{2,1,0:T(8,128)(2,1)}, u32[]{:S(2)}, u32[]{:S(2)}) collective-permute-start(bf16[4,128,1024]{2,1,0:T(8,128)(2,1)} %slice_bitcast_fusion.10), channel_id=1, source_target_pairs={{0,1},{1,0},{2,3},{3,2},{4,5},{5,4},{6,7},{7,6},{8,9},{9,8},{10,11... | collective-permute-start | bytes 3145736 | tf_op jit(solution)/shard_map/ppermute | solution.py:545
  242.0 2.7 fusion.149
  259.4 2.0 collective-permute-start.47
  264.0 7.4 %collective-permute-done.25 = bf16[128,1024]{1,0:T(8,128)(2,1)S(1)} collective-permute-done((bf16[128,1024]{1,0:T(8,128)(2,1)S(1)}, bf16[128,1024]{1,0:T(8,128)(2,1)S(1)}, u32[]{:S(2)}, u32[]{:S(2)}) %collective-permute-start.25) | collective-permute-done | bytes 262176 | tf_op jit(solution)/shard_map/ppermute | solution.py:544
  273.5 8.8 %collective-permute-done.58 = bf16[128,1024]{1,0:T(8,128)(2,1)S(1)} collective-permute-done((bf16[128,1024]{1,0:T(8,128)(2,1)S(1)}, bf16[128,1024]{1,0:T(8,128)(2,1)S(1)}, u32[]{:S(2)}, u32[]{:S(2)}) %collective-permute-start.58) | collective-permute-done | bytes 262176 | tf_op jit(solution)/shard_map/ppermute | solution.py:544
  282.4 2.1 collective-permute-start.26
  288.5 3.1 collective-permute-done.79
  291.6 3.1 collective-permute-start.100
  294.7 2.5 collective-permute-done.26
  297.2 5.6 %collective-permute-done.59 = bf16[128,1024]{1,0:T(8,128)(2,1)} collective-permute-done((bf16[128,1024]{1,0:T(8,128)(2,1)S(1)}, bf16[128,1024]{1,0:T(8,128)(2,1)}, u32[]{:S(2)}, u32[]{:S(2)}) %collective-permute-start.59) | collective-permute-done | bytes 262176 | tf_op jit(solution)/shard_map/ppermute | solution.py:545
  302.9 3.5 multiply_reduce_fusion.2
  306.4 1.7 constant_dynamic-update-slice_fusion.31
  309.6 2.6 collective-permute-start.61
  313.5 1.8 convert_element_type.505
  317.9 2.4 collective-permute-start.65
  322.3 2.1 collective-permute-done.83
  326.6 3.0 collective-permute-done.65
  331.3 1.9 collective-permute-done.87
  336.8 3.0 convolution_convert_fusion.4.grad_ref
  339.8 9.7 %attend_back.3 = (bf16[1024,128]{1,0:T(8,128)(2,1)}, bf16[1024,128]{1,0:T(8,128)(2,1)}, bf16[1024,128]{1,0:T(8,128)(2,1)}) custom-call(bf16[1024,384]{1,0:T(8,128)(2,1)} %get-tuple-element.31.q_ref.k_ref.v_ref, bf16[1024,384]{1,0:T(8,128)(2,1)} %get-tuple-element.31.q_ref.k_ref.v_ref, bf16[1024,384]{1,0:T(8,128)(2,1)} %get-tuple-element.31.q_ref.k_ref.v_ref, ...), custom_call_target="tpu_custom_call" | custom-call | tf_op jit(solution)/shard_map/attend_back/pallas_call | solution.py:511
  351.9 9.7 %attend_back.2 = (bf16[1024,128]{1,0:T(8,128)(2,1)}, bf16[1024,128]{1,0:T(8,128)(2,1)}, bf16[1024,128]{1,0:T(8,128)(2,1)}) custom-call(bf16[1024,384]{1,0:T(8,128)(2,1)} %get-tuple-element.28.q_ref.k_ref.v_ref, bf16[1024,384]{1,0:T(8,128)(2,1)} %get-tuple-element.28.q_ref.k_ref.v_ref, bf16[1024,384]{1,0:T(8,128)(2,1)} %get-tuple-element.28.q_ref.k_ref.v_ref, ...), custom_call_target="tpu_custom_call" | custom-call | tf_op jit(solution)/shard_map/attend_back/pallas_call | solution.py:511
  366.4 2.3 multiply_reduce_fusion
  369.3 3.8 convolution_convert_fusion.1
  373.1 2.7 convolution_convert_fusion
  377.8 1.7 collective-permute-done.102
  383.2 2.3 slice_bitcast_fusion
  388.6 2.7 collective-permute-done.105
  396.6 2.0 collective-permute-done.97
  409.4 2.1 collective-permute-start.91
  415.2 2.8 collective-permute-start.70
  420.5 3.0 reduce-scatter.5.cloned.1.call-done
  426.1 3.9 collective-permute-done.70
  431.5 2.3 fusion.134
  434.3 1.8 collective-permute-start.95
  (524 shorter events, 165.2 us)
Async XLA Ops:
  7.2 147.6 %all-gather.4.cloned.1.call-start = ((), (), s32[]{:S(2)}) async-start(), calls=%async_computation.8 | async-start | bytes 1679360 | tf_op jit(solution)/shard_map/all_gather | solution.py:645
  9.2 46.6 %collective-permute-start.50 = (bf16[128,1024]{1,0:T(8,128)(2,1)}, bf16[128,1024]{1,0:T(8,128)(2,1)}, u32[]{:S(2)}, u32[]{:S(2)}) collective-permute-start(bf16[128,1024]{1,0:T(8,128)(2,1)} %get-tuple-element.163), channel_id=1, source_target_pairs={{0,2},{1,3},{2,0},{3,1},{4,6},{5,7},{6,4},{7,5},{8,10},{9,11},{10,... | collective-permute-start | bytes 786440 | tf_op jit(solution)/shard_map/ppermute | solution.py:545
  12.1 45.2 %collective-permute-start.49 = (bf16[128,1024]{1,0:T(8,128)(2,1)}, bf16[128,1024]{1,0:T(8,128)(2,1)}, u32[]{:S(2)}, u32[]{:S(2)}) collective-permute-start(bf16[128,1024]{1,0:T(8,128)(2,1)} %get-tuple-element.163), channel_id=1, source_target_pairs={{0,1},{1,0},{2,3},{3,2},{4,5},{5,4},{6,7},{7,6},{8,9},{9,8},{10,11... | collective-permute-start | bytes 786440 | tf_op jit(solution)/shard_map/ppermute | solution.py:545
  12.1 45.7 %collective-permute-start.52 = (bf16[128,1024]{1,0:T(8,128)(2,1)}, bf16[128,1024]{1,0:T(8,128)(2,1)}, u32[]{:S(2)}, u32[]{:S(2)}) collective-permute-start(bf16[128,1024]{1,0:T(8,128)(2,1)} %get-tuple-element.163), channel_id=1, source_target_pairs={{0,4},{4,0},{1,5},{5,1},{2,6},{6,2},{3,7},{7,3},{8,12},{12,8},{9,1... | collective-permute-start | bytes 786440 | tf_op jit(solution)/shard_map/ppermute | solution.py:544
  14.9 24.6 %collective-permute-start.8 = (bf16[16,384]{1,0:T(8,128)(2,1)}, bf16[16,384]{1,0:T(8,128)(2,1)}, u32[]{:S(2)}, u32[]{:S(2)}) collective-permute-start(bf16[16,384]{1,0:T(8,128)(2,1)} %get-tuple-element.196), channel_id=1, source_target_pairs={{0,4},{4,0},{1,5},{5,1},{2,6},{6,2},{3,7},{7,3},{8,12},{12,8},{9,1... | collective-permute-start | bytes 36872 | tf_op jit(solution)/shard_map/ppermute | solution.py:544
  15.5 40.3 %collective-permute-start.9 = (bf16[128,1024]{1,0:T(8,128)(2,1)}, bf16[128,1024]{1,0:T(8,128)(2,1)S(1)}, u32[]{:S(2)}, u32[]{:S(2)}) collective-permute-start(bf16[128,1024]{1,0:T(8,128)(2,1)} %param.15), channel_id=1, source_target_pairs={{0,0},{8,1},{16,2},{24,3},{1,8},{9,9},{17,10},{25,11},{2,16},{10,1... | collective-permute-start | bytes 786440 | tf_op jit(solution)/shard_map/ppermute | solution.py:569
  51.2 25.5 %collective-permute-start.72 = (bf16[128,1024]{1,0:T(8,128)(2,1)}, bf16[128,1024]{1,0:T(8,128)(2,1)S(1)}, u32[]{:S(2)}, u32[]{:S(2)}) collective-permute-start(bf16[128,1024]{1,0:T(8,128)(2,1)} %get-tuple-element.164), channel_id=1, source_target_pairs={{0,2},{1,3},{2,0},{3,1},{4,6},{5,7},{6,4},{7,5},{8,10},{9,11},{10,... | collective-permute-start | bytes 786440 | tf_op jit(solution)/shard_map/ppermute | solution.py:545
  55.8 21.1 %collective-permute-start.71 = (bf16[128,1024]{1,0:T(8,128)(2,1)}, bf16[128,1024]{1,0:T(8,128)(2,1)S(1)}, u32[]{:S(2)}, u32[]{:S(2)}) collective-permute-start(bf16[128,1024]{1,0:T(8,128)(2,1)} %get-tuple-element.164), channel_id=1, source_target_pairs={{0,1},{1,0},{2,3},{3,2},{4,5},{5,4},{6,7},{7,6},{8,9},{9,8},{10,11... | collective-permute-start | bytes 786440 | tf_op jit(solution)/shard_map/ppermute | solution.py:545
  55.8 22.6 %collective-permute-start.74 = (bf16[128,1024]{1,0:T(8,128)(2,1)}, bf16[128,1024]{1,0:T(8,128)(2,1)}, u32[]{:S(2)}, u32[]{:S(2)}) collective-permute-start(bf16[128,1024]{1,0:T(8,128)(2,1)} %get-tuple-element.164), channel_id=1, source_target_pairs={{0,4},{4,0},{1,5},{5,1},{2,6},{6,2},{3,7},{7,3},{8,12},{12,8},{9,1... | collective-permute-start | bytes 786440 | tf_op jit(solution)/shard_map/ppermute | solution.py:544
  57.3 22.8 %collective-permute-start.3 = (bf16[128,1024]{1,0:T(8,128)(2,1)S(1)}, bf16[128,1024]{1,0:T(8,128)(2,1)}, u32[]{:S(2)}, u32[]{:S(2)}) collective-permute-start(bf16[128,1024]{1,0:T(8,128)(2,1)S(1)} %get-tuple-element.167.refs_0_), channel_id=1, source_target_pairs={{0,4},{4,0},{1,5},{5,1},{2,6},{6,2},{3,7},{7,3},{8,12},{12,8},{9,1... | collective-permute-start | bytes 786440 | tf_op jit(solution)/shard_map/ppermute | solution.py:544
  57.9 22.3 %collective-permute-start.1 = (bf16[128,1024]{1,0:T(8,128)(2,1)S(1)}, bf16[128,1024]{1,0:T(8,128)(2,1)S(1)}, u32[]{:S(2)}, u32[]{:S(2)}) collective-permute-start(bf16[128,1024]{1,0:T(8,128)(2,1)S(1)} %get-tuple-element.167.refs_0_), channel_id=1, source_target_pairs={{0,2},{1,3},{2,0},{3,1},{4,6},{5,7},{6,4},{7,5},{8,10},{9,11},{10,... | collective-permute-start | bytes 786440 | tf_op jit(solution)/shard_map/ppermute | solution.py:545
  78.4 15.8 %collective-permute-start.28 = (bf16[128,1024]{1,0:T(8,128)(2,1)S(1)}, bf16[128,1024]{1,0:T(8,128)(2,1)S(1)}, u32[]{:S(2)}, u32[]{:S(2)}) collective-permute-start(bf16[128,1024]{1,0:T(8,128)(2,1)S(1)} %get-tuple-element.168.refs_0_), channel_id=1, source_target_pairs={{0,2},{1,3},{2,0},{3,1},{4,6},{5,7},{6,4},{7,5},{8,10},{9,11},{10,... | collective-permute-start | bytes 786440 | tf_op jit(solution)/shard_map/ppermute | solution.py:545
  80.1 14.6 %collective-permute-start.27 = (bf16[128,1024]{1,0:T(8,128)(2,1)S(1)}, bf16[128,1024]{1,0:T(8,128)(2,1)S(1)}, u32[]{:S(2)}, u32[]{:S(2)}) collective-permute-start(bf16[128,1024]{1,0:T(8,128)(2,1)S(1)} %get-tuple-element.168.refs_0_), channel_id=1, source_target_pairs={{0,1},{1,0},{2,3},{3,2},{4,5},{5,4},{6,7},{7,6},{8,9},{9,8},{10,11... | collective-permute-start | bytes 786440 | tf_op jit(solution)/shard_map/ppermute | solution.py:545
  80.9 11.5 %collective-permute-start.5 = (bf16[128,1024]{1,0:T(8,128)(2,1)}, bf16[128,1024]{1,0:T(8,128)(2,1)}, u32[]{:S(2)}, u32[]{:S(2)}) collective-permute-start(bf16[128,1024]{1,0:T(8,128)(2,1)} %collective-permute-done.3.refs_4_), channel_id=1, source_target_pairs={{0,2},{1,3},{2,0},{3,1},{4,6},{5,7},{6,4},{7,5},{8,10},{9,11},{10,... | collective-permute-start | bytes 786440 | tf_op jit(solution)/shard_map/ppermute | solution.py:545
  83.6 208.1 %reduce-scatter.11.cloned.1.call-start = ((), (), s32[]{:S(2)}) async-start(), calls=%async_computation.7 | async-start | bytes 839680 | tf_op jit(solution)/shard_map/reduce_scatter | solution.py:730
  83.6 15.2 %collective-permute-start.4 = (bf16[128,1024]{1,0:T(8,128)(2,1)}, bf16[128,1024]{1,0:T(8,128)(2,1)S(1)}, u32[]{:S(2)}, u32[]{:S(2)}) collective-permute-start(bf16[128,1024]{1,0:T(8,128)(2,1)} %collective-permute-done.3.refs_4_), channel_id=1, source_target_pairs={{0,1},{1,0},{2,3},{3,2},{4,5},{5,4},{6,7},{7,6},{8,9},{9,8},{10,11... | collective-permute-start | bytes 786440 | tf_op jit(solution)/shard_map/ppermute | solution.py:545
  85.5 13.3 %collective-permute-start.2 = (bf16[128,1024]{1,0:T(8,128)(2,1)}, bf16[128,1024]{1,0:T(8,128)(2,1)S(1)}, u32[]{:S(2)}, u32[]{:S(2)}) collective-permute-start(bf16[128,1024]{1,0:T(8,128)(2,1)} %copy-done.38), channel_id=1, source_target_pairs={{0,1},{1,0},{2,3},{3,2},{4,5},{5,4},{6,7},{7,6},{8,9},{9,8},{10,11... | collective-permute-start | bytes 786440 | tf_op jit(solution)/shard_map/ppermute | solution.py:545
  94.1 21.4 %collective-permute-start.51 = (bf16[128,1024]{1,0:T(8,128)(2,1)}, bf16[128,1024]{1,0:T(8,128)(2,1)S(1)}, u32[]{:S(2)}, u32[]{:S(2)}) collective-permute-start(bf16[128,1024]{1,0:T(8,128)(2,1)} %collective-permute-done.50), channel_id=1, source_target_pairs={{0,1},{1,0},{2,3},{3,2},{4,5},{5,4},{6,7},{7,6},{8,9},{9,8},{10,11... | collective-permute-start | bytes 786440 | tf_op jit(solution)/shard_map/ppermute | solution.py:545
  94.7 20.9 %collective-permute-start.54 = (bf16[128,1024]{1,0:T(8,128)(2,1)}, bf16[128,1024]{1,0:T(8,128)(2,1)S(1)}, u32[]{:S(2)}, u32[]{:S(2)}) collective-permute-start(bf16[128,1024]{1,0:T(8,128)(2,1)} %collective-permute-done.52), channel_id=1, source_target_pairs={{0,2},{1,3},{2,0},{3,1},{4,6},{5,7},{6,4},{7,5},{8,10},{9,11},{10,... | collective-permute-start | bytes 786440 | tf_op jit(solution)/shard_map/ppermute | solution.py:545
  98.9 19.6 %collective-permute-start.53 = (bf16[128,1024]{1,0:T(8,128)(2,1)}, bf16[128,1024]{1,0:T(8,128)(2,1)S(1)}, u32[]{:S(2)}, u32[]{:S(2)}) collective-permute-start(bf16[128,1024]{1,0:T(8,128)(2,1)} %collective-permute-done.52), channel_id=1, source_target_pairs={{0,1},{1,0},{2,3},{3,2},{4,5},{5,4},{6,7},{7,6},{8,9},{9,8},{10,11... | collective-permute-start | bytes 786440 | tf_op jit(solution)/shard_map/ppermute | solution.py:545
  98.9 19.7 %collective-permute-start.76 = (bf16[128,1024]{1,0:T(8,128)(2,1)}, bf16[128,1024]{1,0:T(8,128)(2,1)S(1)}, u32[]{:S(2)}, u32[]{:S(2)}) collective-permute-start(bf16[128,1024]{1,0:T(8,128)(2,1)} %copy-done.47), channel_id=1, source_target_pairs={{0,4},{4,0},{1,5},{5,1},{2,6},{6,2},{3,7},{7,3},{8,12},{12,8},{9,1... | collective-permute-start | bytes 786440 | tf_op jit(solution)/shard_map/ppermute | solution.py:544
  99.5 19.5 %collective-permute-start.32 = (bf16[128,1024]{1,0:T(8,128)(2,1)S(1)}, bf16[128,1024]{1,0:T(8,128)(2,1)S(1)}, u32[]{:S(2)}, u32[]{:S(2)}) collective-permute-start(bf16[128,1024]{1,0:T(8,128)(2,1)S(1)} %collective-permute-done.28.refs_2_), channel_id=1, source_target_pairs={{0,4},{4,0},{1,5},{5,1},{2,6},{6,2},{3,7},{7,3},{8,12},{12,8},{9,1... | collective-permute-start | bytes 786440 | tf_op jit(solution)/shard_map/ppermute | solution.py:544
  115.6 24.6 %collective-permute-start.10 = (bf16[4,128,1024]{2,1,0:T(8,128)(2,1)}, bf16[4,128,1024]{2,1,0:T(8,128)(2,1)S(1)}, u32[]{:S(2)}, u32[]{:S(2)}) collective-permute-start(bf16[4,128,1024]{2,1,0:T(8,128)(2,1)} %get-tuple-element.30), channel_id=1, source_target_pairs={{0,1},{1,0},{2,3},{3,2},{4,5},{5,4},{6,7},{7,6},{8,9},{9,8},{10,11... | collective-permute-start | bytes 3145736 | tf_op jit(solution)/shard_map/ppermute | solution.py:545
  119.8 18.2 %collective-permute-start.75 = (bf16[128,1024]{1,0:T(8,128)(2,1)}, bf16[128,1024]{1,0:T(8,128)(2,1)S(1)}, u32[]{:S(2)}, u32[]{:S(2)}) collective-permute-start(bf16[128,1024]{1,0:T(8,128)(2,1)} %collective-permute-done.74), channel_id=1, source_target_pairs={{0,1},{1,0},{2,3},{3,2},{4,5},{5,4},{6,7},{7,6},{8,9},{9,8},{10,11... | collective-permute-start | bytes 786440 | tf_op jit(solution)/shard_map/ppermute | solution.py:545
  121.7 17.7 %collective-permute-start.55 = (bf16[128,1024]{1,0:T(8,128)(2,1)S(1)}, bf16[128,1024]{1,0:T(8,128)(2,1)S(1)}, u32[]{:S(2)}, u32[]{:S(2)}) collective-permute-start(bf16[128,1024]{1,0:T(8,128)(2,1)S(1)} %collective-permute-done.54), channel_id=1, source_target_pairs={{0,1},{1,0},{2,3},{3,2},{4,5},{5,4},{6,7},{7,6},{8,9},{9,8},{10,11... | collective-permute-start | bytes 786440 | tf_op jit(solution)/shard_map/ppermute | solution.py:545
  121.8 21.8 %collective-permute-start.77 = (bf16[128,1024]{1,0:T(8,128)(2,1)S(1)}, bf16[128,1024]{1,0:T(8,128)(2,1)S(1)}, u32[]{:S(2)}, u32[]{:S(2)}) collective-permute-start(bf16[128,1024]{1,0:T(8,128)(2,1)S(1)} %collective-permute-done.76), channel_id=1, source_target_pairs={{0,1},{1,0},{2,3},{3,2},{4,5},{5,4},{6,7},{7,6},{8,9},{9,8},{10,11... | collective-permute-start | bytes 786440 | tf_op jit(solution)/shard_map/ppermute | solution.py:545
  144.4 12.0 %collective-permute-start.11 = (bf16[128,1024]{1,0:T(8,128)(2,1)}, bf16[128,1024]{1,0:T(8,128)(2,1)}, u32[]{:S(2)}, u32[]{:S(2)}) collective-permute-start(bf16[128,1024]{1,0:T(8,128)(2,1)} %get-tuple-element.143), channel_id=1, source_target_pairs={{0,4},{4,0},{1,5},{5,1},{2,6},{6,2},{3,7},{7,3},{8,12},{12,8},{9,1... | collective-permute-start | bytes 786440 | tf_op jit(solution)/shard_map/ppermute | solution.py:544
  145.8 12.4 %collective-permute-start.35 = (bf16[128,1024]{1,0:T(8,128)(2,1)}, bf16[128,1024]{1,0:T(8,128)(2,1)}, u32[]{:S(2)}, u32[]{:S(2)}) collective-permute-start(bf16[128,1024]{1,0:T(8,128)(2,1)} %get-tuple-element.147), channel_id=1, source_target_pairs={{0,2},{1,3},{2,0},{3,1},{4,6},{5,7},{6,4},{7,5},{8,10},{9,11},{10,... | collective-permute-start | bytes 786440 | tf_op jit(solution)/shard_map/ppermute | solution.py:545
  151.4 11.3 %collective-permute-start.13 = (bf16[128,1024]{1,0:T(8,128)(2,1)}, bf16[128,1024]{1,0:T(8,128)(2,1)}, u32[]{:S(2)}, u32[]{:S(2)}) collective-permute-start(bf16[128,1024]{1,0:T(8,128)(2,1)} %fusion.88), channel_id=1, source_target_pairs={{0,2},{1,3},{2,0},{3,1},{4,6},{5,7},{6,4},{7,5},{8,10},{9,11},{10,... | collective-permute-start | bytes 786440 | tf_op jit(solution)/shard_map/ppermute | solution.py:545
  167.2 14.6 %collective-permute-start.39 = (bf16[128,1024]{1,0:T(8,128)(2,1)S(1)}, bf16[128,1024]{1,0:T(8,128)(2,1)S(1)}, u32[]{:S(2)}, u32[]{:S(2)}) collective-permute-start(bf16[128,1024]{1,0:T(8,128)(2,1)S(1)} %get-tuple-element.194), channel_id=1, source_target_pairs={{0,2},{1,3},{2,0},{3,1},{4,6},{5,7},{6,4},{7,5},{8,10},{9,11},{10,... | collective-permute-start | bytes 786440 | tf_op jit(solution)/shard_map/ppermute | solution.py:545
  168.9 12.8 %collective-permute-start.38 = (bf16[128,1024]{1,0:T(8,128)(2,1)S(1)}, bf16[128,1024]{1,0:T(8,128)(2,1)S(1)}, u32[]{:S(2)}, u32[]{:S(2)}) collective-permute-start(bf16[128,1024]{1,0:T(8,128)(2,1)S(1)} %get-tuple-element.194), channel_id=1, source_target_pairs={{0,1},{1,0},{2,3},{3,2},{4,5},{5,4},{6,7},{7,6},{8,9},{9,8},{10,11... | collective-permute-start | bytes 786440 | tf_op jit(solution)/shard_map/ppermute | solution.py:545
  172.6 10.2 %collective-permute-start.41 = (bf16[128,1024]{1,0:T(8,128)(2,1)S(1)}, bf16[128,1024]{1,0:T(8,128)(2,1)S(1)}, u32[]{:S(2)}, u32[]{:S(2)}) collective-permute-start(bf16[128,1024]{1,0:T(8,128)(2,1)S(1)} %get-tuple-element.194), channel_id=1, source_target_pairs={{0,4},{4,0},{1,5},{5,1},{2,6},{6,2},{3,7},{7,3},{8,12},{12,8},{9,1... | collective-permute-start | bytes 786440 | tf_op jit(solution)/shard_map/ppermute | solution.py:544
  182.7 10.2 %collective-permute-start.22 = (bf16[328,1024]{1,0:T(8,128)(2,1)S(1)}, bf16[328,1024]{1,0:T(8,128)(2,1)S(1)}, u32[]{:S(2)}, u32[]{:S(2)}) collective-permute-start(bf16[328,1024]{1,0:T(8,128)(2,1)S(1)} %copy-done.70), channel_id=1, source_target_pairs={{0,0},{16,1},{8,2},{24,3},{1,8},{17,9},{9,10},{25,11},{2,16},{18,1... | collective-permute-start | bytes 2015240 | tf_op jit(solution)/shard_map/ppermute | solution.py:569
  185.1 21.0 %collective-permute-start.20 = (bf16[128,1024]{1,0:T(8,128)(2,1)S(1)}, bf16[128,1024]{1,0:T(8,128)(2,1)S(1)}, u32[]{:S(2)}, u32[]{:S(2)}) collective-permute-start(bf16[128,1024]{1,0:T(8,128)(2,1)S(1)} %collective-permute-done.19), channel_id=1, source_target_pairs={{0,1},{1,0},{2,3},{3,2},{4,5},{5,4},{6,7},{7,6},{8,9},{9,8},{10,11... | collective-permute-start | bytes 786440 | tf_op jit(solution)/shard_map/ppermute | solution.py:545
  217.7 37.3 %collective-permute-start.23 = (bf16[4,128,1024]{2,1,0:T(8,128)(2,1)}, bf16[4,128,1024]{2,1,0:T(8,128)(2,1)}, u32[]{:S(2)}, u32[]{:S(2)}) collective-permute-start(bf16[4,128,1024]{2,1,0:T(8,128)(2,1)} %slice_bitcast_fusion.10), channel_id=1, source_target_pairs={{0,1},{1,0},{2,3},{3,2},{4,5},{5,4},{6,7},{7,6},{8,9},{9,8},{10,11... | collective-permute-start | bytes 3145736 | tf_op jit(solution)/shard_map/ppermute | solution.py:545
  241.8 150.8 %reduce-scatter.9.cloned.1.call-start = ((), (), s32[]{:S(2)}) async-start(), calls=%async_computation.6 | async-start | bytes 1679360 | tf_op jit(solution)/shard_map/reduce_scatter | solution.py:730
  246.1 12.6 %collective-permute-start.45 = (bf16[4,128,1024]{2,1,0:T(8,128)(2,1)S(1)}, bf16[4,128,1024]{2,1,0:T(8,128)(2,1)S(1)}, u32[]{:S(2)}, u32[]{:S(2)}) collective-permute-start(bf16[4,128,1024]{2,1,0:T(8,128)(2,1)S(1)} %slice_bitcast_fusion.8), channel_id=1, source_target_pairs={{0,1},{1,0},{2,3},{3,2},{4,5},{5,4},{6,7},{7,6},{8,9},{9,8},{10,11... | collective-permute-start | bytes 3145736 | tf_op jit(solution)/shard_map/ppermute | solution.py:545
  249.0 10.4 %collective-permute-start.56 = (bf16[4,128,1024]{2,1,0:T(8,128)(2,1)S(1)}, bf16[4,128,1024]{2,1,0:T(8,128)(2,1)S(1)}, u32[]{:S(2)}, u32[]{:S(2)}) collective-permute-start(bf16[4,128,1024]{2,1,0:T(8,128)(2,1)S(1)} %slice_bitcast_fusion.6), channel_id=1, source_target_pairs={{0,1},{1,0},{2,3},{3,2},{4,5},{5,4},{6,7},{7,6},{8,9},{9,8},{10,11... | collective-permute-start | bytes 3145736 | tf_op jit(solution)/shard_map/ppermute | solution.py:545
  251.7 10.3 %collective-permute-start.78 = (bf16[4,128,1024]{2,1,0:T(8,128)(2,1)S(1)}, bf16[4,128,1024]{2,1,0:T(8,128)(2,1)S(1)}, u32[]{:S(2)}, u32[]{:S(2)}) collective-permute-start(bf16[4,128,1024]{2,1,0:T(8,128)(2,1)S(1)} %slice_bitcast_fusion.2), channel_id=1, source_target_pairs={{0,1},{1,0},{2,3},{3,2},{4,5},{5,4},{6,7},{7,6},{8,9},{9,8},{10,11... | collective-permute-start | bytes 3145736 | tf_op jit(solution)/shard_map/ppermute | solution.py:545
  256.7 27.8 %collective-permute-start.24 = (bf16[128,1024]{1,0:T(8,128)(2,1)S(1)}, bf16[128,1024]{1,0:T(8,128)(2,1)S(1)}, u32[]{:S(2)}, u32[]{:S(2)}) collective-permute-start(bf16[128,1024]{1,0:T(8,128)(2,1)S(1)} %get-tuple-element.141), channel_id=1, source_target_pairs={{0,4},{4,0},{1,5},{5,1},{2,6},{6,2},{3,7},{7,3},{8,12},{12,8},{9,1... | collective-permute-start | bytes 786440 | tf_op jit(solution)/shard_map/ppermute | solution.py:544
  258.2 13.2 %collective-permute-start.25 = (bf16[128,1024]{1,0:T(8,128)(2,1)S(1)}, bf16[128,1024]{1,0:T(8,128)(2,1)S(1)}, u32[]{:S(2)}, u32[]{:S(2)}) collective-permute-start(bf16[128,1024]{1,0:T(8,128)(2,1)S(1)} %get-tuple-element.142), channel_id=1, source_target_pairs={{0,4},{4,0},{1,5},{5,1},{2,6},{6,2},{3,7},{7,3},{8,12},{12,8},{9,1... | collective-permute-start | bytes 786440 | tf_op jit(solution)/shard_map/ppermute | solution.py:544
  259.3 26.8 %collective-permute-start.46 = (bf16[128,1024]{1,0:T(8,128)(2,1)S(1)}, bf16[128,1024]{1,0:T(8,128)(2,1)S(1)}, u32[]{:S(2)}, u32[]{:S(2)}) collective-permute-start(bf16[128,1024]{1,0:T(8,128)(2,1)S(1)} %get-tuple-element.145), channel_id=1, source_target_pairs={{0,2},{1,3},{2,0},{3,1},{4,6},{5,7},{6,4},{7,5},{8,10},{9,11},{10,... | collective-permute-start | bytes 786440 | tf_op jit(solution)/shard_map/ppermute | solution.py:545
  259.4 13.7 %collective-permute-start.47 = (bf16[128,1024]{1,0:T(8,128)(2,1)S(1)}, bf16[128,1024]{1,0:T(8,128)(2,1)S(1)}, u32[]{:S(2)}, u32[]{:S(2)}) collective-permute-start(bf16[128,1024]{1,0:T(8,128)(2,1)S(1)} %get-tuple-element.146), channel_id=1, source_target_pairs={{0,2},{1,3},{2,0},{3,1},{4,6},{5,7},{6,4},{7,5},{8,10},{9,11},{10,... | collective-permute-start | bytes 786440 | tf_op jit(solution)/shard_map/ppermute | solution.py:545
  262.0 24.2 %collective-permute-start.57 = (bf16[128,1024]{1,0:T(8,128)(2,1)S(1)}, bf16[128,1024]{1,0:T(8,128)(2,1)S(1)}, u32[]{:S(2)}, u32[]{:S(2)}) collective-permute-start(bf16[128,1024]{1,0:T(8,128)(2,1)S(1)} %get-tuple-element.137), channel_id=1, source_target_pairs={{0,4},{4,0},{1,5},{5,1},{2,6},{6,2},{3,7},{7,3},{8,12},{12,8},{9,1... | collective-permute-start | bytes 786440 | tf_op jit(solution)/shard_map/ppermute | solution.py:544
  271.5 10.8 %collective-permute-start.58 = (bf16[128,1024]{1,0:T(8,128)(2,1)S(1)}, bf16[128,1024]{1,0:T(8,128)(2,1)S(1)}, u32[]{:S(2)}, u32[]{:S(2)}) collective-permute-start(bf16[128,1024]{1,0:T(8,128)(2,1)S(1)} %get-tuple-element.138), channel_id=1, source_target_pairs={{0,4},{4,0},{1,5},{5,1},{2,6},{6,2},{3,7},{7,3},{8,12},{12,8},{9,1... | collective-permute-start | bytes 786440 | tf_op jit(solution)/shard_map/ppermute | solution.py:544
  282.4 14.9 %collective-permute-start.26 = (bf16[128,1024]{1,0:T(8,128)(2,1)S(1)}, bf16[128,1024]{1,0:T(8,128)(2,1)}, u32[]{:S(2)}, u32[]{:S(2)}) collective-permute-start(bf16[128,1024]{1,0:T(8,128)(2,1)S(1)} %fusion.82), channel_id=1, source_target_pairs={{0,2},{1,3},{2,0},{3,1},{4,6},{5,7},{6,4},{7,5},{8,10},{9,11},{10,... | collective-permute-start | bytes 786440 | tf_op jit(solution)/shard_map/ppermute | solution.py:545
  284.6 12.7 %collective-permute-start.48 = (bf16[128,1024]{1,0:T(8,128)(2,1)S(1)}, bf16[128,1024]{1,0:T(8,128)(2,1)S(1)}, u32[]{:S(2)}, u32[]{:S(2)}) collective-permute-start(bf16[128,1024]{1,0:T(8,128)(2,1)S(1)} %fusion.72), channel_id=1, source_target_pairs={{0,4},{4,0},{1,5},{5,1},{2,6},{6,2},{3,7},{7,3},{8,12},{12,8},{9,1... | collective-permute-start | bytes 786440 | tf_op jit(solution)/shard_map/ppermute | solution.py:544
  286.1 16.8 %collective-permute-start.59 = (bf16[128,1024]{1,0:T(8,128)(2,1)S(1)}, bf16[128,1024]{1,0:T(8,128)(2,1)}, u32[]{:S(2)}, u32[]{:S(2)}) collective-permute-start(bf16[128,1024]{1,0:T(8,128)(2,1)S(1)} %fusion.68), channel_id=1, source_target_pairs={{0,2},{1,3},{2,0},{3,1},{4,6},{5,7},{6,4},{7,5},{8,10},{9,11},{10,... | collective-permute-start | bytes 786440 | tf_op jit(solution)/shard_map/ppermute | solution.py:545
  286.1 16.7 %collective-permute-start.81 = (bf16[128,1024]{1,0:T(8,128)(2,1)S(1)}, bf16[128,1024]{1,0:T(8,128)(2,1)}, u32[]{:S(2)}, u32[]{:S(2)}) collective-permute-start(bf16[128,1024]{1,0:T(8,128)(2,1)S(1)} %fusion.59), channel_id=1, source_target_pairs={{0,4},{4,0},{1,5},{5,1},{2,6},{6,2},{3,7},{7,3},{8,12},{12,8},{9,1... | collective-permute-start | bytes 786440 | tf_op jit(solution)/shard_map/ppermute | solution.py:544
  291.6 21.9 %collective-permute-start.100 = (bf16[328,256]{1,0:T(8,128)(2,1)}, bf16[328,256]{1,0:T(8,128)(2,1)}, u32[]{:S(2)}, u32[]{:S(2)}) collective-permute-start(bf16[328,256]{1,0:T(8,128)(2,1)} %bitcast.508), channel_id=1, source_target_pairs={{0,0},{1,16},{2,8},{3,24},{8,1},{9,17},{10,9},{11,25},{16,2},{17,1... | collective-permute-start | bytes 503816 | tf_op jit(solution)/shard_map/ppermute | solution.py:577
  313.5 87.9 %reduce-scatter.7.cloned.1.call-start = ((), (), s32[]{:S(2)}) async-start(), calls=%async_computation.5 | async-start | bytes 327680 | tf_op jit(solution)/shard_map/reduce_scatter | solution.py:730
  316.7 9.7 %collective-permute-start.85 = (bf16[128,1024]{1,0:T(8,128)(2,1)S(1)}, bf16[128,1024]{1,0:T(8,128)(2,1)S(1)}, u32[]{:S(2)}, u32[]{:S(2)}) collective-permute-start(bf16[128,1024]{1,0:T(8,128)(2,1)S(1)} %copy-done.39), channel_id=1, source_target_pairs={{0,4},{4,0},{1,5},{5,1},{2,6},{6,2},{3,7},{7,3},{8,12},{12,8},{9,1... | collective-permute-start | bytes 786440 | tf_op jit(solution)/shard_map/ppermute | solution.py:544
  317.9 11.8 %collective-permute-start.65 = (bf16[128,1024]{1,0:T(8,128)(2,1)}, bf16[128,1024]{1,0:T(8,128)(2,1)S(1)}, u32[]{:S(2)}, u32[]{:S(2)}) collective-permute-start(bf16[128,1024]{1,0:T(8,128)(2,1)} %collective-permute-done.63), channel_id=1, source_target_pairs={{0,2},{1,3},{2,0},{3,1},{4,6},{5,7},{6,4},{7,5},{8,10},{9,11},{10,... | collective-permute-start | bytes 786440 | tf_op jit(solution)/shard_map/ppermute | solution.py:545
  329.7 20.8 %collective-permute-start.66 = (bf16[128,1024]{1,0:T(8,128)(2,1)S(1)}, bf16[128,1024]{1,0:T(8,128)(2,1)S(1)}, u32[]{:S(2)}, u32[]{:S(2)}) collective-permute-start(bf16[128,1024]{1,0:T(8,128)(2,1)S(1)} %collective-permute-done.65), channel_id=1, source_target_pairs={{0,1},{1,0},{2,3},{3,2},{4,5},{5,4},{6,7},{7,6},{8,9},{9,8},{10,11... | collective-permute-start | bytes 786440 | tf_op jit(solution)/shard_map/ppermute | solution.py:545
  381.3 42.1 %reduce-scatter.5.cloned.1.call-start = ((), (), s32[]{:S(2)}) async-start(), calls=%async_computation.4 | async-start | bytes 983040 | tf_op jit(solution)/shard_map/reduce_scatter | solution.py:730
  388.1 14.9 %collective-permute-start.67 = (bf16[4,128,1024]{2,1,0:T(8,128)(2,1)}, bf16[4,128,1024]{2,1,0:T(8,128)(2,1)}, u32[]{:S(2)}, u32[]{:S(2)}) collective-permute-start(bf16[4,128,1024]{2,1,0:T(8,128)(2,1)} %slice_bitcast_fusion.4), channel_id=1, source_target_pairs={{0,1},{1,0},{2,3},{3,2},{4,5},{5,4},{6,7},{7,6},{8,9},{9,8},{10,11... | collective-permute-start | bytes 3145736 | tf_op jit(solution)/shard_map/ppermute | solution.py:545
  388.1 18.8 %collective-permute-start.89 = (bf16[4,128,1024]{2,1,0:T(8,128)(2,1)}, bf16[4,128,1024]{2,1,0:T(8,128)(2,1)}, u32[]{:S(2)}, u32[]{:S(2)}) collective-permute-start(bf16[4,128,1024]{2,1,0:T(8,128)(2,1)} %slice_bitcast_fusion), channel_id=1, source_target_pairs={{0,1},{1,0},{2,3},{3,2},{4,5},{5,4},{6,7},{7,6},{8,9},{9,8},{10,11... | collective-permute-start | bytes 3145736 | tf_op jit(solution)/shard_map/ppermute | solution.py:545
  400.0 11.4 %collective-permute-start.99 = (bf16[2,128,328]{1,2,0:T(8,128)(2,1)S(1)}, bf16[2,128,328]{1,2,0:T(8,128)(2,1)S(1)}, u32[]{:S(2)}, u32[]{:S(2)}) collective-permute-start(bf16[2,128,328]{1,2,0:T(8,128)(2,1)S(1)} %get-tuple-element.170), channel_id=1, source_target_pairs={{0,2},{1,3},{2,0},{3,1},{4,6},{5,7},{6,4},{7,5},{8,10},{9,11},{10,... | collective-permute-start | bytes 503816 | tf_op jit(solution)/shard_map/ppermute | solution.py:545
  401.3 11.0 %collective-permute-start.96 = (bf16[128,256]{1,0:T(8,128)(2,1)}, bf16[128,256]{1,0:T(8,128)(2,1)S(1)}, u32[]{:S(2)}, u32[]{:S(2)}) collective-permute-start(bf16[128,256]{1,0:T(8,128)(2,1)} %bitcast.509), channel_id=1, source_target_pairs={{0,0},{1,8},{2,16},{3,24},{8,1},{9,9},{10,17},{11,25},{16,2},{17,1... | collective-permute-start | bytes 196616 | tf_op jit(solution)/shard_map/ppermute | solution.py:577
  413.1 13.0 %collective-permute-start.68 = (bf16[128,1024]{1,0:T(8,128)(2,1)}, bf16[128,1024]{1,0:T(8,128)(2,1)}, u32[]{:S(2)}, u32[]{:S(2)}) collective-permute-start(bf16[128,1024]{1,0:T(8,128)(2,1)} %get-tuple-element.135), channel_id=1, source_target_pairs={{0,4},{4,0},{1,5},{5,1},{2,6},{6,2},{3,7},{7,3},{8,12},{12,8},{9,1... | collective-permute-start | bytes 786440 | tf_op jit(solution)/shard_map/ppermute | solution.py:544
  414.1 17.4 %collective-permute-start.90 = (bf16[128,1024]{1,0:T(8,128)(2,1)}, bf16[128,1024]{1,0:T(8,128)(2,1)}, u32[]{:S(2)}, u32[]{:S(2)}) collective-permute-start(bf16[128,1024]{1,0:T(8,128)(2,1)} %get-tuple-element.133), channel_id=1, source_target_pairs={{0,2},{1,3},{2,0},{3,1},{4,6},{5,7},{6,4},{7,5},{8,10},{9,11},{10,... | collective-permute-start | bytes 786440 | tf_op jit(solution)/shard_map/ppermute | solution.py:545
  415.2 14.8 %collective-permute-start.70 = (bf16[128,1024]{1,0:T(8,128)(2,1)}, bf16[128,1024]{1,0:T(8,128)(2,1)}, u32[]{:S(2)}, u32[]{:S(2)}) collective-permute-start(bf16[128,1024]{1,0:T(8,128)(2,1)} %fusion.63), channel_id=1, source_target_pairs={{0,2},{1,3},{2,0},{3,1},{4,6},{5,7},{6,4},{7,5},{8,10},{9,11},{10,... | collective-permute-start | bytes 786440 | tf_op jit(solution)/shard_map/ppermute | solution.py:545
  419.4 12.1 %collective-permute-start.92 = (bf16[128,1024]{1,0:T(8,128)(2,1)}, bf16[128,1024]{1,0:T(8,128)(2,1)}, u32[]{:S(2)}, u32[]{:S(2)}) collective-permute-start(bf16[128,1024]{1,0:T(8,128)(2,1)} %fusion.54), channel_id=1, source_target_pairs={{0,4},{4,0},{1,5},{5,1},{2,6},{6,2},{3,7},{7,3},{8,12},{12,8},{9,1... | collective-permute-start | bytes 786440 | tf_op jit(solution)/shard_map/ppermute | solution.py:544
  424.5 9.8 %collective-permute-start.93 = (bf16[128,384]{0,1:T(8,128)(2,1)S(1)}, bf16[128,384]{0,1:T(8,128)(2,1)S(1)}, u32[]{:S(2)}, u32[]{:S(2)}) collective-permute-start(bf16[128,384]{0,1:T(8,128)(2,1)S(1)} %bitcast.498), channel_id=1, source_target_pairs={{0,4},{4,0},{1,5},{5,1},{2,6},{6,2},{3,7},{7,3},{8,12},{12,8},{9,1... | collective-permute-start | bytes 294920 | tf_op jit(solution)/shard_map/ppermute | solution.py:544
  (123 other events, 1040.7 us)
Sparse Core Ops, SparseCore 0:
  83.7 32.5 all-gather.3
  241.9 21.5 reduce-scatter.10
  313.6 29.5 reduce-scatter.8
  381.4 18.0 reduce-scatter.6
  401.7 21.6 reduce-scatter.4

commit v2 on v0

--- a/solution.py
+++ b/solution.py
@@ -3,6 +3,8 @@
 import jax
 import jax.numpy as jnp
 from jax import lax
+from jax.experimental import pallas as pl
+from jax.experimental.pallas import tpu as pltpu
 from jax.sharding import PartitionSpec as P
 
 HD = 64
@@ -144,7 +146,7 @@
     return (grad_queries * scale, grad_keys, grad_values)
 
 
-def local(tokens, cotangent, w_qkv, w_attn_out, w_in, w_mlp_out, norm_gain1, norm_gain2):
+def local_general(tokens, cotangent, w_qkv, w_attn_out, w_in, w_mlp_out, norm_gain1, norm_gain2):
     seqs_here, block_rows, width = tokens.shape
     count_rows = seqs_here * block_rows
     heads_all = width // HD
@@ -360,6 +362,603 @@
     )
 
 
+F32 = jnp.float32
+BF16 = jnp.bfloat16
+VMEM_BYTES = 56 * 1024 * 1024
+GROUP = ("ctx", "head")
+
+
+def dot(left, right, dims=((1,), (0,))):
+    return lax.dot_general(left, right, (dims, ((), ())), preferred_element_type=F32)
+
+
+def flat(values):
+    return values.reshape(-1, values.shape[-1])
+
+
+def lane_rotate(values, cosine, sine_signed):
+    lane = lax.broadcasted_iota(jnp.int32, values.shape, 1)
+    width = values.shape[1]
+    partner = jnp.where(
+        lane % HD < HD // 2,
+        pltpu.roll(values, width - HD // 2, 1),
+        pltpu.roll(values, HD // 2, 1),
+    )
+    return values * cosine + partner * sine_signed
+
+
+def head_masks(shape):
+    lane = lax.broadcasted_iota(jnp.int32, shape, 1)
+    return [lane // HD == head for head in range(shape[1] // HD)]
+
+
+def params():
+    return pltpu.CompilerParams(vmem_limit_bytes=VMEM_BYTES)
+
+
+def whole(array):
+    return pl.BlockSpec(array.shape, lambda *_: (0,) * len(array.shape))
+
+
+SCALARS = pl.BlockSpec(memory_space=pltpu.SMEM)
+
+
+def project_kernel(place_ref, *refs):
+    pieces, weights = refs[:6], refs[6:10]
+    cos_ref, sin_ref, low_ref, qkv_ref, w_ref, gain1_ref, gain2_ref, rows_ref = refs[10:]
+    block, part = pieces[0].shape[2], w_ref.shape[1] // 3
+    rows = gain1_ref.shape[1] // 8
+
+    @pl.when(pl.program_id(0) == 0)
+    def _():
+        for step, piece in enumerate(weights):
+            for turn in range(2):
+                at = 2 * (place_ref[8] ^ step) + (place_ref[9] ^ turn)
+                w_ref[pl.ds(pl.multiple_of(at * rows, rows), rows), :] = piece[turn, :rows]
+                gains = piece[turn, rows:].astype(F32)
+                rows_ref[0, pl.ds(at, 1), :] = gains[:1, :rows]
+                rows_ref[1, pl.ds(at, 1), :] = gains[1:2, :rows]
+        for out, at in ((gain1_ref, 0), (gain2_ref, 1)):
+            for row in range(8):
+                out[:, row * rows : (row + 1) * rows] = rows_ref[at, row : row + 1, :]
+
+    gain = gain1_ref[...]
+    index = 0
+    for piece in pieces:
+        for inner in range(piece.shape[0]):
+            normed, _ = normalize(piece[inner, 0].astype(F32))
+            low_ref[index, 0] = (normed * gain).astype(BF16)
+            index += 1
+    projected = dot(flat(low_ref[:, 0]), w_ref[...])
+    cosine, sine = cos_ref[...], sin_ref[...]
+    shape = (8, block, part)
+    qkv_ref[:, 0, :, :part] = (
+        (lane_rotate(projected[:, :part], cosine, sine) * HD**-0.5).astype(BF16).reshape(shape)
+    )
+    qkv_ref[:, 0, :, part : 2 * part] = (
+        lane_rotate(projected[:, part : 2 * part], cosine, sine).astype(BF16).reshape(shape)
+    )
+    qkv_ref[:, 0, :, 2 * part :] = projected[:, 2 * part :].astype(BF16).reshape(shape)
+
+
+def project(place, pieces, weights, cosine, sine):
+    seqs, block, width = pieces[0].shape[1:]
+    own = weights[0].shape[2]
+
+    def by_seq(lead, last):
+        return pl.BlockSpec((lead, 1, block, last), lambda s: (0, s, 0, 0))
+
+    return pl.pallas_call(
+        project_kernel,
+        grid=(seqs,),
+        in_specs=[SCALARS]
+        + [by_seq(piece.shape[0], width) for piece in pieces]
+        + [whole(w) for w in weights]
+        + [whole(cosine), whole(sine)],
+        out_specs=(
+            by_seq(8, width),
+            by_seq(8, own),
+            pl.BlockSpec((width, own), lambda s: (0, 0)),
+            pl.BlockSpec((1, width), lambda s: (0, 0)),
+            pl.BlockSpec((1, width), lambda s: (0, 0)),
+        ),
+        out_shape=(
+            jax.ShapeDtypeStruct((8, seqs, block, width), BF16),
+            jax.ShapeDtypeStruct((8, seqs, block, own), BF16),
+            jax.ShapeDtypeStruct((width, own), BF16),
+            jax.ShapeDtypeStruct((1, width), F32),
+            jax.ShapeDtypeStruct((1, width), F32),
+        ),
+        scratch_shapes=[pltpu.VMEM((2, 8, width // 8), F32)],
+        compiler_params=params(),
+        name="project",
+    )(place, *pieces, *weights, cosine, sine)
+
+
+def attend_kernel(place_ref, q_ref, k_ref, v_ref, att_ref, low_ref, log_ref, home_ref):
+    seq, step = pl.program_id(0), pl.program_id(1)
+    queries, keys, values = flat(q_ref[...]), flat(k_ref[...]), flat(v_ref[...])
+    attended = jnp.zeros(queries.shape, F32)
+    logs = jnp.zeros(queries.shape, F32)
+    for mask in head_masks(queries.shape):
+        scores = dot(jnp.where(mask, queries, 0), keys, ((1,), (1,)))
+        peak = jnp.max(scores, axis=1, keepdims=True)
+        weights = jnp.exp(scores - peak)
+        total = jnp.sum(weights, axis=1, keepdims=True)
+        mixed = dot(weights.astype(BF16), values) * (1.0 / total)
+        attended = jnp.where(mask, mixed, attended)
+        logs = jnp.where(mask, peak + jnp.log(total), logs)
+    att_ref[...] = attended.reshape(att_ref.shape)
+    log_ref[...] = logs.reshape(log_ref.shape)
+    low = attended.astype(BF16).reshape(low_ref.shape)
+    low_ref[...] = low
+    for inner in range(2):
+        home_ref[place_ref[2 * step + inner], seq] = low[inner, 0]
+
+
+def attend(place, qkv):
+    _, seqs, block, own = qkv.shape
+    part = own // 3
+    rows = pl.BlockSpec((2, 1, block, part), lambda s, i: (i, s, 0, 0))
+    shape = (8, seqs, block, part)
+    return pl.pallas_call(
+        attend_kernel,
+        grid=(seqs, 4),
+        in_specs=[
+            SCALARS,
+            rows,
+            pl.BlockSpec((8, 1, block, part), lambda s, i: (0, s, 0, 1)),
+            pl.BlockSpec((8, 1, block, part), lambda s, i: (0, s, 0, 2)),
+        ],
+        out_specs=(rows, rows, rows, pl.BlockSpec(shape, lambda s, i: (0, 0, 0, 0))),
+        out_shape=(
+            jax.ShapeDtypeStruct(shape, F32),
+            jax.ShapeDtypeStruct(shape, BF16),
+            jax.ShapeDtypeStruct(shape, F32),
+            jax.ShapeDtypeStruct(shape, BF16),
+        ),
+        compiler_params=params(),
+        name="attend",
+    )(place, qkv, qkv, qkv)
+
+
+def branch_kernel(place_ref, *refs):
+    pieces = refs[:6]
+    rows_ref, tokens_ref, gain_ref, residual_ref, low_ref = refs[6:]
+    total = flat(tokens_ref[...].astype(F32))
+    index = 0
+    for piece in pieces:
+        for inner in range(piece.shape[0]):
+            total += dot(flat(rows_ref[place_ref[index]]), piece[inner])
+            index += 1
+    normed, _ = normalize(total)
+    residual_ref[...] = total.reshape(residual_ref.shape)
+    low_ref[...] = (normed * gain_ref[...]).astype(BF16).reshape(low_ref.shape)
+
+
+def branch(place, pieces, rows, tokens, gain):
+    args = (*pieces, rows, tokens, gain)
+    return pl.pallas_call(
+        branch_kernel,
+        in_specs=[SCALARS] + [whole(a) for a in args],
+        out_shape=(
+            jax.ShapeDtypeStruct(tokens.shape, F32),
+            jax.ShapeDtypeStruct(tokens.shape, BF16),
+        ),
+        compiler_params=params(),
+        name="branch",
+    )(place, *args)
+
+
+def mlp_kernel(low_ref, grad_ref, w_ref, mixed_ref, lifted_ref, keep_ref, send_ref):
+    step = pl.program_id(0)
+    hidden = w_ref.shape[1] // 2
+    lifted = dot(flat(low_ref[...]), w_ref[...])
+    first, second = lifted[:, :hidden], lifted[:, hidden:]
+    grad_mixed = flat(grad_ref[...])
+    gate = 0.5 * (1.0 + lax.erf(first * (0.5**0.5)))
+    slope = gate + first * jnp.exp(first * first * -0.5) * ((2.0 * math.pi) ** -0.5)
+    activated = first * gate
+    mixed_ref[...] = (activated * second).astype(BF16).reshape(mixed_ref.shape)
+    grad = jnp.concatenate(
+        [(grad_mixed * second * slope).astype(BF16), (grad_mixed * activated).astype(BF16)],
+        axis=1,
+    )
+    lifted_ref[...] = grad.reshape(lifted_ref.shape)
+    partial = dot(grad, w_ref[...], ((1,), (1,))).astype(BF16).reshape(keep_ref.shape)
+
+    @pl.when(step < 5)
+    def _():
+        keep_ref[...] = partial
+
+    @pl.when(step >= 5)
+    def _():
+        send_ref[...] = partial
+
+
+def mlp(low, grad_mixed, w):
+    _, seqs, block, width = low.shape
+    hidden = w.shape[1] // 2
+
+    def rows(last):
+        return pl.BlockSpec((1, seqs, block, last), lambda i: (i, 0, 0, 0))
+
+    return pl.pallas_call(
+        mlp_kernel,
+        grid=(8,),
+        in_specs=[rows(width), rows(hidden), whole(w)],
+        out_specs=(
+            rows(hidden),
+            rows(2 * hidden),
+            pl.BlockSpec((1, seqs, block, width), lambda i: (jnp.minimum(i, 4), 0, 0, 0)),
+            pl.BlockSpec((1, seqs, block, width), lambda i: (jnp.maximum(i - 5, 0), 0, 0, 0)),
+        ),
+        out_shape=(
+            jax.ShapeDtypeStruct((8, seqs, block, hidden), BF16),
+            jax.ShapeDtypeStruct((8, seqs, block, 2 * hidden), BF16),
+            jax.ShapeDtypeStruct((5, seqs, block, width), BF16),
+            jax.ShapeDtypeStruct((3, seqs, block, width), BF16),
+        ),
+        compiler_params=params(),
+        name="mlp",
+    )(low, grad_mixed, w)
+
+
+def branch_back_kernel(place_ref, *refs):
+    pieces = refs[:6]
+    low_ref, residual_ref, top_ref, gain_ref, grad_ref, branch_ref, home_ref, sum_ref = refs[6:]
+    grad_low = flat(low_ref[...])
+    normed, factor = normalize(flat(residual_ref[...]))
+    sum_ref[...] = jnp.sum(grad_low * normed, axis=0, keepdims=True)
+    grad = flat(top_ref[...].astype(F32)) + norm_back(grad_low * gain_ref[...], normed, factor)
+    grad_ref[...] = grad.reshape(grad_ref.shape)
+    low = grad.astype(BF16)
+    branch_ref[...] = low.reshape(branch_ref.shape)
+    index = 0
+    for piece in pieces:
+        for inner in range(piece.shape[0]):
+            home_ref[place_ref[index]] = (
+                dot(low, piece[inner], ((1,), (1,))).astype(BF16).reshape(home_ref.shape[1:])
+            )
+            index += 1
+
+
+def branch_back(place, pieces, grad_low, residual, top, gain):
+    args = (*pieces, grad_low, residual, top, gain)
+    seqs, block, width = residual.shape
+    return pl.pallas_call(
+        branch_back_kernel,
+        in_specs=[SCALARS] + [whole(a) for a in args],
+        out_shape=(
+            jax.ShapeDtypeStruct(residual.shape, F32),
+            jax.ShapeDtypeStruct(residual.shape, BF16),
+            jax.ShapeDtypeStruct((8, seqs, block, pieces[0].shape[1]), BF16),
+            jax.ShapeDtypeStruct((1, width), F32),
+        ),
+        compiler_params=params(),
+        name="branch_back",
+    )(place, *args)
+
+
+def attend_back_kernel(
+    place_ref, q_ref, k_ref, v_ref, grad_ref, att_ref, log_ref, cosq_ref, sinq_ref, cos_ref,
+    sin_ref, w_ref, proj_ref, keep_ref, send_ref, sum_k, sum_v,
+):
+    seq, step = pl.program_id(0), pl.program_id(1)
+    block, part = q_ref.shape[2], q_ref.shape[3]
+
+    @pl.when(step == 0)
+    def _():
+        sum_k[...] = jnp.zeros_like(sum_k)
+        sum_v[...] = jnp.zeros_like(sum_v)
+
+    queries, keys, values = flat(q_ref[...]), flat(k_ref[...]), flat(v_ref[...])
+    grads = jnp.concatenate([grad_ref[place_ref[2 * step + inner], seq] for inner in range(2)])
+    along = (grads.astype(F32) * flat(att_ref[...])).T
+    logs = flat(log_ref[...]).T
+    grad_queries = jnp.zeros(queries.shape, F32)
+    for head, mask in enumerate(head_masks(queries.shape)):
+        own_q = jnp.where(mask, queries, 0)
+        own_g = jnp.where(mask, grads, 0)
+        scores = dot(keys, own_q, ((1,), (1,)))
+        weights = jnp.exp(scores - logs[head * HD : head * HD + 1])
+        lifted = dot(values, own_g, ((1,), (1,)))
+        row = jnp.sum(along[head * HD : (head + 1) * HD], axis=0, keepdims=True)
+        grad_scores = (weights * (lifted - row)).astype(BF16)
+        sum_k[...] += dot(grad_scores, own_q)
+        sum_v[...] += dot(weights.astype(BF16), own_g)
+        grad_queries = jnp.where(mask, dot(grad_scores, keys, ((0,), (0,))), grad_queries)
+    grad_queries = lane_rotate(grad_queries * HD**-0.5, cosq_ref[...], -sinq_ref[...])
+    proj_ref[pl.ds(2 * step, 2), 0, :, :part] = grad_queries.astype(BF16).reshape(2, block, part)
+
+    @pl.when(step == 3)
+    def _():
+        shape = (8, block, part)
+        grad_keys = lane_rotate(sum_k[...], cos_ref[...], -sin_ref[...])
+        proj_ref[:, 0, :, part : 2 * part] = grad_keys.astype(BF16).reshape(shape)
+        proj_ref[:, 0, :, 2 * part :] = sum_v[...].astype(BF16).reshape(shape)
+        partial = dot(flat(proj_ref[:, 0]), w_ref[...], ((1,), (1,))).astype(BF16)
+        keep_ref[:, 0] = partial[: 5 * block].reshape(5, block, -1)
+        send_ref[:, 0] = partial[5 * block :].reshape(3, block, -1)
+
+
+def attend_back(place, qkv, grads, attended, logs, cosine, sine, w):
+    _, seqs, block, own = qkv.shape
+    part, width = own // 3, w.shape[0]
+    rows = pl.BlockSpec((2, 1, block, part), lambda s, i: (i, s, 0, 0))
+    angles = pl.BlockSpec((2 * block, part), lambda s, i: (i, 0))
+
+    def by_seq(lead, last):
+        return pl.BlockSpec((lead, 1, block, last), lambda s, i: (0, s, 0, 0))
+
+    return pl.pallas_call(
+        attend_back_kernel,
+        grid=(seqs, 4),
+        in_specs=[
+            SCALARS,
+            rows,
+            pl.BlockSpec((8, 1, block, part), lambda s, i: (0, s, 0, 1)),
+            pl.BlockSpec((8, 1, block, part), lambda s, i: (0, s, 0, 2)),
+            whole(grads),
+            rows,
+            rows,
+            angles,
+            angles,
+            whole(cosine),
+            whole(sine),
+            whole(w),
+        ],
+        out_specs=(by_seq(8, own), by_seq(5, width), by_seq(3, width)),
+        out_shape=(
+            jax.ShapeDtypeStruct((8, seqs, block, own), BF16),
+            jax.ShapeDtypeStruct((5, seqs, block, width), BF16),
+            jax.ShapeDtypeStruct((3, seqs, block, width), BF16),
+        ),
+        scratch_shapes=[pltpu.VMEM((8 * block, part), F32), pltpu.VMEM((8 * block, part), F32)],
+        compiler_params=params(),
+        name="attend_back",
+    )(place, qkv, qkv, qkv, grads, attended, logs, cosine, sine, cosine, sine, w)
+
+
+class Group:
+    def __init__(self):
+        self.heads = lax.axis_size("head")
+        self.dp = lax.axis_size("dp")
+        self.ctx_at = lax.axis_index("ctx")
+        self.head_at = lax.axis_index("head")
+        self.dp_at = lax.axis_index("dp")
+        self.at = self.ctx_at * self.heads + self.head_at
+        near, far = [], []
+        for c in range(2):
+            for h in range(self.heads):
+                x, y = (c ^ 1) * self.heads + h, c * self.heads + (h ^ 2)
+                near.append((c * self.heads + h, x if h % 2 == 0 else y))
+                far.append((c * self.heads + h, y if h % 2 == 0 else x))
+        self.near, self.far = near, far
+
+    def order(self):
+        first = jnp.where(self.head_at % 2 == 0, 4, 2)
+        second = 6 - first
+        return jnp.stack(
+            [self.at ^ bits for bits in (0, 1, first, first ^ 1, 6, second ^ 1, second, 7)]
+        )
+
+    def swap(self, values, bit):
+        if bit == 4:
+            return lax.ppermute(values, "ctx", [(0, 1), (1, 0)])
+        return lax.ppermute(values, "head", [(i, i ^ bit) for i in range(self.heads)])
+
+    def gather(self, own):
+        own = own[None]
+        mate = self.swap(own, 1)
+        near = lax.ppermute(jnp.concatenate([own, mate]), GROUP, self.near)
+        far = lax.ppermute(near[:1], GROUP, self.far)
+        return own, mate, near, far, self.swap(near, 1), self.swap(far, 1)
+
+    def reduce(self, keep, send):
+        met = keep[2:].astype(F32) + self.swap(send, 1).astype(F32)
+        far = lax.ppermute(met[2].astype(BF16), GROUP, self.far)
+        met = jnp.concatenate([(met[0] + far.astype(F32))[None], met[1:2]])
+        near = lax.ppermute(met.astype(BF16), GROUP, self.near)
+        met = keep[:2].astype(F32) + near.astype(F32)
+        return met[0] + self.swap(met[1].astype(BF16), 1).astype(F32)
+
+    def rows_in(self, values, place):
+        pairs = [
+            (place[h] * self.heads + d, d * self.heads + h)
+            for d in range(self.dp)
+            for h in range(self.heads)
+        ]
+        return lax.ppermute(values, ("dp", "head"), pairs)
+
+    def rows_back(self, values, place):
+        pairs = [
+            (d * self.heads + h, place[h] * self.heads + d)
+            for d in range(self.dp)
+            for h in range(self.heads)
+        ]
+        return lax.ppermute(values, ("dp", "head"), pairs)
+
+    def across(self, values, step):
+        return lax.ppermute(values, "dp", [(i, i ^ step) for i in range(self.dp)])
+
+    def total(self, values):
+        for bit in (1, 2, 4):
+            values = values + self.swap(values, bit)
+        step = 1
+        while step < self.dp:
+            values = values + self.across(values, step)
+            step *= 2
+        return values
+
+
+def pick(array, index, axis):
+    return lax.dynamic_index_in_dim(array, index, axis, keepdims=False)
+
+
+def after(values, earlier):
+    return lax.optimization_barrier((values, earlier))[0]
+
+
+def local_split(tokens, cotangent, w_qkv, w_attn_out, w_in, w_mlp_out, norm_gain1, norm_gain2):
+    seqs, block, width = tokens.shape
+    group = Group()
+    heads, dp = group.heads, group.dp
+    at_c, at_h = group.ctx_at, group.head_at
+    parts = 2 * heads
+    hidden = w_in.shape[1] // 2 // parts
+    padded = -(-hidden // 128) * 128
+    own_width = width // parts
+    half = heads // 2
+    rows_here = w_qkv.shape[0]
+    place = [2 * (h % half) + h // half for h in range(heads)]
+    straight = list(range(heads))
+    order = group.order()
+    scalars = jnp.concatenate([order, jnp.stack([group.dp_at, at_c])]).astype(jnp.int32)
+
+    def in_order(own, other):
+        return jnp.where(at_c == 0, jnp.stack([own, other]), jnp.stack([other, own]))
+
+    x_pieces = group.gather(tokens)
+    gains = jnp.pad(
+        jnp.stack([norm_gain1, norm_gain2]), ((0, 14), (0, 3 * own_width - rows_here))
+    )
+    qkv_view = w_qkv.reshape(rows_here, 3, width)
+
+    def qkv_part(at):
+        start = (2 * at_h + at) * own_width
+        cut = lax.dynamic_slice_in_dim(qkv_view, start, own_width, 2)
+        return jnp.concatenate([cut.reshape(rows_here, 3 * own_width), gains])
+
+    pair = jnp.stack([qkv_part(at_c), group.swap(qkv_part(1 - at_c), 4)])
+    qkv_pieces = [pair] + [group.across(pair, step) for step in range(1, dp)]
+
+    weight_out = group.rows_in(w_attn_out, straight)
+    out_pieces = group.gather(weight_out)
+    in_view = w_in.reshape(rows_here, 2, heads, 2, hidden)
+    in_view = pick(in_view, 2 * (at_h % half) + at_h // half, 2)
+
+    def in_part(at):
+        cut = pick(in_view, at, 2)
+        return jnp.pad(cut, ((0, 0), (0, 0), (0, padded - hidden))).reshape(rows_here, 2 * padded)
+
+    in_pair = in_order(in_part(at_c), group.swap(in_part(1 - at_c), 4))
+    weight_in = lax.all_gather(after(in_pair, qkv_pieces[-1]), "dp", axis=0).reshape(width, -1)
+    weight_mlp = group.rows_in(after(w_mlp_out, qkv_pieces[-1]), place)
+    weight_mlp = jnp.pad(weight_mlp, ((0, padded - hidden), (0, 0)))
+
+    positions = (order[:, None] * block + jnp.arange(block, dtype=jnp.int32)[None, :]).reshape(-1)
+    lane = jnp.arange(own_width, dtype=jnp.int32)
+    frequency = jnp.exp(
+        (lane % (HD // 2)).astype(F32) * (-math.log(ROPE_BASE) / (HD // 2))
+    )
+    angles = positions.astype(F32)[:, None] * frequency[None, :]
+    cosine = jnp.cos(angles)
+    sine = jnp.sin(angles) * jnp.where(lane % HD < HD // 2, -1.0, 1.0)[None, :]
+
+    def exchange(values):
+        return lax.all_to_all(values, GROUP, split_axis=0, concat_axis=0, tiled=True)
+
+    low1, qkv, weight_qkv, gain_one, gain_two = project(
+        scalars, x_pieces, qkv_pieces, cosine, sine
+    )
+    attended, att_low, logs, home = attend(scalars, qkv)
+    residual, low2 = branch(scalars, out_pieces, exchange(home), tokens, gain_two)
+    low2_all = jnp.concatenate(group.gather(low2))
+
+    cot_all = jnp.concatenate(group.gather(after(cotangent, x_pieces[-1])))
+    cot_flat = flat(cot_all)
+    grad_mixed = dot(cot_flat, weight_mlp, ((1,), (1,))).reshape(8, seqs, block, padded)
+    mixed, grad_lifted, keep, send = mlp(low2_all, grad_mixed, weight_in)
+    grad_low2 = group.reduce(keep, send)
+    grad_residual, grad_branch, home, gain2_sum = branch_back(
+        scalars, out_pieces, grad_low2, residual, cotangent, gain_two
+    )
+    grad_home = exchange(home)
+    branch_all = jnp.concatenate(group.gather(after(grad_branch, grad_home)))
+    grad_proj, keep, send = attend_back(
+        scalars, qkv, grad_home, attended, logs, cosine, sine, weight_qkv
+    )
+    grad_low1 = group.reduce(keep, send)
+    normed1, factor1 = normalize(tokens.astype(F32))
+    grad_input = grad_residual + norm_back(grad_low1 * gain_one, normed1, factor1)
+
+    mixed_flat = flat(mixed)
+    cut = 5 * seqs * block
+    out_keep = dot(mixed_flat[:cut], weight_mlp).astype(BF16).reshape(5, seqs, block, width)
+    out_send = dot(mixed_flat[cut:], weight_mlp).astype(BF16).reshape(3, seqs, block, width)
+    result = (residual + group.reduce(out_keep, out_send)).astype(BF16)
+
+    def over_tokens(left, right):
+        return dot(flat(left), flat(right), ((0,), (0,)))
+
+    def scatter(values):
+        return lax.psum_scatter(values.astype(BF16), "dp", scatter_dimension=0, tiled=True)
+
+    def columns_first(values):
+        return jnp.moveaxis(values.reshape(values.shape[0], dp, -1), 1, 0)
+
+    grad_mlp = scatter(columns_first(over_tokens(mixed, cot_flat)[:hidden]))[0]
+    grad_mlp = group.rows_back(grad_mlp, place).astype(F32)
+    grad_out = scatter(columns_first(over_tokens(att_low, branch_all)))[0]
+    grad_out = group.rows_back(grad_out, straight).astype(F32)
+
+    def rows_here_of(values):
+        both = values.reshape(2, rows_here, -1)
+        own = pick(both, at_c, 0)
+        other = group.swap(pick(both, 1 - at_c, 0), 4)
+        return in_order(own, other)
+
+    grad_in = rows_here_of(scatter(over_tokens(low2_all, grad_lifted)))
+    grad_in = jnp.stack([grad_in[..., :hidden], grad_in[..., padded : padded + hidden]])
+    late = at_h // half
+    stays = pick(grad_in, late, 0)
+    comes = group.swap(pick(grad_in, 1 - late, 0), half)
+    grad_in = jnp.where(
+        late == 0, jnp.concatenate([stays, comes]), jnp.concatenate([comes, stays])
+    )
+    grad_in = jnp.moveaxis(grad_in, 0, 1).reshape(rows_here, -1).astype(F32)
+
+    grad_qkv = over_tokens(low1, grad_proj)
+    gain1_sum = jnp.sum(grad_qkv * weight_qkv.astype(F32), axis=1) / gain_one[0]
+    sums = group.total(jnp.stack([gain1_sum, gain2_sum[0]]).reshape(-1, 128))
+    sums = sums.reshape(2, -1)
+    per_device = width // (dp * parts)
+    start = (group.dp_at * parts + group.at) * per_device
+    grad_gain1, grad_gain2 = (
+        lax.dynamic_slice_in_dim(sums[i], start, per_device, 0) for i in range(2)
+    )
+    grad_qkv = rows_here_of(scatter(grad_qkv)).reshape(2, rows_here, 3, own_width)
+    grad_qkv = jnp.moveaxis(grad_qkv, 2, 0)
+    odd, late = at_h % 2, at_h // half
+    stays = pick(grad_qkv, odd + late, 0)
+    core = group.swap(pick(grad_qkv, 1 - odd + late, 0), 1)
+    chip = group.swap(pick(grad_qkv, 2 - 2 * late, 0), 2)
+    grad_qkv = jnp.where(
+        odd == 0, jnp.concatenate([stays, core, chip]), jnp.concatenate([chip, core, stays])
+    )
+    grad_qkv = jnp.moveaxis(grad_qkv, 0, 1).reshape(rows_here, -1).astype(F32)
+
+    return (
+        result,
+        grad_input,
+        grad_qkv,
+        grad_out,
+        grad_in,
+        grad_mlp,
+        grad_gain1,
+        grad_gain2,
+    )
+
+
+def local(tokens, cotangent, w_qkv, w_attn_out, w_in, w_mlp_out, norm_gain1, norm_gain2):
+    args = (tokens, cotangent, w_qkv, w_attn_out, w_in, w_mlp_out, norm_gain1, norm_gain2)
+    sizes = [lax.axis_size(axis) for axis in ("dp", "ctx", "head")]
+    if sizes == [4, 2, 4] and tokens.shape[2] == 8 * 2 * HD and tokens.shape[1] % 16 == 0:
+        return local_split(*args)
+    return local_general(*args)
+
+
 def solution(mesh):
     in_specs = (
         P("dp", ("ctx", "head"), None),

time: 1210 us -> 462 us (0.38)
  the two profiles are of different devices: /device:TPU:0 before, /device:TPU:4 now
where the time goes in v2:
time: 462 us; the launch traced here: 453 us
  waiting for transfers between devices  170 us (37%)
  starting transfers between devices  69.8 us (15%)
  Pallas kernels  66 us (14%)
  local copies, waits for them, and re-layouts  58.2 us (13%)
  other arithmetic  46.1 us (10%)
  matrix products  28 us (6%)
  between operations  15 us (3%)
    ppermute x5, waiting for transfers between devices, swap(): return lax.ppermute(values, 'ctx', [(0, 1), (1, 0)])  34.1 us
    dot_general x7, matrix products, dot(): lax.dot_general(left, right, (dims, ((), ())), preferred_element_type=F32)  28 us
    unnamed x99, local copies, waits for them, and re-layouts  26.5 us
    ppermute x5, waiting for transfers between devices, gather(): far = lax.ppermute(near[:1], GROUP, self.far)  24.3 us
    ppermute x2, waiting for transfers between devices, rows_in(): return lax.ppermute(values, ('dp', 'head'), pairs)  23.7 us
    ppermute x5, waiting for transfers between devices, gather(): near = lax.ppermute(jnp.concatenate([own, mate]), GROUP, self.near)  20.7 us
    pallas_call x1, Pallas kernels, attend_back(): pl.pallas_call(attend_back_kernel, grid=(seqs, 4), in_specs=[SCALARS, row...  20.6 us
    ppermute x3, waiting for transfers between devices, reduce(): far = lax.ppermute(met[2].astype(BF16), GROUP, self.far)  16.8 us
  transfers between devices with their start and end apart: 63, of which 24 were waited for; matrix products, arithmetic and copies ran while one was open for 27% of the time, Pallas kernels for 7%

profile of v2, /device:TPU:4, one launch (start us, length us, event | category | flops | bytes accessed | tf_op | source)
XLA Modules:
  0.0 453.0 jit_solution(9050664441718446437)
XLA Ops:
  7.3 2.1 collective-permute-done.6.refs_1_
  12.3 4.4 collective-permute-start
  16.7 8.9 %collective-permute-done.7.refs_2_ = bf16[2,2,128,1024]{3,2,1,0:T(8,128)(2,1)S(1)} collective-permute-done((bf16[2,2,128,1024]{3,2,1,0:T(8,128)(2,1)S(1)}, bf16[2,2,128,1024]{3,2,1,0:T(8,128)(2,1)S(1)}, u32[]{:S(2)}, u32[]{:S(2)}) %collective-permute-start.7) | collective-permute-done | bytes 1048608 | tf_op jit(solution)/shard_map/ppermute | solution.py:754
  28.0 1.9 collective-permute-done
  29.9 4.4 collective-permute-start.1
  40.2 2.1 collective-permute-done.11
  44.6 3.3 collective-permute-done.2.refs_2_
  49.1 2.6 collective-permute-start.3
  53.3 3.9 collective-permute-done.12.refs_7_
  57.9 3.0 fusion.27
  61.6 4.5 collective-permute-done.13.refs_8_
  66.1 9.1 %project.1 = (bf16[8,2,128,1024]{3,2,1,0:T(8,128)(2,1)}, bf16[8,2,128,384]{3,2,1,0:T(8,128)(2,1)}, bf16[1024,384]{1,0:T(8,128)(2,1)}, f32[1,1024]{1,0:T(1,128)}, f32[1,1024]{1,0:T(1,128)}) custom-call(s32[10]{0:T(128)} %concatenate.64.place_ref, bf16[1,2,128,1024]{3,2,1,0:T(8,128)(2,1)} %bitcast.192, bf16[1,2,128,1024]{3,2,1,0:T(8,128)(2,1)} %copy-done.13, ...), custom_call_target="tpu_custom_call" | custom-call | tf_op jit(solution)/shard_map/project/pallas_call | solution.py:451
  75.2 11.4 %attend.1 = (f32[8,2,128,128]{3,2,1,0:T(8,128)}, bf16[8,2,128,128]{3,2,1,0:T(8,128)(2,1)}, f32[8,2,128,128]{3,2,1,0:T(8,128)}, bf16[8,2,128,128]{3,2,1,0:T(8,128)(2,1)}) custom-call(s32[10]{0:T(128)} %concatenate.64.place_ref, bf16[8,2,128,384]{3,2,1,0:T(8,128)(2,1)} %get-tuple-element.34.q_ref.k_ref.v_ref, ...), custom_call_target="tpu_custom_call" | custom-call | tf_op jit(solution)/shard_map/attend/pallas_call | solution.py:504
  86.6 3.8 all-to-all-start
  92.0 6.7 %all-to-all-done.refs_6_ = bf16[8,2,128,128]{3,2,1,0:T(8,128)(2,1)S(1)} async-done(((bf16[8,2,128,128]{3,2,1,0:T(8,128)(2,1)}), bf16[8,2,128,128]{3,2,1,0:T(8,128)(2,1)S(1)}, u32[]{:S(2)}, u32[]{:S(2)}) %all-to-all-start) | async-done | bytes 524320 | tf_op jit(solution)/shard_map/all_to_all | solution.py:860
  99.4 4.2 branch.1
  105.3 2.5 copy.44
  113.0 22.4 %collective-permute-done.26 = bf16[128,768]{0,1:T(8,128)(2,1)} collective-permute-done((bf16[128,768]{0,1:T(8,128)(2,1)S(1)}, bf16[128,768]{0,1:T(8,128)(2,1)}, u32[]{:S(2)}, u32[]{:S(2)}) %collective-permute-start.26) | collective-permute-done | bytes 196640 | tf_op jit(solution)/shard_map/ppermute | solution.py:748
  137.5 2.6 collective-permute-start.25
  140.0 2.8 collective-permute-start.23
  143.0 1.9 constant_dynamic-update-slice_fusion.5
  145.0 2.1 collective-permute-start.17
  148.1 10.0 %collective-permute-done.22 = bf16[1,2,128,1024]{3,2,1,0:T(8,128)(2,1)S(1)} collective-permute-done((bf16[1,2,128,1024]{3,2,1,0:T(8,128)(2,1)S(1)}, bf16[1,2,128,1024]{3,2,1,0:T(8,128)(2,1)S(1)}, u32[]{:S(2)}, u32[]{:S(2)}) %collective-permute-start.22) | collective-permute-done | bytes 524320 | tf_op jit(solution)/shard_map/ppermute | solution.py:755
  159.2 5.7 %collective-permute-done.17 = bf16[1,2,128,1024]{3,2,1,0:T(8,128)(2,1)S(1)} collective-permute-done((bf16[1,2,128,1024]{3,2,1,0:T(8,128)(2,1)S(1)}, bf16[1,2,128,1024]{3,2,1,0:T(8,128)(2,1)S(1)}, u32[]{:S(2)}, u32[]{:S(2)}) %collective-permute-start.17) | collective-permute-done | bytes 524320 | tf_op jit(solution)/shard_map/ppermute | solution.py:755
  165.9 21.8 %collective-permute-done.25 = bf16[328,1024]{1,0:T(8,128)(2,1)S(1)} collective-permute-done((bf16[328,1024]{1,0:T(8,128)(2,1)}, bf16[328,1024]{1,0:T(8,128)(2,1)S(1)}, u32[]{:S(2)}, u32[]{:S(2)}) %collective-permute-start.25) | collective-permute-done | bytes 671776 | tf_op jit(solution)/shard_map/ppermute | solution.py:772
  187.7 4.1 fusion.22.grad_ref
  193.7 15.7 %mlp.1 = (bf16[8,2,128,384]{3,2,1,0:T(8,128)(2,1)}, bf16[8,2,128,768]{3,2,1,0:T(8,128)(2,1)}, bf16[5,2,128,1024]{3,2,1,0:T(8,128)(2,1)}, bf16[3,2,128,1024]{3,2,1,0:T(8,128)(2,1)}) custom-call(bf16[8,2,128,1024]{3,2,1,0:T(8,128)(2,1)} %constant_dynamic-update-slice_fusion.low_ref, f32[8,2,128,384]{3,2,1,0:T(8,128)} %fusion.22.grad_ref, ...), custom_call_target="tpu_custom_call" | custom-call | tf_op jit(solution)/shard_map/mlp/pallas_call | solution.py:586
  210.6 3.2 convolution_bitcast_fusion
  215.1 2.2 convolution_convert_fusion.1
  217.8 8.0 %bitcast_convert_fusion = bf16[1024,768]{1,0:T(8,128)(2,1)} fusion(bf16[8,2,128,1024]{3,2,1,0:T(8,128)(2,1)} %constant_dynamic-update-slice_fusion.low_ref, bf16[8,2,128,768]{3,2,1,0:T(8,128)(2,1)} %get-tuple-element.58), kind=kOutput, calls=%fused_computation.1 | convolution fusion | flops 3222011904 | bytes 8912896 | tf_op jit(solution)/shard_map/dot_general | solution.py:372
  225.9 3.9 convert_add_fusion.2
  233.2 3.8 convert_add_fusion
  237.0 2.2 collective-permute-done.32
  242.6 14.6 %collective-permute-done.28 = bf16[2,128,1024]{2,1,0:T(8,128)(2,1)S(1)} collective-permute-done((bf16[2,128,1024]{2,1,0:T(8,128)(2,1)S(1)}, bf16[2,128,1024]{2,1,0:T(8,128)(2,1)S(1)}, u32[]{:S(2)}, u32[]{:S(2)}) %collective-permute-start.28) | collective-permute-done | bytes 524320 | tf_op jit(solution)/shard_map/ppermute | solution.py:760
  260.2 1.9 convert_add_fusion.5
  263.4 9.4 %collective-permute-start.50 = (bf16[328,256]{1,0:T(8,128)(2,1)}, bf16[328,256]{1,0:T(8,128)(2,1)S(1)}, u32[]{:S(2)}, u32[]{:S(2)}) collective-permute-start(bf16[328,256]{1,0:T(8,128)(2,1)} %bitcast.232), channel_id=1, source_target_pairs={{0,0},{1,16},{2,8},{3,24},{8,1},{9,17},{10,9},{11,25},{16,2},{17,1... | collective-permute-start | bytes 503816 | tf_op jit(solution)/shard_map/ppermute | solution.py:780
  272.8 2.3 slice.158
  275.0 7.9 %collective-permute-done.50 = bf16[328,256]{1,0:T(8,128)(2,1)S(1)} collective-permute-done((bf16[328,256]{1,0:T(8,128)(2,1)}, bf16[328,256]{1,0:T(8,128)(2,1)S(1)}, u32[]{:S(2)}, u32[]{:S(2)}) %collective-permute-start.50) | collective-permute-done | bytes 167968 | tf_op jit(solution)/shard_map/ppermute | solution.py:780
  284.8 5.0 %branch_back.1 = (f32[2,128,1024]{2,1,0:T(8,128)}, bf16[2,128,1024]{2,1,0:T(8,128)(2,1)}, bf16[8,2,128,128]{3,2,1,0:T(8,128)(2,1)}, f32[1,1024]{1,0:T(1,128)}) custom-call(s32[10]{0:T(128)} %concatenate.64.place_ref, bf16[1,128,1024]{2,1,0:T(8,128)(2,1)} %bitcast.203, bf16[1,128,1024]{2,1,0:T(8,128)(2,1)} %copy-done.11, bf16[2,128,1024]{2,1,0:T(8,128)(2,1)} %copy-done.6, ...), custom_call_target="tpu_custom_call" | custom-call | tf_op jit(solution)/shard_map/branch_back/pallas_call | solution.py:629
  289.8 4.6 %all-to-all-start.1 = ((bf16[8,2,128,128]{3,2,1,0:T(8,128)(2,1)}), bf16[8,2,128,128]{3,2,1,0:T(8,128)(2,1)S(1)}, u32[]{:S(2)}, u32[]{:S(2)}) async-start(bf16[8,2,128,128]{3,2,1,0:T(8,128)(2,1)} %get-tuple-element.46), calls=%async_computation.1 | async-start | bytes 1048576 | tf_op jit(solution)/shard_map/all_to_all | solution.py:860
  298.2 2.0 convert_add_fusion.3
  300.2 6.7 %collective-permute-done.48 = bf16[128,768]{0,1:T(8,128)(2,1)S(1)} collective-permute-done((bf16[128,768]{0,1:T(8,128)(2,1)S(1)}, bf16[128,768]{0,1:T(8,128)(2,1)S(1)}, u32[]{:S(2)}, u32[]{:S(2)}) %collective-permute-start.48) | collective-permute-done | bytes 196640 | tf_op jit(solution)/shard_map/ppermute | solution.py:748
  309.5 20.6 %attend_back.1 = (bf16[8,2,128,384]{3,2,1,0:T(8,128)(2,1)}, bf16[5,2,128,1024]{3,2,1,0:T(8,128)(2,1)}, bf16[3,2,128,1024]{3,2,1,0:T(8,128)(2,1)}) custom-call(s32[10]{0:T(128)} %concatenate.64.place_ref, bf16[8,2,128,384]{3,2,1,0:T(8,128)(2,1)} %get-tuple-element.34.q_ref.k_ref.v_ref, bf16[8,2,128,384]{3,2,1,0:T(8,128)(2,1)} %get-tuple-element.34.q_ref.k_ref.v_ref, ...), custom_call_target="tpu_custom_call" | custom-call | tf_op jit(solution)/shard_map/attend_back/pallas_call | solution.py:694
  331.0 4.6 %fusion.60 = (bf16[1024,384]{0,1:T(8,128)(2,1)}, f32[1024,384]{0,1:T(8,128)}) fusion(bf16[8,2,128,1024]{3,2,1,0:T(8,128)(2,1)S(1)} %copy-done.35, bf16[8,2,128,384]{3,2,1,0:T(8,128)(2,1)} %get-tuple-element.54), kind=kOutput, calls=%fused_computation.157 | convolution fusion | flops 1611005952 | bytes 8126464 | tf_op jit(solution)/shard_map/dot_general | solution.py:372
  335.6 3.1 copy.57
  344.4 4.7 %collective-permute-done.52 = f32[16,128]{1,0:T(8,128)S(1)} collective-permute-done((f32[16,128]{1,0:T(8,128)S(1)}, f32[16,128]{1,0:T(8,128)S(1)}, u32[]{:S(2)}, u32[]{:S(2)}) %collective-permute-start.52) | collective-permute-done | bytes 8224 | tf_op jit(solution)/shard_map/ppermute | solution.py:749
  349.6 2.3 pad_maximum_fusion.6
  355.3 2.7 convert_add_fusion.1
  358.7 2.1 fusion.19
  360.9 3.3 collective-permute-start.55
  364.1 8.5 %collective-permute-done.43 = bf16[2,2,128,1024]{3,2,1,0:T(8,128)(2,1)} collective-permute-done((bf16[2,2,128,1024]{3,2,1,0:T(8,128)(2,1)}, bf16[2,2,128,1024]{3,2,1,0:T(8,128)(2,1)}, u32[]{:S(2)}, u32[]{:S(2)}) %collective-permute-start.43) | collective-permute-done | bytes 1048608 | tf_op jit(solution)/shard_map/ppermute | solution.py:754
  377.0 1.9 constant_dynamic-update-slice_fusion.16
  379.9 8.6 %collective-permute-done.44 = bf16[1,2,128,1024]{3,2,1,0:T(8,128)(2,1)} collective-permute-done((bf16[1,2,128,1024]{3,2,1,0:T(8,128)(2,1)S(1)}, bf16[1,2,128,1024]{3,2,1,0:T(8,128)(2,1)}, u32[]{:S(2)}, u32[]{:S(2)}) %collective-permute-start.44) | collective-permute-done | bytes 524320 | tf_op jit(solution)/shard_map/ppermute | solution.py:755
  389.0 2.4 collective-permute-start.39
  391.4 2.3 constant_dynamic-update-slice_fusion.15
  393.7 3.0 collective-permute-done.39
  399.8 1.9 constant_dynamic-update-slice_fusion.12
  401.7 6.6 %copy.50 = bf16[1024,2048]{1,0:T(8,128)(2,1)} copy(bf16[1024,2048]{0,1:T(8,128)(2,1)} %bitcast.66) | data formatting | bytes 8388608 | tf_op jit(solution)/shard_map/dot_general | solution.py:372
  408.3 4.4 fusion.4
  412.7 1.9 convert_add_fusion.4
  418.3 15.1 %reduce-scatter.7.cloned.1.call-done = bf16[1,128,256]{2,1,0:T(8,128)(2,1)} async-done(((bf16[4,128,256]{2,1,0:T(8,128)(2,1)}), bf16[1,128,256]{2,1,0:T(8,128)(2,1)}) %reduce-scatter.7.cloned.1.call-update) | async-done | bytes 65552 | tf_op jit(solution)/shard_map/reduce_scatter | solution.py:896
  433.4 2.6 collective-permute-start.47
  439.2 2.5 collective-permute-done.47
  443.6 2.6 fusion.8
  (271 shorter events, 84.9 us)
Async XLA Ops:
  7.2 2.2 collective-permute-start.6
  10.7 46.5 %copy-start.4 = (bf16[2,128,1024]{2,1,0:T(8,128)(2,1)S(1)}, bf16[2,128,1024]{2,1,0:T(8,128)(2,1)}, u32[]{:S(2)}) copy-start(bf16[2,128,1024]{2,1,0:T(8,128)(2,1)} %refs_8_.1) | copy-start | bytes 1572868
  10.7 14.9 %collective-permute-start.7 = (bf16[2,2,128,1024]{3,2,1,0:T(8,128)(2,1)S(1)}, bf16[2,2,128,1024]{3,2,1,0:T(8,128)(2,1)S(1)}, u32[]{:S(2)}, u32[]{:S(2)}) collective-permute-start(bf16[2,2,128,1024]{3,2,1,0:T(8,128)(2,1)S(1)} %pad_maximum_fusion), channel_id=1, source_target_pairs={{0,4},{1,3},{2,6},{3,1},{4,0},{5,7},{6,2},{7,5},{8,12},{9,11},{10,... | collective-permute-start | bytes 3145736 | tf_op jit(solution)/shard_map/ppermute | solution.py:754
  12.3 17.6 %collective-permute-start = (bf16[128,1024]{1,0:T(8,128)(2,1)}, bf16[128,1024]{1,0:T(8,128)(2,1)S(1)}, u32[]{:S(2)}, u32[]{:S(2)}) collective-permute-start(bf16[128,1024]{1,0:T(8,128)(2,1)} %param.11), channel_id=1, source_target_pairs={{0,0},{8,1},{16,2},{24,3},{1,8},{9,9},{17,10},{25,11},{2,16},{10,1... | collective-permute-start | bytes 786440 | tf_op jit(solution)/shard_map/ppermute | solution.py:772
  26.5 12.1 %collective-permute-start.8 = (bf16[1,2,128,1024]{3,2,1,0:T(8,128)(2,1)}, bf16[1,2,128,1024]{3,2,1,0:T(8,128)(2,1)}, u32[]{:S(2)}, u32[]{:S(2)}) collective-permute-start(bf16[1,2,128,1024]{3,2,1,0:T(8,128)(2,1)} %slice.155), channel_id=1, source_target_pairs={{0,2},{1,5},{2,0},{3,7},{4,6},{5,1},{6,4},{7,3},{8,10},{9,13},{10,... | collective-permute-start | bytes 1572872 | tf_op jit(solution)/shard_map/ppermute | solution.py:755
  29.9 7.0 %collective-permute-start.1 = (bf16[1,128,1024]{2,1,0:T(8,128)(2,1)S(1)}, bf16[1,128,1024]{2,1,0:T(8,128)(2,1)S(1)}, u32[]{:S(2)}, u32[]{:S(2)}) collective-permute-start(bf16[1,128,1024]{2,1,0:T(8,128)(2,1)S(1)} %bitcast.200), channel_id=1, source_target_pairs={{0,1},{1,0},{2,3},{3,2},{4,5},{5,4},{6,7},{7,6},{8,9},{9,8},{10,11... | collective-permute-start | bytes 786440 | tf_op jit(solution)/shard_map/ppermute | solution.py:749
  36.2 6.1 %collective-permute-start.11 = (bf16[144,384]{1,0:T(8,128)(2,1)S(1)}, bf16[144,384]{1,0:T(8,128)(2,1)S(1)}, u32[]{:S(2)}, u32[]{:S(2)}) collective-permute-start(bf16[144,384]{1,0:T(8,128)(2,1)S(1)} %get-tuple-element.106), channel_id=1, source_target_pairs={{0,4},{4,0},{1,5},{5,1},{2,6},{6,2},{3,7},{7,3},{8,12},{12,8},{9,1... | collective-permute-start | bytes 331784 | tf_op jit(solution)/shard_map/ppermute | solution.py:748
  36.9 29.2 %collective-permute-start.9 = (bf16[2,2,128,1024]{3,2,1,0:T(8,128)(2,1)S(1)}, bf16[2,2,128,1024]{3,2,1,0:T(8,128)(2,1)}, u32[]{:S(2)}, u32[]{:S(2)}) collective-permute-start(bf16[2,2,128,1024]{3,2,1,0:T(8,128)(2,1)S(1)} %collective-permute-done.7.refs_2_), channel_id=1, source_target_pairs={{0,1},{1,0},{2,3},{3,2},{4,5},{5,4},{6,7},{7,6},{8,9},{9,8},{10,11... | collective-permute-start | bytes 3145736 | tf_op jit(solution)/shard_map/ppermute | solution.py:749
  37.0 10.9 %collective-permute-start.2 = (bf16[2,128,1024]{2,1,0:T(8,128)(2,1)S(1)}, bf16[2,128,1024]{2,1,0:T(8,128)(2,1)S(1)}, u32[]{:S(2)}, u32[]{:S(2)}) collective-permute-start(bf16[2,128,1024]{2,1,0:T(8,128)(2,1)S(1)} %pad_maximum_fusion.7), channel_id=1, source_target_pairs={{0,4},{1,3},{2,6},{3,1},{4,0},{5,7},{6,2},{7,5},{8,12},{9,11},{10,... | collective-permute-start | bytes 1572872 | tf_op jit(solution)/shard_map/ppermute | solution.py:754
  38.6 10.6 %collective-permute-start.10 = (bf16[1,2,128,1024]{3,2,1,0:T(8,128)(2,1)}, bf16[1,2,128,1024]{3,2,1,0:T(8,128)(2,1)S(1)}, u32[]{:S(2)}, u32[]{:S(2)}) collective-permute-start(bf16[1,2,128,1024]{3,2,1,0:T(8,128)(2,1)} %collective-permute-done.8.refs_3_), channel_id=1, source_target_pairs={{0,1},{1,0},{2,3},{3,2},{4,5},{5,4},{6,7},{7,6},{8,9},{9,8},{10,11... | collective-permute-start | bytes 1572872 | tf_op jit(solution)/shard_map/ppermute | solution.py:749
  43.0 10.3 %collective-permute-start.14 = (bf16[2,144,384]{2,1,0:T(8,128)(2,1)}, bf16[2,144,384]{2,1,0:T(8,128)(2,1)S(1)}, u32[]{:S(2)}, u32[]{:S(2)}) collective-permute-start(bf16[2,144,384]{2,1,0:T(8,128)(2,1)} %pad_maximum_fusion.10.refs_6_), channel_id=1, source_target_pairs={{0,24},{8,16},{16,8},{24,0},{1,25},{9,17},{17,9},{25,1},{2,26},{10... | collective-permute-start | bytes 663560 | tf_op jit(solution)/shard_map/ppermute | solution.py:783
  44.4 12.8 %collective-permute-start.12 = (bf16[2,144,384]{2,1,0:T(8,128)(2,1)}, bf16[2,144,384]{2,1,0:T(8,128)(2,1)S(1)}, u32[]{:S(2)}, u32[]{:S(2)}) collective-permute-start(bf16[2,144,384]{2,1,0:T(8,128)(2,1)} %pad_maximum_fusion.10.refs_6_), channel_id=1, source_target_pairs={{0,8},{8,0},{16,24},{24,16},{1,9},{9,1},{17,25},{25,17},{2,10},{10... | collective-permute-start | bytes 663560 | tf_op jit(solution)/shard_map/ppermute | solution.py:783
  47.9 18.1 %collective-permute-start.13 = (bf16[2,144,384]{2,1,0:T(8,128)(2,1)}, bf16[2,144,384]{2,1,0:T(8,128)(2,1)}, u32[]{:S(2)}, u32[]{:S(2)}) collective-permute-start(bf16[2,144,384]{2,1,0:T(8,128)(2,1)} %pad_maximum_fusion.10.refs_6_), channel_id=1, source_target_pairs={{0,16},{8,24},{16,0},{24,8},{1,17},{9,25},{17,1},{25,9},{2,18},{10... | collective-permute-start | bytes 663560 | tf_op jit(solution)/shard_map/ppermute | solution.py:783
  49.1 41.2 %collective-permute-start.3 = (bf16[1,128,1024]{2,1,0:T(8,128)(2,1)}, bf16[1,128,1024]{2,1,0:T(8,128)(2,1)S(1)}, u32[]{:S(2)}, u32[]{:S(2)}) collective-permute-start(bf16[1,128,1024]{2,1,0:T(8,128)(2,1)} %slice.154), channel_id=1, source_target_pairs={{0,2},{1,5},{2,0},{3,7},{4,6},{5,1},{6,4},{7,3},{8,10},{9,13},{10,... | collective-permute-start | bytes 786440 | tf_op jit(solution)/shard_map/ppermute | solution.py:755
  53.3 37.3 %collective-permute-start.4 = (bf16[2,128,1024]{2,1,0:T(8,128)(2,1)S(1)}, bf16[2,128,1024]{2,1,0:T(8,128)(2,1)}, u32[]{:S(2)}, u32[]{:S(2)}) collective-permute-start(bf16[2,128,1024]{2,1,0:T(8,128)(2,1)S(1)} %collective-permute-done.2.refs_2_), channel_id=1, source_target_pairs={{0,1},{1,0},{2,3},{3,2},{4,5},{5,4},{6,7},{7,6},{8,9},{9,8},{10,11... | collective-permute-start | bytes 1572872 | tf_op jit(solution)/shard_map/ppermute | solution.py:749
  57.2 46.4 %collective-permute-start.20 = (bf16[1,2,128,1024]{3,2,1,0:T(8,128)(2,1)S(1)}, bf16[1,2,128,1024]{3,2,1,0:T(8,128)(2,1)S(1)}, u32[]{:S(2)}, u32[]{:S(2)}) collective-permute-start(bf16[1,2,128,1024]{3,2,1,0:T(8,128)(2,1)S(1)} %bitcast.195), channel_id=1, source_target_pairs={{0,1},{1,0},{2,3},{3,2},{4,5},{5,4},{6,7},{7,6},{8,9},{9,8},{10,11... | collective-permute-start | bytes 1572872 | tf_op jit(solution)/shard_map/ppermute | solution.py:749
  86.6 12.1 %all-to-all-start = ((bf16[8,2,128,128]{3,2,1,0:T(8,128)(2,1)}), bf16[8,2,128,128]{3,2,1,0:T(8,128)(2,1)S(1)}, u32[]{:S(2)}, u32[]{:S(2)}) async-start(bf16[8,2,128,128]{3,2,1,0:T(8,128)(2,1)} %get-tuple-element.35), calls=%async_computation | async-start | bytes 1048576 | tf_op jit(solution)/shard_map/all_to_all | solution.py:860
  90.3 103.4 %all-gather.3.cloned.1.call-start = ((), (), s32[]{:S(2)}) async-start(), calls=%async_computation.10 | async-start | bytes 1966080 | tf_op jit(solution)/shard_map/all_gather | solution.py:846
  90.4 1.6 collective-permute-start.5
  103.7 4.2 collective-permute-start.15
  104.8 35.3 %collective-permute-start.21 = (bf16[2,2,128,1024]{3,2,1,0:T(8,128)(2,1)}, bf16[2,2,128,1024]{3,2,1,0:T(8,128)(2,1)S(1)}, u32[]{:S(2)}, u32[]{:S(2)}) collective-permute-start(bf16[2,2,128,1024]{3,2,1,0:T(8,128)(2,1)} %pad_maximum_fusion.2), channel_id=1, source_target_pairs={{0,4},{1,3},{2,6},{3,1},{4,0},{5,7},{6,2},{7,5},{8,12},{9,11},{10,... | collective-permute-start | bytes 3145736 | tf_op jit(solution)/shard_map/ppermute | solution.py:754
  109.7 35.2 %collective-permute-start.16 = (bf16[2,2,128,1024]{3,2,1,0:T(8,128)(2,1)}, bf16[2,2,128,1024]{3,2,1,0:T(8,128)(2,1)S(1)}, u32[]{:S(2)}, u32[]{:S(2)}) collective-permute-start(bf16[2,2,128,1024]{3,2,1,0:T(8,128)(2,1)} %pad_maximum_fusion.1), channel_id=1, source_target_pairs={{0,4},{1,3},{2,6},{3,1},{4,0},{5,7},{6,2},{7,5},{8,12},{9,11},{10,... | collective-permute-start | bytes 3145736 | tf_op jit(solution)/shard_map/ppermute | solution.py:754
  112.3 23.0 %collective-permute-start.26 = (bf16[128,768]{0,1:T(8,128)(2,1)S(1)}, bf16[128,768]{0,1:T(8,128)(2,1)}, u32[]{:S(2)}, u32[]{:S(2)}) collective-permute-start(bf16[128,768]{0,1:T(8,128)(2,1)S(1)} %bitcast.223), channel_id=1, source_target_pairs={{0,4},{4,0},{1,5},{5,1},{2,6},{6,2},{3,7},{7,3},{8,12},{12,8},{9,1... | collective-permute-start | bytes 589832 | tf_op jit(solution)/shard_map/ppermute | solution.py:748
  137.4 126.0 %reduce-scatter.11.cloned.1.call-start = ((), (), s32[]{:S(2)}) async-start(), calls=%async_computation.9 | async-start | bytes 839680 | tf_op jit(solution)/shard_map/reduce_scatter | solution.py:896
  137.5 50.2 %collective-permute-start.25 = (bf16[328,1024]{1,0:T(8,128)(2,1)}, bf16[328,1024]{1,0:T(8,128)(2,1)S(1)}, u32[]{:S(2)}, u32[]{:S(2)}) collective-permute-start(bf16[328,1024]{1,0:T(8,128)(2,1)} %param.13), channel_id=1, source_target_pairs={{0,0},{16,1},{8,2},{24,3},{1,8},{17,9},{9,10},{25,11},{2,16},{18,1... | collective-permute-start | bytes 2015240 | tf_op jit(solution)/shard_map/ppermute | solution.py:772
  140.0 25.7 %collective-permute-start.23 = (bf16[2,2,128,1024]{3,2,1,0:T(8,128)(2,1)S(1)}, bf16[2,2,128,1024]{3,2,1,0:T(8,128)(2,1)S(1)}, u32[]{:S(2)}, u32[]{:S(2)}) collective-permute-start(bf16[2,2,128,1024]{3,2,1,0:T(8,128)(2,1)S(1)} %collective-permute-done.21), channel_id=1, source_target_pairs={{0,1},{1,0},{2,3},{3,2},{4,5},{5,4},{6,7},{7,6},{8,9},{9,8},{10,11... | collective-permute-start | bytes 3145736 | tf_op jit(solution)/shard_map/ppermute | solution.py:749
  142.9 15.2 %collective-permute-start.22 = (bf16[1,2,128,1024]{3,2,1,0:T(8,128)(2,1)S(1)}, bf16[1,2,128,1024]{3,2,1,0:T(8,128)(2,1)S(1)}, u32[]{:S(2)}, u32[]{:S(2)}) collective-permute-start(bf16[1,2,128,1024]{3,2,1,0:T(8,128)(2,1)S(1)} %slice.157), channel_id=1, source_target_pairs={{0,2},{1,5},{2,0},{3,7},{4,6},{5,1},{6,4},{7,3},{8,10},{9,13},{10,... | collective-permute-start | bytes 1572872 | tf_op jit(solution)/shard_map/ppermute | solution.py:755
  145.0 19.9 %collective-permute-start.17 = (bf16[1,2,128,1024]{3,2,1,0:T(8,128)(2,1)S(1)}, bf16[1,2,128,1024]{3,2,1,0:T(8,128)(2,1)S(1)}, u32[]{:S(2)}, u32[]{:S(2)}) collective-permute-start(bf16[1,2,128,1024]{3,2,1,0:T(8,128)(2,1)S(1)} %slice.156), channel_id=1, source_target_pairs={{0,2},{1,5},{2,0},{3,7},{4,6},{5,1},{6,4},{7,3},{8,10},{9,13},{10,... | collective-permute-start | bytes 1572872 | tf_op jit(solution)/shard_map/ppermute | solution.py:755
  148.0 43.7 %collective-permute-start.18 = (bf16[2,2,128,1024]{3,2,1,0:T(8,128)(2,1)S(1)}, bf16[2,2,128,1024]{3,2,1,0:T(8,128)(2,1)S(1)}, u32[]{:S(2)}, u32[]{:S(2)}) collective-permute-start(bf16[2,2,128,1024]{3,2,1,0:T(8,128)(2,1)S(1)} %collective-permute-done.16), channel_id=1, source_target_pairs={{0,1},{1,0},{2,3},{3,2},{4,5},{5,4},{6,7},{7,6},{8,9},{9,8},{10,11... | collective-permute-start | bytes 3145736 | tf_op jit(solution)/shard_map/ppermute | solution.py:749
  158.1 7.7 %collective-permute-start.24 = (bf16[1,2,128,1024]{3,2,1,0:T(8,128)(2,1)S(1)}, bf16[1,2,128,1024]{3,2,1,0:T(8,128)(2,1)S(1)}, u32[]{:S(2)}, u32[]{:S(2)}) collective-permute-start(bf16[1,2,128,1024]{3,2,1,0:T(8,128)(2,1)S(1)} %collective-permute-done.22), channel_id=1, source_target_pairs={{0,1},{1,0},{2,3},{3,2},{4,5},{5,4},{6,7},{7,6},{8,9},{9,8},{10,11... | collective-permute-start | bytes 1572872 | tf_op jit(solution)/shard_map/ppermute | solution.py:749
  164.9 27.9 %collective-permute-start.19 = (bf16[1,2,128,1024]{3,2,1,0:T(8,128)(2,1)S(1)}, bf16[1,2,128,1024]{3,2,1,0:T(8,128)(2,1)S(1)}, u32[]{:S(2)}, u32[]{:S(2)}) collective-permute-start(bf16[1,2,128,1024]{3,2,1,0:T(8,128)(2,1)S(1)} %collective-permute-done.17), channel_id=1, source_target_pairs={{0,1},{1,0},{2,3},{3,2},{4,5},{5,4},{6,7},{7,6},{8,9},{9,8},{10,11... | collective-permute-start | bytes 1572872 | tf_op jit(solution)/shard_map/ppermute | solution.py:749
  209.4 16.4 %collective-permute-start.31 = (bf16[3,2,128,1024]{3,2,1,0:T(8,128)(2,1)}, bf16[3,2,128,1024]{3,2,1,0:T(8,128)(2,1)S(1)}, u32[]{:S(2)}, u32[]{:S(2)}) collective-permute-start(bf16[3,2,128,1024]{3,2,1,0:T(8,128)(2,1)} %get-tuple-element.44), channel_id=1, source_target_pairs={{0,1},{1,0},{2,3},{3,2},{4,5},{5,4},{6,7},{7,6},{8,9},{9,8},{10,11... | collective-permute-start | bytes 4718600 | tf_op jit(solution)/shard_map/ppermute | solution.py:749
  214.8 79.9 %reduce-scatter.9.cloned.1.call-start = ((), (), s32[]{:S(2)}) async-start(), calls=%async_computation.8 | async-start | bytes 1966080 | tf_op jit(solution)/shard_map/reduce_scatter | solution.py:896
  217.3 15.9 %collective-permute-start.27 = (bf16[3,2,128,1024]{3,2,1,0:T(8,128)(2,1)}, bf16[3,2,128,1024]{3,2,1,0:T(8,128)(2,1)}, u32[]{:S(2)}, u32[]{:S(2)}) collective-permute-start(bf16[3,2,128,1024]{3,2,1,0:T(8,128)(2,1)} %bitcast.35), channel_id=1, source_target_pairs={{0,1},{1,0},{2,3},{3,2},{4,5},{5,4},{6,7},{7,6},{8,9},{9,8},{10,11... | collective-permute-start | bytes 4718600 | tf_op jit(solution)/shard_map/ppermute | solution.py:749
  229.9 9.2 %collective-permute-start.32 = (bf16[2,128,1024]{2,1,0:T(8,128)(2,1)S(1)}, bf16[2,128,1024]{2,1,0:T(8,128)(2,1)S(1)}, u32[]{:S(2)}, u32[]{:S(2)}) collective-permute-start(bf16[2,128,1024]{2,1,0:T(8,128)(2,1)S(1)} %get-tuple-element.86), channel_id=1, source_target_pairs={{0,2},{1,5},{2,0},{3,7},{4,6},{5,1},{6,4},{7,3},{8,10},{9,13},{10,... | collective-permute-start | bytes 1572872 | tf_op jit(solution)/shard_map/ppermute | solution.py:760
  240.7 19.6 %collective-permute-start.33 = (bf16[2,2,128,1024]{3,2,1,0:T(8,128)(2,1)S(1)}, bf16[2,2,128,1024]{3,2,1,0:T(8,128)(2,1)}, u32[]{:S(2)}, u32[]{:S(2)}) collective-permute-start(bf16[2,2,128,1024]{3,2,1,0:T(8,128)(2,1)S(1)} %pad_maximum_fusion.4), channel_id=1, source_target_pairs={{0,4},{1,3},{2,6},{3,1},{4,0},{5,7},{6,2},{7,5},{8,12},{9,11},{10,... | collective-permute-start | bytes 3145736 | tf_op jit(solution)/shard_map/ppermute | solution.py:762
  242.3 14.9 %collective-permute-start.28 = (bf16[2,128,1024]{2,1,0:T(8,128)(2,1)S(1)}, bf16[2,128,1024]{2,1,0:T(8,128)(2,1)S(1)}, u32[]{:S(2)}, u32[]{:S(2)}) collective-permute-start(bf16[2,128,1024]{2,1,0:T(8,128)(2,1)S(1)} %get-tuple-element.88), channel_id=1, source_target_pairs={{0,2},{1,5},{2,0},{3,7},{4,6},{5,1},{6,4},{7,3},{8,10},{9,13},{10,... | collective-permute-start | bytes 1572872 | tf_op jit(solution)/shard_map/ppermute | solution.py:760
  259.7 38.5 %collective-permute-start.29 = (bf16[2,2,128,1024]{3,2,1,0:T(8,128)(2,1)}, bf16[2,2,128,1024]{3,2,1,0:T(8,128)(2,1)}, u32[]{:S(2)}, u32[]{:S(2)}) collective-permute-start(bf16[2,2,128,1024]{3,2,1,0:T(8,128)(2,1)} %pad_maximum_fusion.3), channel_id=1, source_target_pairs={{0,4},{1,3},{2,6},{3,1},{4,0},{5,7},{6,2},{7,5},{8,12},{9,11},{10,... | collective-permute-start | bytes 3145736 | tf_op jit(solution)/shard_map/ppermute | solution.py:762
  263.0 20.6 %collective-permute-start.34 = (bf16[2,128,1024]{2,1,0:T(8,128)(2,1)}, bf16[2,128,1024]{2,1,0:T(8,128)(2,1)S(1)}, u32[]{:S(2)}, u32[]{:S(2)}) collective-permute-start(bf16[2,128,1024]{2,1,0:T(8,128)(2,1)} %fusion.31), channel_id=1, source_target_pairs={{0,1},{1,0},{2,3},{3,2},{4,5},{5,4},{6,7},{7,6},{8,9},{9,8},{10,11... | collective-permute-start | bytes 1572872 | tf_op jit(solution)/shard_map/ppermute | solution.py:749
  263.4 19.6 %collective-permute-start.50 = (bf16[328,256]{1,0:T(8,128)(2,1)}, bf16[328,256]{1,0:T(8,128)(2,1)S(1)}, u32[]{:S(2)}, u32[]{:S(2)}) collective-permute-start(bf16[328,256]{1,0:T(8,128)(2,1)} %bitcast.232), channel_id=1, source_target_pairs={{0,0},{1,16},{2,8},{3,24},{8,1},{9,17},{10,9},{11,25},{16,2},{17,1... | collective-permute-start | bytes 503816 | tf_op jit(solution)/shard_map/ppermute | solution.py:780
  289.8 18.9 %all-to-all-start.1 = ((bf16[8,2,128,128]{3,2,1,0:T(8,128)(2,1)}), bf16[8,2,128,128]{3,2,1,0:T(8,128)(2,1)S(1)}, u32[]{:S(2)}, u32[]{:S(2)}) async-start(bf16[8,2,128,128]{3,2,1,0:T(8,128)(2,1)} %get-tuple-element.46), calls=%async_computation.1 | async-start | bytes 1048576 | tf_op jit(solution)/shard_map/all_to_all | solution.py:860
  294.4 84.5 %reduce-scatter.5.cloned.1.call-start = ((), (), s32[]{:S(2)}) async-start(), calls=%async_computation.6 | async-start | bytes 983040 | tf_op jit(solution)/shard_map/reduce_scatter | solution.py:896
  295.9 11.0 %collective-permute-start.48 = (bf16[128,768]{0,1:T(8,128)(2,1)S(1)}, bf16[128,768]{0,1:T(8,128)(2,1)S(1)}, u32[]{:S(2)}, u32[]{:S(2)}) collective-permute-start(bf16[128,768]{0,1:T(8,128)(2,1)S(1)} %bitcast.222), channel_id=1, source_target_pairs={{0,4},{4,0},{1,5},{5,1},{2,6},{6,2},{3,7},{7,3},{8,12},{12,8},{9,1... | collective-permute-start | bytes 589832 | tf_op jit(solution)/shard_map/ppermute | solution.py:748
  330.1 25.2 %collective-permute-start.35 = (bf16[3,2,128,1024]{3,2,1,0:T(8,128)(2,1)}, bf16[3,2,128,1024]{3,2,1,0:T(8,128)(2,1)}, u32[]{:S(2)}, u32[]{:S(2)}) collective-permute-start(bf16[3,2,128,1024]{3,2,1,0:T(8,128)(2,1)} %get-tuple-element.51), channel_id=1, source_target_pairs={{0,1},{1,0},{2,3},{3,2},{4,5},{5,4},{6,7},{7,6},{8,9},{9,8},{10,11... | collective-permute-start | bytes 4718600 | tf_op jit(solution)/shard_map/ppermute | solution.py:749
  338.7 10.9 %collective-permute-start.42 = (bf16[1,2,128,1024]{3,2,1,0:T(8,128)(2,1)}, bf16[1,2,128,1024]{3,2,1,0:T(8,128)(2,1)}, u32[]{:S(2)}, u32[]{:S(2)}) collective-permute-start(bf16[1,2,128,1024]{3,2,1,0:T(8,128)(2,1)} %bitcast.205), channel_id=1, source_target_pairs={{0,1},{1,0},{2,3},{3,2},{4,5},{5,4},{6,7},{7,6},{8,9},{9,8},{10,11... | collective-permute-start | bytes 1572872 | tf_op jit(solution)/shard_map/ppermute | solution.py:749
  340.9 1.9 collective-permute-start.51
  342.1 11.2 %collective-permute-start.49 = (bf16[2,128,328]{1,2,0:T(8,128)(2,1)S(1)}, bf16[2,128,328]{1,2,0:T(8,128)(2,1)S(1)}, u32[]{:S(2)}, u32[]{:S(2)}) collective-permute-start(bf16[2,128,328]{1,2,0:T(8,128)(2,1)S(1)} %get-tuple-element.99), channel_id=1, source_target_pairs={{0,2},{1,3},{2,0},{3,1},{4,6},{5,7},{6,4},{7,5},{8,10},{9,11},{10,... | collective-permute-start | bytes 503816 | tf_op jit(solution)/shard_map/ppermute | solution.py:749
  342.7 6.3 %collective-permute-start.52 = (f32[16,128]{1,0:T(8,128)S(1)}, f32[16,128]{1,0:T(8,128)S(1)}, u32[]{:S(2)}, u32[]{:S(2)}) collective-permute-start(f32[16,128]{1,0:T(8,128)S(1)} %add.244), channel_id=1, source_target_pairs={{0,2},{1,3},{2,0},{3,1},{4,6},{5,7},{6,4},{7,5},{8,10},{9,11},{10,... | collective-permute-start | bytes 24584 | tf_op jit(solution)/shard_map/ppermute | solution.py:749
  344.3 14.5 %collective-permute-start.30 = (bf16[2,128,1024]{2,1,0:T(8,128)(2,1)S(1)}, bf16[2,128,1024]{2,1,0:T(8,128)(2,1)}, u32[]{:S(2)}, u32[]{:S(2)}) collective-permute-start(bf16[2,128,1024]{2,1,0:T(8,128)(2,1)S(1)} %fusion.29), channel_id=1, source_target_pairs={{0,1},{1,0},{2,3},{3,2},{4,5},{5,4},{6,7},{7,6},{8,9},{9,8},{10,11... | collective-permute-start | bytes 1572872 | tf_op jit(solution)/shard_map/ppermute | solution.py:749
  349.0 5.5 %collective-permute-start.53 = (f32[16,128]{1,0:T(8,128)S(1)}, f32[16,128]{1,0:T(8,128)S(1)}, u32[]{:S(2)}, u32[]{:S(2)}) collective-permute-start(f32[16,128]{1,0:T(8,128)S(1)} %add.245), channel_id=1, source_target_pairs={{0,4},{4,0},{1,5},{5,1},{2,6},{6,2},{3,7},{7,3},{8,12},{12,8},{9,1... | collective-permute-start | bytes 24584 | tf_op jit(solution)/shard_map/ppermute | solution.py:748
  351.9 20.7 %collective-permute-start.43 = (bf16[2,2,128,1024]{3,2,1,0:T(8,128)(2,1)}, bf16[2,2,128,1024]{3,2,1,0:T(8,128)(2,1)}, u32[]{:S(2)}, u32[]{:S(2)}) collective-permute-start(bf16[2,2,128,1024]{3,2,1,0:T(8,128)(2,1)} %pad_maximum_fusion.6), channel_id=1, source_target_pairs={{0,4},{1,3},{2,6},{3,1},{4,0},{5,7},{6,2},{7,5},{8,12},{9,11},{10,... | collective-permute-start | bytes 3145736 | tf_op jit(solution)/shard_map/ppermute | solution.py:754
  354.3 79.1 %reduce-scatter.7.cloned.1.call-start = ((), (), s32[]{:S(2)}) async-start(), calls=%async_computation.7 | async-start | bytes 327680 | tf_op jit(solution)/shard_map/reduce_scatter | solution.py:896
  354.6 6.3 %collective-permute-start.54 = (f32[16,128]{1,0:T(8,128)S(1)}, f32[16,128]{1,0:T(8,128)S(1)}, u32[]{:S(2)}, u32[]{:S(2)}) collective-permute-start(f32[16,128]{1,0:T(8,128)S(1)} %add.246), channel_id=1, source_target_pairs={{0,8},{8,0},{16,24},{24,16},{1,9},{9,1},{17,25},{25,17},{2,10},{10... | collective-permute-start | bytes 24584 | tf_op jit(solution)/shard_map/ppermute | solution.py:783
  358.1 16.9 %collective-permute-start.36 = (bf16[2,128,1024]{2,1,0:T(8,128)(2,1)S(1)}, bf16[2,128,1024]{2,1,0:T(8,128)(2,1)S(1)}, u32[]{:S(2)}, u32[]{:S(2)}) collective-permute-start(bf16[2,128,1024]{2,1,0:T(8,128)(2,1)S(1)} %get-tuple-element.84), channel_id=1, source_target_pairs={{0,2},{1,5},{2,0},{3,7},{4,6},{5,1},{6,4},{7,3},{8,10},{9,13},{10,... | collective-permute-start | bytes 1572872 | tf_op jit(solution)/shard_map/ppermute | solution.py:760
  360.9 12.6 %collective-permute-start.55 = (f32[16,128]{1,0:T(8,128)S(1)}, f32[16,128]{1,0:T(8,128)S(1)}, u32[]{:S(2)}, u32[]{:S(2)}) collective-permute-start(f32[16,128]{1,0:T(8,128)S(1)} %add.247), channel_id=1, source_target_pairs={{0,16},{8,24},{16,0},{24,8},{1,17},{9,25},{17,1},{25,9},{2,18},{10... | collective-permute-start | bytes 24584 | tf_op jit(solution)/shard_map/ppermute | solution.py:783
  372.6 26.1 %collective-permute-start.45 = (bf16[2,2,128,1024]{3,2,1,0:T(8,128)(2,1)}, bf16[2,2,128,1024]{3,2,1,0:T(8,128)(2,1)S(1)}, u32[]{:S(2)}, u32[]{:S(2)}) collective-permute-start(bf16[2,2,128,1024]{3,2,1,0:T(8,128)(2,1)} %collective-permute-done.43), channel_id=1, source_target_pairs={{0,1},{1,0},{2,3},{3,2},{4,5},{5,4},{6,7},{7,6},{8,9},{9,8},{10,11... | collective-permute-start | bytes 3145736 | tf_op jit(solution)/shard_map/ppermute | solution.py:749
  374.5 13.9 %collective-permute-start.44 = (bf16[1,2,128,1024]{3,2,1,0:T(8,128)(2,1)S(1)}, bf16[1,2,128,1024]{3,2,1,0:T(8,128)(2,1)}, u32[]{:S(2)}, u32[]{:S(2)}) collective-permute-start(bf16[1,2,128,1024]{3,2,1,0:T(8,128)(2,1)S(1)} %slice.175), channel_id=1, source_target_pairs={{0,2},{1,5},{2,0},{3,7},{4,6},{5,1},{6,4},{7,3},{8,10},{9,13},{10,... | collective-permute-start | bytes 1572872 | tf_op jit(solution)/shard_map/ppermute | solution.py:755
  375.3 37.4 %collective-permute-start.37 = (bf16[2,2,128,1024]{3,2,1,0:T(8,128)(2,1)S(1)}, bf16[2,2,128,1024]{3,2,1,0:T(8,128)(2,1)}, u32[]{:S(2)}, u32[]{:S(2)}) collective-permute-start(bf16[2,2,128,1024]{3,2,1,0:T(8,128)(2,1)S(1)} %pad_maximum_fusion.5), channel_id=1, source_target_pairs={{0,4},{1,3},{2,6},{3,1},{4,0},{5,7},{6,2},{7,5},{8,12},{9,11},{10,... | collective-permute-start | bytes 3145736 | tf_op jit(solution)/shard_map/ppermute | solution.py:762
  388.4 11.3 %collective-permute-start.46 = (bf16[1,2,128,1024]{3,2,1,0:T(8,128)(2,1)}, bf16[1,2,128,1024]{3,2,1,0:T(8,128)(2,1)}, u32[]{:S(2)}, u32[]{:S(2)}) collective-permute-start(bf16[1,2,128,1024]{3,2,1,0:T(8,128)(2,1)} %collective-permute-done.44), channel_id=1, source_target_pairs={{0,1},{1,0},{2,3},{3,2},{4,5},{5,4},{6,7},{7,6},{8,9},{9,8},{10,11... | collective-permute-start | bytes 1572872 | tf_op jit(solution)/shard_map/ppermute | solution.py:749
  389.0 7.7 %collective-permute-start.39 = (bf16[128,384]{1,0:T(8,128)(2,1)S(1)}, bf16[128,384]{1,0:T(8,128)(2,1)S(1)}, u32[]{:S(2)}, u32[]{:S(2)}) collective-permute-start(bf16[128,384]{1,0:T(8,128)(2,1)S(1)} %bitcast.226), channel_id=1, source_target_pairs={{0,4},{4,0},{1,5},{5,1},{2,6},{6,2},{3,7},{7,3},{8,12},{12,8},{9,1... | collective-permute-start | bytes 294920 | tf_op jit(solution)/shard_map/ppermute | solution.py:748
  415.5 27.6 %collective-permute-start.38 = (bf16[2,128,1024]{2,1,0:T(8,128)(2,1)}, bf16[2,128,1024]{2,1,0:T(8,128)(2,1)S(1)}, u32[]{:S(2)}, u32[]{:S(2)}) collective-permute-start(bf16[2,128,1024]{2,1,0:T(8,128)(2,1)} %fusion.33), channel_id=1, source_target_pairs={{0,1},{1,0},{2,3},{3,2},{4,5},{5,4},{6,7},{7,6},{8,9},{9,8},{10,11... | collective-permute-start | bytes 1572872 | tf_op jit(solution)/shard_map/ppermute | solution.py:749
  416.2 19.8 %collective-permute-start.40 = (bf16[2,128,128]{1,2,0:T(8,128)(2,1)S(1)}, bf16[2,128,128]{1,2,0:T(8,128)(2,1)S(1)}, u32[]{:S(2)}, u32[]{:S(2)}) collective-permute-start(bf16[2,128,128]{1,2,0:T(8,128)(2,1)S(1)} %get-tuple-element.102), channel_id=1, source_target_pairs={{0,1},{1,0},{2,3},{3,2},{4,5},{5,4},{6,7},{7,6},{8,9},{9,8},{10,11... | collective-permute-start | bytes 196616 | tf_op jit(solution)/shard_map/ppermute | solution.py:749
  416.7 19.3 %collective-permute-start.41 = (bf16[2,128,128]{1,2,0:T(8,128)(2,1)S(1)}, bf16[2,128,128]{1,2,0:T(8,128)(2,1)S(1)}, u32[]{:S(2)}, u32[]{:S(2)}) collective-permute-start(bf16[2,128,128]{1,2,0:T(8,128)(2,1)S(1)} %get-tuple-element.101), channel_id=1, source_target_pairs={{0,2},{1,3},{2,0},{3,1},{4,6},{5,7},{6,4},{7,5},{8,10},{9,11},{10,... | collective-permute-start | bytes 196616 | tf_op jit(solution)/shard_map/ppermute | solution.py:749
  433.4 8.3 %collective-permute-start.47 = (bf16[128,256]{1,0:T(8,128)(2,1)}, bf16[128,256]{1,0:T(8,128)(2,1)}, u32[]{:S(2)}, u32[]{:S(2)}) collective-permute-start(bf16[128,256]{1,0:T(8,128)(2,1)} %bitcast.233), channel_id=1, source_target_pairs={{0,0},{1,8},{2,16},{3,24},{8,1},{9,9},{10,17},{11,25},{16,2},{17,1... | collective-permute-start | bytes 196616 | tf_op jit(solution)/shard_map/ppermute | solution.py:780
  (38 other events, 451.0 us)
Sparse Core Ops, SparseCore 0:
  137.5 44.9 all-gather.2
  214.9 29.3 reduce-scatter.10
  246.7 35.4 reduce-scatter.8
  354.4 23.3 reduce-scatter.4
  412.8 20.5 reduce-scatter.6

commit v3 on v2

--- a/solution.py
+++ b/solution.py
@@ -1,3 +1,4 @@
+import functools
 import math
 
 import jax
@@ -475,8 +476,8 @@
     )(place, *pieces, *weights, cosine, sine)
 
 
-def attend_kernel(place_ref, q_ref, k_ref, v_ref, att_ref, low_ref, log_ref, home_ref):
-    seq, step = pl.program_id(0), pl.program_id(1)
+def attend_kernel(place_ref, q_ref, k_ref, v_ref, att_ref, log_ref, home_ref):
+    step = pl.program_id(0)
     queries, keys, values = flat(q_ref[...]), flat(k_ref[...]), flat(v_ref[...])
     attended = jnp.zeros(queries.shape, F32)
     logs = jnp.zeros(queries.shape, F32)
@@ -490,30 +491,28 @@
         logs = jnp.where(mask, peak + jnp.log(total), logs)
     att_ref[...] = attended.reshape(att_ref.shape)
     log_ref[...] = logs.reshape(log_ref.shape)
-    low = attended.astype(BF16).reshape(low_ref.shape)
-    low_ref[...] = low
+    low = attended.astype(BF16).reshape(att_ref.shape)
     for inner in range(2):
-        home_ref[place_ref[2 * step + inner], seq] = low[inner, 0]
-
-
-def attend(place, qkv):
-    _, seqs, block, own = qkv.shape
+        home_ref[place_ref[2 * step + inner], 0] = low[inner, 0]
+
+
+def attend(place, qkv, seq):
+    _, _, block, own = qkv.shape
     part = own // 3
-    rows = pl.BlockSpec((2, 1, block, part), lambda s, i: (i, s, 0, 0))
-    shape = (8, seqs, block, part)
+    rows = pl.BlockSpec((2, 1, block, part), lambda i: (i, 0, 0, 0))
+    shape = (8, 1, block, part)
     return pl.pallas_call(
         attend_kernel,
-        grid=(seqs, 4),
+        grid=(4,),
         in_specs=[
             SCALARS,
-            rows,
-            pl.BlockSpec((8, 1, block, part), lambda s, i: (0, s, 0, 1)),
-            pl.BlockSpec((8, 1, block, part), lambda s, i: (0, s, 0, 2)),
+            pl.BlockSpec((2, 1, block, part), lambda i: (i, seq, 0, 0)),
+            pl.BlockSpec((8, 1, block, part), lambda i: (0, seq, 0, 1)),
+            pl.BlockSpec((8, 1, block, part), lambda i: (0, seq, 0, 2)),
         ],
-        out_specs=(rows, rows, rows, pl.BlockSpec(shape, lambda s, i: (0, 0, 0, 0))),
+        out_specs=(rows, rows, pl.BlockSpec(shape, lambda i: (0, 0, 0, 0))),
         out_shape=(
             jax.ShapeDtypeStruct(shape, F32),
-            jax.ShapeDtypeStruct(shape, BF16),
             jax.ShapeDtypeStruct(shape, F32),
             jax.ShapeDtypeStruct(shape, BF16),
         ),
@@ -550,8 +549,19 @@
     )(place, *args)
 
 
-def mlp_kernel(low_ref, grad_ref, w_ref, mixed_ref, lifted_ref, keep_ref, send_ref):
+PIECES = (0, 1, 2, 4, 5, 7, 8)
+
+
+def mlp_kernel(*refs):
+    pieces = refs[:6]
+    grad_ref, w_ref, low_ref, mixed_ref, lifted_ref, keep_ref, send_ref = refs[6:]
     step = pl.program_id(0)
+    for at, piece in enumerate(pieces):
+
+        @pl.when((step >= PIECES[at]) & (step < PIECES[at + 1]))
+        def _(piece=piece):
+            low_ref[...] = piece[...]
+
     hidden = w_ref.shape[1] // 2
     lifted = dot(flat(low_ref[...]), w_ref[...])
     first, second = lifted[:, :hidden], lifted[:, hidden:]
@@ -576,24 +586,27 @@
         send_ref[...] = partial
 
 
-def mlp(low, grad_mixed, w):
-    _, seqs, block, width = low.shape
+def mlp(pieces, grad_mixed, w):
+    seqs, block, width = pieces[0].shape[1:]
     hidden = w.shape[1] // 2
 
     def rows(last):
         return pl.BlockSpec((1, seqs, block, last), lambda i: (i, 0, 0, 0))
+
+    def within(start, count):
+        return pl.BlockSpec(
+            (1, seqs, block, width),
+            lambda i: (jnp.clip(i - start, 0, count - 1), 0, 0, 0),
+        )
 
     return pl.pallas_call(
         mlp_kernel,
         grid=(8,),
-        in_specs=[rows(width), rows(hidden), whole(w)],
-        out_specs=(
-            rows(hidden),
-            rows(2 * hidden),
-            pl.BlockSpec((1, seqs, block, width), lambda i: (jnp.minimum(i, 4), 0, 0, 0)),
-            pl.BlockSpec((1, seqs, block, width), lambda i: (jnp.maximum(i - 5, 0), 0, 0, 0)),
-        ),
+        in_specs=[within(at, piece.shape[0]) for at, piece in zip(PIECES, pieces)]
+        + [rows(hidden), whole(w)],
+        out_specs=(rows(width), rows(hidden), rows(2 * hidden), within(0, 5), within(5, 3)),
         out_shape=(
+            jax.ShapeDtypeStruct((8, seqs, block, width), BF16),
             jax.ShapeDtypeStruct((8, seqs, block, hidden), BF16),
             jax.ShapeDtypeStruct((8, seqs, block, 2 * hidden), BF16),
             jax.ShapeDtypeStruct((5, seqs, block, width), BF16),
@@ -601,7 +614,31 @@
         ),
         compiler_params=params(),
         name="mlp",
-    )(low, grad_mixed, w)
+    )(*pieces, grad_mixed, w)
+
+
+def out_grad_kernel(place_ref, rows_ref, grad_ref, keep_ref, send_ref):
+    grads = flat(grad_ref[...])
+    for index in range(8):
+        part = dot(flat(rows_ref[place_ref[index]]), grads, ((0,), (0,))).astype(BF16)
+        if index < 5:
+            keep_ref[index] = part
+        else:
+            send_ref[index - 5] = part
+
+
+def out_grad(place, rows, grads):
+    part, width = rows.shape[-1], grads.shape[-1]
+    return pl.pallas_call(
+        out_grad_kernel,
+        in_specs=[SCALARS, whole(rows), whole(grads)],
+        out_shape=(
+            jax.ShapeDtypeStruct((5, part, width), BF16),
+            jax.ShapeDtypeStruct((3, part, width), BF16),
+        ),
+        compiler_params=params(),
+        name="out_grad",
+    )(place, rows, grads)
 
 
 def branch_back_kernel(place_ref, *refs):
@@ -642,9 +679,13 @@
 
 def attend_back_kernel(
     place_ref, q_ref, k_ref, v_ref, grad_ref, att_ref, log_ref, cosq_ref, sinq_ref, cos_ref,
-    sin_ref, w_ref, proj_ref, keep_ref, send_ref, sum_k, sum_v,
+    sin_ref, w_ref, low_ref, *refs, seq, last,
 ):
-    seq, step = pl.program_id(0), pl.program_id(1)
+    if last:
+        before_ref, keep_ref, send_ref, grad_w_ref, gain_ref, proj_ref, sum_k, sum_v = refs
+    else:
+        keep_ref, send_ref, before_ref, proj_ref, sum_k, sum_v = refs
+    step = pl.program_id(0)
     block, part = q_ref.shape[2], q_ref.shape[3]
 
     @pl.when(step == 0)
@@ -669,55 +710,74 @@
         sum_v[...] += dot(weights.astype(BF16), own_g)
         grad_queries = jnp.where(mask, dot(grad_scores, keys, ((0,), (0,))), grad_queries)
     grad_queries = lane_rotate(grad_queries * HD**-0.5, cosq_ref[...], -sinq_ref[...])
-    proj_ref[pl.ds(2 * step, 2), 0, :, :part] = grad_queries.astype(BF16).reshape(2, block, part)
+    rows = pl.multiple_of(step * 2 * block, 2 * block)
+    proj_ref[pl.ds(rows, 2 * block), :part] = grad_queries.astype(BF16)
 
     @pl.when(step == 3)
     def _():
-        shape = (8, block, part)
         grad_keys = lane_rotate(sum_k[...], cos_ref[...], -sin_ref[...])
-        proj_ref[:, 0, :, part : 2 * part] = grad_keys.astype(BF16).reshape(shape)
-        proj_ref[:, 0, :, 2 * part :] = sum_v[...].astype(BF16).reshape(shape)
-        partial = dot(flat(proj_ref[:, 0]), w_ref[...], ((1,), (1,))).astype(BF16)
+        proj_ref[:, part : 2 * part] = grad_keys.astype(BF16)
+        proj_ref[:, 2 * part :] = sum_v[...].astype(BF16)
+        partial = dot(proj_ref[...], w_ref[...], ((1,), (1,))).astype(BF16)
         keep_ref[:, 0] = partial[: 5 * block].reshape(5, block, -1)
         send_ref[:, 0] = partial[5 * block :].reshape(3, block, -1)
-
-
-def attend_back(place, qkv, grads, attended, logs, cosine, sine, w):
-    _, seqs, block, own = qkv.shape
+        grad_w = dot(proj_ref[...], flat(low_ref[...]), ((0,), (0,)))
+        if last:
+            grad_w = (grad_w + before_ref[...]).T
+            grad_w_ref[...] = grad_w.astype(BF16)
+            along_w = jnp.sum(grad_w * w_ref[...].astype(F32), axis=1, keepdims=True)
+            gain_ref[...] = jnp.broadcast_to(along_w, (w_ref.shape[0], 128)).T[:8]
+        else:
+            before_ref[...] = grad_w
+
+
+def attend_back(place, qkv, grads, attended, logs, cosine, sine, w, low, seq, before=None):
+    _, _, block, own = qkv.shape
     part, width = own // 3, w.shape[0]
-    rows = pl.BlockSpec((2, 1, block, part), lambda s, i: (i, s, 0, 0))
-    angles = pl.BlockSpec((2 * block, part), lambda s, i: (i, 0))
-
-    def by_seq(lead, last):
-        return pl.BlockSpec((lead, 1, block, last), lambda s, i: (0, s, 0, 0))
-
+    last = before is not None
+    rows = pl.BlockSpec((2, 1, block, part), lambda i: (i, 0, 0, 0))
+    angles = pl.BlockSpec((2 * block, part), lambda i: (i, 0))
+
+    def full(*shape):
+        return pl.BlockSpec(shape, lambda i: (0,) * len(shape))
+
+    args = [place, qkv, qkv, qkv, grads, attended, logs, cosine, sine, cosine, sine, w, low]
+    in_specs = [
+        SCALARS,
+        pl.BlockSpec((2, 1, block, part), lambda i: (i, seq, 0, 0)),
+        pl.BlockSpec((8, 1, block, part), lambda i: (0, seq, 0, 1)),
+        pl.BlockSpec((8, 1, block, part), lambda i: (0, seq, 0, 2)),
+        whole(grads),
+        rows,
+        rows,
+        angles,
+        angles,
+        whole(cosine),
+        whole(sine),
+        whole(w),
+        pl.BlockSpec((8, 1, block, width), lambda i: (0, seq, 0, 0)),
+    ]
+    shapes = [((5, 1, block, width), BF16), ((3, 1, block, width), BF16)]
+    if last:
+        args.append(before)
+        in_specs.append(whole(before))
+        shapes += [((width, own), BF16), ((8, width), F32)]
+    else:
+        shapes += [((own, width), F32)]
     return pl.pallas_call(
-        attend_back_kernel,
-        grid=(seqs, 4),
-        in_specs=[
-            SCALARS,
-            rows,
-            pl.BlockSpec((8, 1, block, part), lambda s, i: (0, s, 0, 1)),
-            pl.BlockSpec((8, 1, block, part), lambda s, i: (0, s, 0, 2)),
-            whole(grads),
-            rows,
-            rows,
-            angles,
-            angles,
-            whole(cosine),
-            whole(sine),
-            whole(w),
+        functools.partial(attend_back_kernel, seq=seq, last=last),
+        grid=(4,),
+        in_specs=in_specs,
+        out_specs=tuple(full(*shape) for shape, _ in shapes),
+        out_shape=tuple(jax.ShapeDtypeStruct(shape, kind) for shape, kind in shapes),
+        scratch_shapes=[
+            pltpu.VMEM((8 * block, own), BF16),
+            pltpu.VMEM((8 * block, part), F32),
+            pltpu.VMEM((8 * block, part), F32),
         ],
-        out_specs=(by_seq(8, own), by_seq(5, width), by_seq(3, width)),
-        out_shape=(
-            jax.ShapeDtypeStruct((8, seqs, block, own), BF16),
-            jax.ShapeDtypeStruct((5, seqs, block, width), BF16),
-            jax.ShapeDtypeStruct((3, seqs, block, width), BF16),
-        ),
-        scratch_shapes=[pltpu.VMEM((8 * block, part), F32), pltpu.VMEM((8 * block, part), F32)],
         compiler_params=params(),
         name="attend_back",
-    )(place, qkv, qkv, qkv, grads, attended, logs, cosine, sine, cosine, sine, w)
+    )(*args)
 
 
 class Group:
@@ -748,20 +808,14 @@
             return lax.ppermute(values, "ctx", [(0, 1), (1, 0)])
         return lax.ppermute(values, "head", [(i, i ^ bit) for i in range(self.heads)])
 
-    def gather(self, own):
-        own = own[None]
-        mate = self.swap(own, 1)
-        near = lax.ppermute(jnp.concatenate([own, mate]), GROUP, self.near)
-        far = lax.ppermute(near[:1], GROUP, self.far)
-        return own, mate, near, far, self.swap(near, 1), self.swap(far, 1)
-
-    def reduce(self, keep, send):
-        met = keep[2:].astype(F32) + self.swap(send, 1).astype(F32)
-        far = lax.ppermute(met[2].astype(BF16), GROUP, self.far)
-        met = jnp.concatenate([(met[0] + far.astype(F32))[None], met[1:2]])
-        near = lax.ppermute(met.astype(BF16), GROUP, self.near)
-        met = keep[:2].astype(F32) + near.astype(F32)
-        return met[0] + self.swap(met[1].astype(BF16), 1).astype(F32)
+    def mate(self, values):
+        return self.swap(values, 1)
+
+    def to_near(self, values):
+        return lax.ppermute(values, GROUP, self.near)
+
+    def to_far(self, values):
+        return lax.ppermute(values, GROUP, self.far)
 
     def rows_in(self, values, place):
         pairs = [
@@ -781,6 +835,16 @@
 
     def across(self, values, step):
         return lax.ppermute(values, "dp", [(i, i ^ step) for i in range(self.dp)])
+
+    def scatter_dp(self, values):
+        step = self.dp // 2
+        while step:
+            halves = values.reshape(2, step, *values.shape[1:])
+            bit = (self.dp_at // step) % 2
+            sent = self.across(pick(halves, 1 - bit, 0).astype(BF16), step)
+            values = pick(halves, bit, 0).astype(F32) + sent.astype(F32)
+            step //= 2
+        return values[0]
 
     def total(self, values):
         for bit in (1, 2, 4):
@@ -796,8 +860,12 @@
     return lax.dynamic_index_in_dim(array, index, axis, keepdims=False)
 
 
-def after(values, earlier):
+def after(values, *earlier):
     return lax.optimization_barrier((values, earlier))[0]
+
+
+def wide(values):
+    return values.astype(F32)
 
 
 def local_split(tokens, cotangent, w_qkv, w_attn_out, w_in, w_mlp_out, norm_gain1, norm_gain2):
@@ -815,11 +883,15 @@
     straight = list(range(heads))
     order = group.order()
     scalars = jnp.concatenate([order, jnp.stack([group.dp_at, at_c])]).astype(jnp.int32)
+    mate, near, far = group.mate, group.to_near, group.to_far
 
     def in_order(own, other):
         return jnp.where(at_c == 0, jnp.stack([own, other]), jnp.stack([other, own]))
 
-    x_pieces = group.gather(tokens)
+    def exchange(values):
+        return lax.all_to_all(values, GROUP, split_axis=0, concat_axis=0, tiled=True)
+
+
     gains = jnp.pad(
         jnp.stack([norm_gain1, norm_gain2]), ((0, 14), (0, 3 * own_width - rows_here))
     )
@@ -830,86 +902,202 @@
         cut = lax.dynamic_slice_in_dim(qkv_view, start, own_width, 2)
         return jnp.concatenate([cut.reshape(rows_here, 3 * own_width), gains])
 
-    pair = jnp.stack([qkv_part(at_c), group.swap(qkv_part(1 - at_c), 4)])
-    qkv_pieces = [pair] + [group.across(pair, step) for step in range(1, dp)]
-
-    weight_out = group.rows_in(w_attn_out, straight)
-    out_pieces = group.gather(weight_out)
-    in_view = w_in.reshape(rows_here, 2, heads, 2, hidden)
+    x_own = tokens[None]
+    x_mate = mate(x_own)
+    qkv_other, qkv_own = qkv_part(1 - at_c), qkv_part(at_c)
+    x_chip = jnp.concatenate([x_own, after(x_mate, qkv_other, qkv_own)])
+    x_near = near(x_chip)
+    qkv_cross = group.swap(after(qkv_other, x_chip), 4)
+    qkv_pair = jnp.stack([qkv_own, qkv_cross])
+    qkv_pieces = [qkv_pair] + [group.across(qkv_pair, step) for step in range(1, dp)]
+    out_rows = group.rows_in(after(w_attn_out, qkv_pair), straight)
+
+    in_view = after(w_in, qkv_pair).reshape(rows_here, 2, heads, 2, hidden)
     in_view = pick(in_view, 2 * (at_h % half) + at_h // half, 2)
 
     def in_part(at):
         cut = pick(in_view, at, 2)
         return jnp.pad(cut, ((0, 0), (0, 0), (0, padded - hidden))).reshape(rows_here, 2 * padded)
 
-    in_pair = in_order(in_part(at_c), group.swap(in_part(1 - at_c), 4))
-    weight_in = lax.all_gather(after(in_pair, qkv_pieces[-1]), "dp", axis=0).reshape(width, -1)
-    weight_mlp = group.rows_in(after(w_mlp_out, qkv_pieces[-1]), place)
-    weight_mlp = jnp.pad(weight_mlp, ((0, padded - hidden), (0, 0)))
-
-    positions = (order[:, None] * block + jnp.arange(block, dtype=jnp.int32)[None, :]).reshape(-1)
+    in_other, in_own = in_part(1 - at_c), in_part(at_c)
+    in_cross = group.swap(in_other, 4)
+    positions = after(order, qkv_pair)[:, None] * block + jnp.arange(block, dtype=jnp.int32)
     lane = jnp.arange(own_width, dtype=jnp.int32)
     frequency = jnp.exp(
         (lane % (HD // 2)).astype(F32) * (-math.log(ROPE_BASE) / (HD // 2))
     )
-    angles = positions.astype(F32)[:, None] * frequency[None, :]
+    angles = wide(positions.reshape(-1))[:, None] * frequency[None, :]
     cosine = jnp.cos(angles)
     sine = jnp.sin(angles) * jnp.where(lane % HD < HD // 2, -1.0, 1.0)[None, :]
 
-    def exchange(values):
-        return lax.all_to_all(values, GROUP, split_axis=0, concat_axis=0, tiled=True)
-
+    x_near = after(x_near, in_other, in_own, cosine, sine)
+    x_far = far(x_near[:1])
+    x_near_mate = mate(x_near)
+    in_pair = in_order(in_own, after(in_cross, x_near))
+    out_own = after(out_rows, x_near)[None]
+    out_mate = mate(out_own)
+    cot_own = after(cotangent, x_near)[None]
+    cot_mate = mate(cot_own)
+    out_chip = jnp.concatenate([out_own, out_mate])
+    cot_chip = jnp.concatenate([cot_own, cot_mate])
+    x_far = after(x_far, in_pair, out_chip, cot_chip)
+    x_far_mate = mate(x_far)
+
+    out_near = near(after(out_chip, x_far))
+    cot_near = near(after(cot_chip, x_far))
+    in_pair = after(in_pair, x_far, *qkv_pieces)
+    weight_in = lax.all_gather(in_pair, "dp", axis=0).reshape(width, -1)
+    x_pieces = (x_own, x_mate, x_near, x_far, x_near_mate, after(x_far_mate, in_pair))
     low1, qkv, weight_qkv, gain_one, gain_two = project(
         scalars, x_pieces, qkv_pieces, cosine, sine
     )
-    attended, att_low, logs, home = attend(scalars, qkv)
-    residual, low2 = branch(scalars, out_pieces, exchange(home), tokens, gain_two)
-    low2_all = jnp.concatenate(group.gather(low2))
-
-    cot_all = jnp.concatenate(group.gather(after(cotangent, x_pieces[-1])))
-    cot_flat = flat(cot_all)
-    grad_mixed = dot(cot_flat, weight_mlp, ((1,), (1,))).reshape(8, seqs, block, padded)
-    mixed, grad_lifted, keep, send = mlp(low2_all, grad_mixed, weight_in)
-    grad_low2 = group.reduce(keep, send)
+
+    weight_mlp = group.rows_in(after(w_mlp_out, qkv), place)
+    out_near = after(out_near, qkv)
+    out_far, out_near_mate = far(out_near[:1]), mate(out_near)
+    att_0, log_0, home_0 = attend(scalars, after(qkv, out_near), 0)
+    cot_near = after(cot_near, home_0)
+    cot_far, cot_near_mate = far(cot_near[:1]), mate(cot_near)
+    out_far = after(out_far, home_0)
+    out_far_mate = mate(out_far)
+    out_pieces = (out_own, out_mate, out_near, out_far, out_near_mate, out_far_mate)
+    att_1, log_1, home_1 = attend(scalars, after(qkv, cot_near, out_far), 1)
+    home = jnp.concatenate([home_0, home_1], axis=1)
+    att_rows = exchange(home)
+    cot_far = after(cot_far, home)
+    cot_far_mate = mate(cot_far)
+    residual, low2 = branch(
+        scalars, out_pieces, after(att_rows, cot_far), tokens, gain_two
+    )
+
+    low_own = low2[None]
+    low_mate = mate(low_own)
+    low_near = near(jnp.concatenate([low_own, low_mate]))
+    cot_all = jnp.concatenate(
+        [
+            cot_own,
+            cot_mate,
+            cot_near,
+            cot_far,
+            cot_near_mate,
+            after(cot_far_mate, low_mate),
+        ]
+    )
+    weight_mlp = jnp.pad(weight_mlp, ((0, padded - hidden), (0, 0)))
+    grad_mixed = dot(flat(cot_all), weight_mlp, ((1,), (1,)))
+    low_near = after(low_near, grad_mixed)
+    low_far, low_near_mate = far(low_near[:1]), mate(low_near)
+    low_pieces = (low_own, low_mate, low_near, low_far, low_near_mate, mate(low_far))
+    low2_all, mixed, grad_lifted, keep, send = mlp(
+        low_pieces, grad_mixed.reshape(8, seqs, block, padded), weight_in
+    )
+
+    def over_tokens(left, right):
+        return dot(flat(left), flat(right), ((0,), (0,)))
+
+    def scatter(values):
+        return lax.psum_scatter(values.astype(BF16), "dp", scatter_dimension=0, tiled=True)
+
+    def columns_first(values):
+        return jnp.moveaxis(values.reshape(values.shape[0], dp, -1), 1, 0)
+
+    met = mate(send)
+    grad_mlp = columns_first(over_tokens(after(mixed, send), cot_all)[:hidden]).astype(BF16)
+    grad_mlp = scatter(grad_mlp)[0]
+    met = after(met, grad_mlp)
+    last = (wide(keep[4]) + wide(met[2])).astype(BF16)
+    last_far = far(last)
+    cut = 5 * seqs * block
+    mixed_flat = flat(after(mixed, last))
+    out_keep = dot(mixed_flat[:cut], weight_mlp).astype(BF16).reshape(5, seqs, block, width)
+    out_send = dot(mixed_flat[cut:], weight_mlp).astype(BF16).reshape(3, seqs, block, width)
+    last_far = after(last_far, out_keep, out_send)
+    chip = jnp.stack([wide(keep[2]) + wide(met[0]) + wide(last_far), wide(keep[3]) + wide(met[1])])
+    chip = chip.astype(BF16)
+    chip_near = near(chip)
+    out_met = mate(after(out_send, chip))
+    grad_in = over_tokens(low2_all, after(grad_lifted, chip)).astype(BF16)
+    chip_near = after(chip_near, grad_in)
+    grad_in = scatter(grad_in)
+    home = mate((wide(keep[1]) + wide(chip_near[1])).astype(BF16))
+    grad_low2 = wide(keep[0]) + wide(chip_near[0]) + wide(home)
+
     grad_residual, grad_branch, home, gain2_sum = branch_back(
         scalars, out_pieces, grad_low2, residual, cotangent, gain_two
     )
     grad_home = exchange(home)
-    branch_all = jnp.concatenate(group.gather(after(grad_branch, grad_home)))
-    grad_proj, keep, send = attend_back(
-        scalars, qkv, grad_home, attended, logs, cosine, sine, weight_qkv
-    )
-    grad_low1 = group.reduce(keep, send)
-    normed1, factor1 = normalize(tokens.astype(F32))
+
+    rows_keep, rows_send = out_grad(scalars, after(att_rows, home), grad_branch)
+    rows_met = mate(rows_send)
+    out_last = (wide(out_keep[4]) + wide(after(out_met, home)[2])).astype(BF16)
+    rows_last = (wide(rows_keep[4]) + wide(rows_met[2])).astype(BF16)
+    grad_home = after(grad_home, out_last, rows_last)
+    out_far2, rows_far = far(after(out_last, grad_home)), far(after(rows_last, grad_home))
+    keep_0, send_0, before = attend_back(
+        scalars, qkv, grad_home, att_0, log_0, cosine, sine, weight_qkv, low1, 0
+    )
+    met_0 = mate(send_0)
+    out_far2, rows_far = after((out_far2, rows_far), send_0)
+    out_chip = jnp.stack(
+        [
+            wide(out_keep[2]) + wide(out_met[0]) + wide(out_far2),
+            wide(out_keep[3]) + wide(out_met[1]),
+        ]
+    ).astype(BF16)
+    rows_chip = jnp.stack(
+        [
+            wide(rows_keep[2]) + wide(rows_met[0]) + wide(rows_far),
+            wide(rows_keep[3]) + wide(rows_met[1]),
+        ]
+    ).astype(BF16)
+    out_chip_near, rows_chip_near = near(out_chip), near(rows_chip)
+    keep_1, send_1, grad_qkv, gain1_sum = attend_back(
+        scalars, qkv, after(grad_home, out_chip, rows_chip), att_1, log_1, cosine, sine,
+        weight_qkv, low1, 1, before,
+    )
+
+    met_1 = mate(send_1)
+    grad_qkv = scatter(grad_qkv)
+
+    def both(index, at):
+        return jnp.concatenate(
+            [wide(keep_0[index]) + wide(met_0[at]), wide(keep_1[index]) + wide(met_1[at])]
+        )
+
+    last = both(4, 2).astype(BF16)
+    last_far = far(last)
+    rows_chip_near = after(rows_chip_near, last)
+    out_chip_near = after(out_chip_near, last)
+    rows_home = mate((wide(rows_keep[1]) + wide(rows_chip_near[1])).astype(BF16))
+    out_home = mate((wide(out_keep[1]) + wide(out_chip_near[1])).astype(BF16))
+    gain1_sum = gain1_sum[0] / gain_one[0]
+    sums = jnp.stack([gain1_sum, gain2_sum[0]]).reshape(-1, 128)
+    last_far = after(last_far, sums)
+    chip = jnp.stack([both(2, 0) + wide(last_far), both(3, 1)]).astype(BF16)
+    chip_near = near(chip)
+    result = residual + wide(out_keep[0]) + wide(out_chip_near[0]) + wide(after(out_home, chip))
+    result = result.astype(BF16)
+    grad_out = wide(rows_keep[0]) + wide(rows_chip_near[0]) + wide(after(rows_home, chip))
+    grad_out = group.scatter_dp(columns_first(grad_out)).astype(BF16)
+    grad_out = wide(group.rows_back(grad_out, straight))
+    sums = group.total(sums).reshape(2, -1)
+    home = mate(
+        (jnp.concatenate([wide(keep_0[1]), wide(keep_1[1])]) + wide(chip_near[1])).astype(BF16)
+    )
+    grad_low1 = jnp.concatenate([wide(keep_0[0]), wide(keep_1[0])]) + wide(chip_near[0])
+    grad_low1 = grad_low1 + wide(home)
+    normed1, factor1 = normalize(wide(tokens))
     grad_input = grad_residual + norm_back(grad_low1 * gain_one, normed1, factor1)
 
-    mixed_flat = flat(mixed)
-    cut = 5 * seqs * block
-    out_keep = dot(mixed_flat[:cut], weight_mlp).astype(BF16).reshape(5, seqs, block, width)
-    out_send = dot(mixed_flat[cut:], weight_mlp).astype(BF16).reshape(3, seqs, block, width)
-    result = (residual + group.reduce(out_keep, out_send)).astype(BF16)
-
-    def over_tokens(left, right):
-        return dot(flat(left), flat(right), ((0,), (0,)))
-
-    def scatter(values):
-        return lax.psum_scatter(values.astype(BF16), "dp", scatter_dimension=0, tiled=True)
-
-    def columns_first(values):
-        return jnp.moveaxis(values.reshape(values.shape[0], dp, -1), 1, 0)
-
-    grad_mlp = scatter(columns_first(over_tokens(mixed, cot_flat)[:hidden]))[0]
-    grad_mlp = group.rows_back(grad_mlp, place).astype(F32)
-    grad_out = scatter(columns_first(over_tokens(att_low, branch_all)))[0]
-    grad_out = group.rows_back(grad_out, straight).astype(F32)
+    grad_mlp = wide(group.rows_back(grad_mlp, place))
 
     def rows_here_of(values):
-        both = values.reshape(2, rows_here, -1)
-        own = pick(both, at_c, 0)
-        other = group.swap(pick(both, 1 - at_c, 0), 4)
+        pair = values.reshape(2, rows_here, -1)
+        own = pick(pair, at_c, 0)
+        other = group.swap(pick(pair, 1 - at_c, 0), 4)
         return in_order(own, other)
 
-    grad_in = rows_here_of(scatter(over_tokens(low2_all, grad_lifted)))
+    grad_in = rows_here_of(grad_in)
     grad_in = jnp.stack([grad_in[..., :hidden], grad_in[..., padded : padded + hidden]])
     late = at_h // half
     stays = pick(grad_in, late, 0)
@@ -917,27 +1105,23 @@
     grad_in = jnp.where(
         late == 0, jnp.concatenate([stays, comes]), jnp.concatenate([comes, stays])
     )
-    grad_in = jnp.moveaxis(grad_in, 0, 1).reshape(rows_here, -1).astype(F32)
-
-    grad_qkv = over_tokens(low1, grad_proj)
-    gain1_sum = jnp.sum(grad_qkv * weight_qkv.astype(F32), axis=1) / gain_one[0]
-    sums = group.total(jnp.stack([gain1_sum, gain2_sum[0]]).reshape(-1, 128))
-    sums = sums.reshape(2, -1)
+    grad_in = wide(jnp.moveaxis(grad_in, 0, 1).reshape(rows_here, -1))
+
     per_device = width // (dp * parts)
     start = (group.dp_at * parts + group.at) * per_device
     grad_gain1, grad_gain2 = (
         lax.dynamic_slice_in_dim(sums[i], start, per_device, 0) for i in range(2)
     )
-    grad_qkv = rows_here_of(scatter(grad_qkv)).reshape(2, rows_here, 3, own_width)
+    grad_qkv = rows_here_of(grad_qkv).reshape(2, rows_here, 3, own_width)
     grad_qkv = jnp.moveaxis(grad_qkv, 2, 0)
-    odd, late = at_h % 2, at_h // half
+    odd = at_h % 2
     stays = pick(grad_qkv, odd + late, 0)
     core = group.swap(pick(grad_qkv, 1 - odd + late, 0), 1)
     chip = group.swap(pick(grad_qkv, 2 - 2 * late, 0), 2)
     grad_qkv = jnp.where(
         odd == 0, jnp.concatenate([stays, core, chip]), jnp.concatenate([chip, core, stays])
     )
-    grad_qkv = jnp.moveaxis(grad_qkv, 0, 1).reshape(rows_here, -1).astype(F32)
+    grad_qkv = wide(jnp.moveaxis(grad_qkv, 0, 1).reshape(rows_here, -1))
 
     return (
         result,

time: 462 us -> 456 us (0.987)
  the two profiles are of different devices: /device:TPU:4 before, /device:TPU:0 now
where the time goes in v3:
time: 456 us; the launch traced here: 447 us
  waiting for transfers between devices  131 us (29%)
  starting transfers between devices  117 us (26%)
  Pallas kernels  80 us (18%)
  other arithmetic  51.4 us (11%)
  local copies, waits for them, and re-layouts  36.9 us (8%)
  matrix products  15.6 us (3%)
  between operations  14.9 us (3%)
    ppermute x26, starting transfers between devices, swap(): lax.ppermute(values, 'head', [(i, i ^ bit) for i in range(self.heads)])  48.2 us
    ppermute x7, waiting for transfers between devices, across(): return lax.ppermute(values, 'dp', [(i, i ^ step) for i in range(self.dp)])  31.9 us
    ppermute x5, waiting for transfers between devices, swap(): return lax.ppermute(values, 'ctx', [(0, 1), (1, 0)])  30.2 us
    ppermute x8, starting transfers between devices, to_far(): return lax.ppermute(values, GROUP, self.far)  30.1 us
    pallas_call x2, Pallas kernels, attend_back(): pl.pallas_call(functools.partial(attend_back_kernel, seq=seq, last=last),...  28.3 us
    reduce_scatter x3, waiting for transfers between devices, scatter(): lax.psum_scatter(values.astype(BF16), 'dp', scatter_dimension=0, tiled=True)  21.5 us
    pallas_call x1, Pallas kernels, mlp(): pl.pallas_call(mlp_kernel, grid=(8,), in_specs=[within(at, piece.shape[0]...  17.5 us
    ppermute x8, waiting for transfers between devices, to_far(): return lax.ppermute(values, GROUP, self.far)  16.6 us
  transfers between devices with their start and end apart: 64, of which 22 were waited for; matrix products, arithmetic and copies ran while one was open for 20% of the time, Pallas kernels for 13%

profile of v3, /device:TPU:0, one launch (start us, length us, event | category | flops | bytes accessed | tf_op | source)
XLA Modules:
  0.0 446.6 jit_solution(8455477420524157952)
XLA Ops:
  11.5 2.6 collective-permute-start.3
  14.1 15.3 %collective-permute-done.1 = bf16[144,384]{1,0:T(8,128)(2,1)S(1)} collective-permute-done((bf16[144,384]{1,0:T(8,128)(2,1)S(1)}, bf16[144,384]{1,0:T(8,128)(2,1)S(1)}, u32[]{:S(2)}, u32[]{:S(2)}) %collective-permute-start.1) | collective-permute-done | bytes 110624 | tf_op jit(solution)/shard_map/ppermute | solution.py:808
  31.8 3.1 fusion.25
  34.9 2.5 copy.37
  38.4 2.6 collective-permute-start.7
  43.5 4.5 %collective-permute-start.5 = (bf16[1,2,128,1024]{3,2,1,0:T(8,128)(2,1)}, bf16[1,2,128,1024]{3,2,1,0:T(8,128)(2,1)}, u32[]{:S(2)}, u32[]{:S(2)}) collective-permute-start(bf16[1,2,128,1024]{3,2,1,0:T(8,128)(2,1)} %slice.194), channel_id=1, source_target_pairs={{0,2},{1,5},{2,0},{3,7},{4,6},{5,1},{6,4},{7,3},{8,10},{9,13},{10,... | collective-permute-start | bytes 1572872 | tf_op jit(solution)/shard_map/ppermute | solution.py:818
  52.7 2.8 collective-permute-done.5.refs_3_
  58.5 6.2 %collective-permute-done.11.refs_7_ = bf16[2,144,384]{2,1,0:T(8,128)(2,1)} collective-permute-done((bf16[2,144,384]{2,1,0:T(8,128)(2,1)}, bf16[2,144,384]{2,1,0:T(8,128)(2,1)}, u32[]{:S(2)}, u32[]{:S(2)}) %collective-permute-start.11) | collective-permute-done | bytes 221216 | tf_op jit(solution)/shard_map/ppermute | solution.py:837
  64.6 12.3 %collective-permute-done.12.refs_8_ = bf16[2,144,384]{2,1,0:T(8,128)(2,1)} collective-permute-done((bf16[2,144,384]{2,1,0:T(8,128)(2,1)}, bf16[2,144,384]{2,1,0:T(8,128)(2,1)}, u32[]{:S(2)}, u32[]{:S(2)}) %collective-permute-start.12) | collective-permute-done | bytes 221216 | tf_op jit(solution)/shard_map/ppermute | solution.py:837
  77.8 8.7 %collective-permute-done.13.refs_9_ = bf16[2,144,384]{2,1,0:T(8,128)(2,1)} collective-permute-done((bf16[2,144,384]{2,1,0:T(8,128)(2,1)}, bf16[2,144,384]{2,1,0:T(8,128)(2,1)}, u32[]{:S(2)}, u32[]{:S(2)}) %collective-permute-start.13) | collective-permute-done | bytes 221216 | tf_op jit(solution)/shard_map/ppermute | solution.py:837
  86.5 9.0 %project.1 = (bf16[8,2,128,1024]{3,2,1,0:T(8,128)(2,1)}, bf16[8,2,128,384]{3,2,1,0:T(8,128)(2,1)}, bf16[1024,384]{1,0:T(8,128)(2,1)}, f32[1,1024]{1,0:T(1,128)}, f32[1,1024]{1,0:T(1,128)}) custom-call(s32[10]{0:T(128)} %concatenate.65.place_ref, bf16[1,2,128,1024]{3,2,1,0:T(8,128)(2,1)} %bitcast.197, bf16[1,2,128,1024]{3,2,1,0:T(8,128)(2,1)} %copy-done.15, ...), custom_call_target="tpu_custom_call" | custom-call | tf_op jit(solution)/shard_map/project/pallas_call | solution.py:452
  96.8 6.4 %attend.2 = (f32[8,1,128,128]{3,2,1,0:T(8,128)}, f32[8,1,128,128]{3,2,1,0:T(8,128)}, bf16[8,1,128,128]{3,2,1,0:T(8,128)(2,1)}) custom-call(s32[10]{0:T(128)} %concatenate.65.place_ref, bf16[8,2,128,384]{3,2,1,0:T(8,128)(2,1)} %get-tuple-element.103.q_ref.k_ref.v_ref, bf16[8,2,128,384]{3,2,1,0:T(8,128)(2,1)} %get-tuple-element.103.q_ref.k_ref.v_ref, ...), custom_call_target="tpu_custom_call" | custom-call | tf_op jit(solution)/shard_map/attend/pallas_call | solution.py:504
  103.2 1.7 constant_dynamic-update-slice_fusion.1
  105.8 6.4 %attend.3 = (f32[8,1,128,128]{3,2,1,0:T(8,128)}, f32[8,1,128,128]{3,2,1,0:T(8,128)}, bf16[8,1,128,128]{3,2,1,0:T(8,128)(2,1)}) custom-call(s32[10]{0:T(128)} %concatenate.65.place_ref, bf16[8,2,128,384]{3,2,1,0:T(8,128)(2,1)} %get-tuple-element.103.q_ref.k_ref.v_ref, bf16[8,2,128,384]{3,2,1,0:T(8,128)(2,1)} %get-tuple-element.103.q_ref.k_ref.v_ref, ...), custom_call_target="tpu_custom_call" | custom-call | tf_op jit(solution)/shard_map/attend/pallas_call | solution.py:504
  113.1 1.7 constant_dynamic-update-slice_fusion
  114.8 3.6 all-to-all-start
  119.0 2.8 collective-permute-done.18
  121.7 5.7 %all-to-all-done.refs_6_.rows_ref = bf16[8,2,128,128]{3,2,1,0:T(8,128)(2,1)S(1)} async-done(((bf16[8,2,128,128]{3,2,1,0:T(8,128)(2,1)}), bf16[8,2,128,128]{3,2,1,0:T(8,128)(2,1)S(1)}, u32[]{:S(2)}, u32[]{:S(2)}) %all-to-all-start) | async-done | bytes 524320 | tf_op jit(solution)/shard_map/all_to_all | solution.py:892
  128.4 4.2 branch.1
  134.2 2.3 collective-permute-start.23
  136.5 1.7 collective-permute-start.22
  144.8 4.1 fusion.23
  148.9 5.6 %collective-permute-done.20.refs_2_ = bf16[2,2,128,1024]{3,2,1,0:T(8,128)(2,1)S(1)} collective-permute-done((bf16[2,2,128,1024]{3,2,1,0:T(8,128)(2,1)S(1)}, bf16[2,2,128,1024]{3,2,1,0:T(8,128)(2,1)S(1)}, u32[]{:S(2)}, u32[]{:S(2)}) %collective-permute-start.20) | collective-permute-done | bytes 1048608 | tf_op jit(solution)/shard_map/ppermute | solution.py:815
  154.5 20.8 %collective-permute-start.24 = (bf16[1,2,128,1024]{3,2,1,0:T(8,128)(2,1)S(1)}, bf16[1,2,128,1024]{3,2,1,0:T(8,128)(2,1)S(1)}, u32[]{:S(2)}, u32[]{:S(2)}) collective-permute-start(bf16[1,2,128,1024]{3,2,1,0:T(8,128)(2,1)S(1)} %slice.197), channel_id=1, source_target_pairs={{0,2},{1,5},{2,0},{3,7},{4,6},{5,1},{6,4},{7,3},{8,10},{9,13},{10,... | collective-permute-start | bytes 1572872 | tf_op jit(solution)/shard_map/ppermute | solution.py:818
  175.3 24.1 %collective-permute-start.25 = (bf16[2,2,128,1024]{3,2,1,0:T(8,128)(2,1)S(1)}, bf16[2,2,128,1024]{3,2,1,0:T(8,128)(2,1)S(1)}, u32[]{:S(2)}, u32[]{:S(2)}) collective-permute-start(bf16[2,2,128,1024]{3,2,1,0:T(8,128)(2,1)S(1)} %collective-permute-done.20.refs_2_), channel_id=1, source_target_pairs={{0,1},{1,0},{2,3},{3,2},{4,5},{5,4},{6,7},{7,6},{8,9},{9,8},{10,11... | collective-permute-start | bytes 3145736 | tf_op jit(solution)/shard_map/ppermute | solution.py:809
  199.4 6.7 %collective-permute-start.26 = (bf16[1,2,128,1024]{3,2,1,0:T(8,128)(2,1)S(1)}, bf16[1,2,128,1024]{3,2,1,0:T(8,128)(2,1)S(1)}, u32[]{:S(2)}, u32[]{:S(2)}) collective-permute-start(bf16[1,2,128,1024]{3,2,1,0:T(8,128)(2,1)S(1)} %collective-permute-done.24.refs_3_), channel_id=1, source_target_pairs={{0,1},{1,0},{2,3},{3,2},{4,5},{5,4},{6,7},{7,6},{8,9},{9,8},{10,11... | collective-permute-start | bytes 1572872 | tf_op jit(solution)/shard_map/ppermute | solution.py:809
  208.8 17.5 %mlp.1 = (bf16[8,2,128,1024]{3,2,1,0:T(8,128)(2,1)}, bf16[8,2,128,384]{3,2,1,0:T(8,128)(2,1)}, bf16[8,2,128,768]{3,2,1,0:T(8,128)(2,1)}, bf16[5,2,128,1024]{3,2,1,0:T(8,128)(2,1)}, bf16[3,2,128,1024]{3,2,1,0:T(8,128)(2,1)}) custom-call(bf16[1,2,128,1024]{3,2,1,0:T(8,128)(2,1)} %bitcast.216, bf16[1,2,128,1024]{3,2,1,0:T(8,128)(2,1)} %copy-done.16, ...), custom_call_target="tpu_custom_call" | custom-call | tf_op jit(solution)/shard_map/mlp/pallas_call | solution.py:602
  226.7 3.2 convolution_bitcast_fusion
  231.2 21.5 %reduce-scatter.4.cloned.1.call-done = bf16[1,328,256]{2,1,0:T(8,128)(2,1)} async-done(((bf16[4,328,256]{2,1,0:T(8,128)(2,1)}), bf16[1,328,256]{2,1,0:T(8,128)(2,1)}) %reduce-scatter.4.cloned.1.call-update) | async-done | bytes 167952 | tf_op jit(solution)/shard_map/reduce_scatter | solution.py:999
  255.9 2.1 convolution_convert_fusion.1
  258.0 5.5 %collective-permute-done.28 = bf16[2,128,1024]{2,1,0:T(8,128)(2,1)S(1)} collective-permute-done((bf16[2,128,1024]{2,1,0:T(8,128)(2,1)S(1)}, bf16[2,128,1024]{2,1,0:T(8,128)(2,1)S(1)}, u32[]{:S(2)}, u32[]{:S(2)}) %collective-permute-start.28) | collective-permute-done | bytes 524320 | tf_op jit(solution)/shard_map/ppermute | solution.py:818
  267.4 4.7 %bitcast_convert_fusion = bf16[1024,768]{1,0:T(8,128)(2,1)} fusion(bf16[8,2,128,1024]{3,2,1,0:T(8,128)(2,1)S(1)} %copy-done.31, bf16[8,2,128,768]{3,2,1,0:T(8,128)(2,1)S(1)} %copy-done.32), kind=kOutput, calls=%fused_computation.1 | convolution fusion | flops 3222011904 | bytes 8912896 | tf_op jit(solution)/shard_map/dot_general | solution.py:373
  272.1 8.8 %collective-permute-done.30 = bf16[2,2,128,1024]{3,2,1,0:T(8,128)(2,1)S(1)} collective-permute-done((bf16[2,2,128,1024]{3,2,1,0:T(8,128)(2,1)}, bf16[2,2,128,1024]{3,2,1,0:T(8,128)(2,1)S(1)}, u32[]{:S(2)}, u32[]{:S(2)}) %collective-permute-start.30) | collective-permute-done | bytes 1048608 | tf_op jit(solution)/shard_map/ppermute | solution.py:815
  282.4 1.8 collective-permute-done.31
  284.1 2.4 bitcast_add_fusion.refs_6_
  286.5 5.1 %branch_back.1 = (f32[2,128,1024]{2,1,0:T(8,128)}, bf16[2,128,1024]{2,1,0:T(8,128)(2,1)}, bf16[8,2,128,128]{3,2,1,0:T(8,128)(2,1)}, f32[1,1024]{1,0:T(1,128)}) custom-call(s32[10]{0:T(128)} %concatenate.65.place_ref, bf16[1,128,1024]{2,1,0:T(8,128)(2,1)} %bitcast.208, bf16[1,128,1024]{2,1,0:T(8,128)(2,1)} %copy-done.13, bf16[2,128,1024]{2,1,0:T(8,128)(2,1)} %copy-done.9, ...), custom_call_target="tpu_custom_call" | custom-call | tf_op jit(solution)/shard_map/branch_back/pallas_call | solution.py:666
  291.5 3.1 out_grad.1
  297.6 3.7 all-to-all-start.1
  301.6 2.1 fusion.17
  304.9 5.3 %all-to-all-done.1.grad_ref = bf16[8,2,128,128]{3,2,1,0:T(8,128)(2,1)S(1)} async-done(((bf16[8,2,128,128]{3,2,1,0:T(8,128)(2,1)}), bf16[8,2,128,128]{3,2,1,0:T(8,128)(2,1)S(1)}, u32[]{:S(2)}, u32[]{:S(2)}) %all-to-all-start.1) | async-done | bytes 524320 | tf_op jit(solution)/shard_map/all_to_all | solution.py:892
  313.7 13.7 %attend_back.2 = (bf16[5,1,128,1024]{3,2,1,0:T(8,128)(2,1)}, bf16[3,1,128,1024]{3,2,1,0:T(8,128)(2,1)}, f32[384,1024]{1,0:T(8,128)}) custom-call(s32[10]{0:T(128)} %concatenate.65.place_ref, bf16[8,2,128,384]{3,2,1,0:T(8,128)(2,1)} %get-tuple-element.103.q_ref.k_ref.v_ref, bf16[8,2,128,384]{3,2,1,0:T(8,128)(2,1)} %get-tuple-element.103.q_ref.k_ref.v_ref, ...), custom_call_target="tpu_custom_call" | custom-call | tf_op jit(solution)/shard_map/attend_back/pallas_call | solution.py:767
  330.8 14.5 %attend_back.3 = (bf16[5,1,128,1024]{3,2,1,0:T(8,128)(2,1)}, bf16[3,1,128,1024]{3,2,1,0:T(8,128)(2,1)}, bf16[1024,384]{1,0:T(8,128)(2,1)}, f32[8,1024]{1,0:T(8,128)}) custom-call(s32[10]{0:T(128)} %concatenate.65.place_ref, bf16[8,2,128,384]{3,2,1,0:T(8,128)(2,1)} %get-tuple-element.103.q_ref.k_ref.v_ref, ...), custom_call_target="tpu_custom_call" | custom-call | tf_op jit(solution)/shard_map/attend_back/pallas_call | solution.py:767
  350.2 2.1 collective-permute-start.36
  353.8 2.3 collective-permute-done.55
  356.0 4.0 collective-permute-start.56
  360.0 1.8 slice_bitcast_fusion.6
  361.8 2.0 collective-permute-start.45
  363.8 1.9 collective-permute-start.57
  366.5 2.0 collective-permute-done.57
  368.4 1.8 constant_dynamic-slice_fusion.1
  370.2 1.8 copy.46
  372.1 1.8 copy.53
  373.9 1.7 add_bitcast_fusion.1
  375.5 12.0 %collective-permute-done.50 = bf16[128,768]{0,1:T(8,128)(2,1)} collective-permute-done((bf16[128,768]{0,1:T(8,128)(2,1)}, bf16[128,768]{0,1:T(8,128)(2,1)}, u32[]{:S(2)}, u32[]{:S(2)}) %collective-permute-start.50) | collective-permute-done | bytes 196640 | tf_op jit(solution)/shard_map/ppermute | solution.py:808
  388.8 2.9 collective-permute-start.51
  397.1 5.5 %collective-permute-done.39 = bf16[2,128,1024]{2,1,0:T(8,128)(2,1)S(1)} collective-permute-done((bf16[2,128,1024]{2,1,0:T(8,128)(2,1)S(1)}, bf16[2,128,1024]{2,1,0:T(8,128)(2,1)S(1)}, u32[]{:S(2)}, u32[]{:S(2)}) %collective-permute-start.39) | collective-permute-done | bytes 524320 | tf_op jit(solution)/shard_map/ppermute | solution.py:818
  407.7 2.3 fusion.13
  410.0 2.9 collective-permute-done.47
  414.3 2.0 collective-permute-start.48
  421.7 2.1 collective-permute-start.49
  425.7 1.9 fusion.10
  428.4 2.4 collective-permute-start.44
  430.8 2.3 fusion.15
  437.3 2.5 fusion.7
  (262 shorter events, 87.7 us)
Async XLA Ops:
  7.2 3.1 collective-permute-start
  11.5 26.9 %collective-permute-start.3 = (bf16[2,2,128,1024]{3,2,1,0:T(8,128)(2,1)}, bf16[2,2,128,1024]{3,2,1,0:T(8,128)(2,1)S(1)}, u32[]{:S(2)}, u32[]{:S(2)}) collective-permute-start(bf16[2,2,128,1024]{3,2,1,0:T(8,128)(2,1)} %pad_maximum_fusion), channel_id=1, source_target_pairs={{0,4},{1,3},{2,6},{3,1},{4,0},{5,7},{6,2},{7,5},{8,12},{9,11},{10,... | collective-permute-start | bytes 3145736 | tf_op jit(solution)/shard_map/ppermute | solution.py:815
  14.1 15.4 %collective-permute-start.1 = (bf16[144,384]{1,0:T(8,128)(2,1)S(1)}, bf16[144,384]{1,0:T(8,128)(2,1)S(1)}, u32[]{:S(2)}, u32[]{:S(2)}) collective-permute-start(bf16[144,384]{1,0:T(8,128)(2,1)S(1)} %get-tuple-element.84), channel_id=1, source_target_pairs={{0,4},{4,0},{1,5},{5,1},{2,6},{6,2},{3,7},{7,3},{8,12},{12,8},{9,1... | collective-permute-start | bytes 331784 | tf_op jit(solution)/shard_map/ppermute | solution.py:808
  30.1 12.4 %collective-permute-start.2 = (bf16[128,1024]{1,0:T(8,128)(2,1)}, bf16[128,1024]{1,0:T(8,128)(2,1)S(1)}, u32[]{:S(2)}, u32[]{:S(2)}) collective-permute-start(bf16[128,1024]{1,0:T(8,128)(2,1)} %param.11), channel_id=1, source_target_pairs={{0,0},{8,1},{16,2},{24,3},{1,8},{9,9},{17,10},{25,11},{2,16},{10,1... | collective-permute-start | bytes 786440 | tf_op jit(solution)/shard_map/ppermute | solution.py:826
  38.4 13.0 %collective-permute-start.7 = (bf16[1,2,128,1024]{3,2,1,0:T(8,128)(2,1)S(1)}, bf16[1,2,128,1024]{3,2,1,0:T(8,128)(2,1)S(1)}, u32[]{:S(2)}, u32[]{:S(2)}) collective-permute-start(bf16[1,2,128,1024]{3,2,1,0:T(8,128)(2,1)S(1)} %bitcast.200), channel_id=1, source_target_pairs={{0,1},{1,0},{2,3},{3,2},{4,5},{5,4},{6,7},{7,6},{8,9},{9,8},{10,11... | collective-permute-start | bytes 1572872 | tf_op jit(solution)/shard_map/ppermute | solution.py:809
  41.0 7.8 %collective-permute-start.6 = (bf16[128,768]{0,1:T(8,128)(2,1)S(1)}, bf16[128,768]{0,1:T(8,128)(2,1)S(1)}, u32[]{:S(2)}, u32[]{:S(2)}) collective-permute-start(bf16[128,768]{0,1:T(8,128)(2,1)S(1)} %bitcast.233), channel_id=1, source_target_pairs={{0,4},{4,0},{1,5},{5,1},{2,6},{6,2},{3,7},{7,3},{8,12},{12,8},{9,1... | collective-permute-start | bytes 589832 | tf_op jit(solution)/shard_map/ppermute | solution.py:808
  42.5 8.0 %collective-permute-start.4 = (bf16[1,128,1024]{2,1,0:T(8,128)(2,1)S(1)}, bf16[1,128,1024]{2,1,0:T(8,128)(2,1)S(1)}, u32[]{:S(2)}, u32[]{:S(2)}) collective-permute-start(bf16[1,128,1024]{2,1,0:T(8,128)(2,1)S(1)} %bitcast.205), channel_id=1, source_target_pairs={{0,1},{1,0},{2,3},{3,2},{4,5},{5,4},{6,7},{7,6},{8,9},{9,8},{10,11... | collective-permute-start | bytes 786440 | tf_op jit(solution)/shard_map/ppermute | solution.py:809
  43.5 12.0 %collective-permute-start.5 = (bf16[1,2,128,1024]{3,2,1,0:T(8,128)(2,1)}, bf16[1,2,128,1024]{3,2,1,0:T(8,128)(2,1)}, u32[]{:S(2)}, u32[]{:S(2)}) collective-permute-start(bf16[1,2,128,1024]{3,2,1,0:T(8,128)(2,1)} %slice.194), channel_id=1, source_target_pairs={{0,2},{1,5},{2,0},{3,7},{4,6},{5,1},{6,4},{7,3},{8,10},{9,13},{10,... | collective-permute-start | bytes 1572872 | tf_op jit(solution)/shard_map/ppermute | solution.py:818
  48.0 38.5 %collective-permute-start.9 = (bf16[2,2,128,1024]{3,2,1,0:T(8,128)(2,1)S(1)}, bf16[2,2,128,1024]{3,2,1,0:T(8,128)(2,1)}, u32[]{:S(2)}, u32[]{:S(2)}) collective-permute-start(bf16[2,2,128,1024]{3,2,1,0:T(8,128)(2,1)S(1)} %collective-permute-done.3.refs_2_), channel_id=1, source_target_pairs={{0,1},{1,0},{2,3},{3,2},{4,5},{5,4},{6,7},{7,6},{8,9},{9,8},{10,11... | collective-permute-start | bytes 3145736 | tf_op jit(solution)/shard_map/ppermute | solution.py:809
  55.5 49.4 %collective-permute-start.17 = (bf16[2,2,128,1024]{3,2,1,0:T(8,128)(2,1)}, bf16[2,2,128,1024]{3,2,1,0:T(8,128)(2,1)S(1)}, u32[]{:S(2)}, u32[]{:S(2)}) collective-permute-start(bf16[2,2,128,1024]{3,2,1,0:T(8,128)(2,1)} %pad_maximum_fusion.1), channel_id=1, source_target_pairs={{0,4},{1,3},{2,6},{3,1},{4,0},{5,7},{6,2},{7,5},{8,12},{9,11},{10,... | collective-permute-start | bytes 3145736 | tf_op jit(solution)/shard_map/ppermute | solution.py:815
  57.0 7.7 %collective-permute-start.11 = (bf16[2,144,384]{2,1,0:T(8,128)(2,1)}, bf16[2,144,384]{2,1,0:T(8,128)(2,1)}, u32[]{:S(2)}, u32[]{:S(2)}) collective-permute-start(bf16[2,144,384]{2,1,0:T(8,128)(2,1)} %pad_maximum_fusion.11.refs_6_), channel_id=1, source_target_pairs={{0,8},{8,0},{16,24},{24,16},{1,9},{9,1},{17,25},{25,17},{2,10},{10... | collective-permute-start | bytes 663560 | tf_op jit(solution)/shard_map/ppermute | solution.py:837
  57.2 29.3 %collective-permute-start.10 = (bf16[1,2,128,1024]{3,2,1,0:T(8,128)(2,1)}, bf16[1,2,128,1024]{3,2,1,0:T(8,128)(2,1)}, u32[]{:S(2)}, u32[]{:S(2)}) collective-permute-start(bf16[1,2,128,1024]{3,2,1,0:T(8,128)(2,1)} %collective-permute-done.5.refs_3_), channel_id=1, source_target_pairs={{0,1},{1,0},{2,3},{3,2},{4,5},{5,4},{6,7},{7,6},{8,9},{9,8},{10,11... | collective-permute-start | bytes 1572872 | tf_op jit(solution)/shard_map/ppermute | solution.py:809
  57.2 38.4 %collective-permute-start.8 = (bf16[2,128,1024]{2,1,0:T(8,128)(2,1)}, bf16[2,128,1024]{2,1,0:T(8,128)(2,1)S(1)}, u32[]{:S(2)}, u32[]{:S(2)}) collective-permute-start(bf16[2,128,1024]{2,1,0:T(8,128)(2,1)} %pad_maximum_fusion.6), channel_id=1, source_target_pairs={{0,4},{1,3},{2,6},{3,1},{4,0},{5,7},{6,2},{7,5},{8,12},{9,11},{10,... | collective-permute-start | bytes 1572872 | tf_op jit(solution)/shard_map/ppermute | solution.py:815
  64.6 12.3 %collective-permute-start.12 = (bf16[2,144,384]{2,1,0:T(8,128)(2,1)}, bf16[2,144,384]{2,1,0:T(8,128)(2,1)}, u32[]{:S(2)}, u32[]{:S(2)}) collective-permute-start(bf16[2,144,384]{2,1,0:T(8,128)(2,1)} %pad_maximum_fusion.11.refs_6_), channel_id=1, source_target_pairs={{0,16},{8,24},{16,0},{24,8},{1,17},{9,25},{17,1},{25,9},{2,18},{10... | collective-permute-start | bytes 663560 | tf_op jit(solution)/shard_map/ppermute | solution.py:837
  76.9 9.6 %collective-permute-start.13 = (bf16[2,144,384]{2,1,0:T(8,128)(2,1)}, bf16[2,144,384]{2,1,0:T(8,128)(2,1)}, u32[]{:S(2)}, u32[]{:S(2)}) collective-permute-start(bf16[2,144,384]{2,1,0:T(8,128)(2,1)} %pad_maximum_fusion.11.refs_6_), channel_id=1, source_target_pairs={{0,24},{8,16},{16,8},{24,0},{1,25},{9,17},{17,9},{25,1},{2,26},{10... | collective-permute-start | bytes 663560 | tf_op jit(solution)/shard_map/ppermute | solution.py:837
  95.6 9.3 %collective-permute-start.14 = (bf16[1,128,1024]{2,1,0:T(8,128)(2,1)S(1)}, bf16[1,128,1024]{2,1,0:T(8,128)(2,1)S(1)}, u32[]{:S(2)}, u32[]{:S(2)}) collective-permute-start(bf16[1,128,1024]{2,1,0:T(8,128)(2,1)S(1)} %slice.195), channel_id=1, source_target_pairs={{0,2},{1,5},{2,0},{3,7},{4,6},{5,1},{6,4},{7,3},{8,10},{9,13},{10,... | collective-permute-start | bytes 786440 | tf_op jit(solution)/shard_map/ppermute | solution.py:818
  95.7 31.8 %collective-permute-start.15 = (bf16[2,128,1024]{2,1,0:T(8,128)(2,1)S(1)}, bf16[2,128,1024]{2,1,0:T(8,128)(2,1)S(1)}, u32[]{:S(2)}, u32[]{:S(2)}) collective-permute-start(bf16[2,128,1024]{2,1,0:T(8,128)(2,1)S(1)} %collective-permute-done.8.refs_2_), channel_id=1, source_target_pairs={{0,1},{1,0},{2,3},{3,2},{4,5},{5,4},{6,7},{7,6},{8,9},{9,8},{10,11... | collective-permute-start | bytes 1572872 | tf_op jit(solution)/shard_map/ppermute | solution.py:809
  112.2 9.6 %collective-permute-start.18 = (bf16[1,2,128,1024]{3,2,1,0:T(8,128)(2,1)}, bf16[1,2,128,1024]{3,2,1,0:T(8,128)(2,1)}, u32[]{:S(2)}, u32[]{:S(2)}) collective-permute-start(bf16[1,2,128,1024]{3,2,1,0:T(8,128)(2,1)} %slice.196), channel_id=1, source_target_pairs={{0,2},{1,5},{2,0},{3,7},{4,6},{5,1},{6,4},{7,3},{8,10},{9,13},{10,... | collective-permute-start | bytes 1572872 | tf_op jit(solution)/shard_map/ppermute | solution.py:818
  114.8 12.6 %all-to-all-start = ((bf16[8,2,128,128]{3,2,1,0:T(8,128)(2,1)}), bf16[8,2,128,128]{3,2,1,0:T(8,128)(2,1)S(1)}, u32[]{:S(2)}, u32[]{:S(2)}) async-start(bf16[8,2,128,128]{3,2,1,0:T(8,128)(2,1)} %constant_dynamic-update-slice_fusion), calls=%async_computation | async-start | bytes 1048576 | tf_op jit(solution)/shard_map/all_to_all | solution.py:892
  118.4 87.6 %all-gather.3.cloned.1.call-start = ((), (), s32[]{:S(2)}) async-start(), calls=%async_computation.8 | async-start | bytes 1966080 | tf_op jit(solution)/shard_map/all_gather | solution.py:949
  118.5 9.0 %collective-permute-start.16 = (bf16[1,128,1024]{2,1,0:T(8,128)(2,1)}, bf16[1,128,1024]{2,1,0:T(8,128)(2,1)}, u32[]{:S(2)}, u32[]{:S(2)}) collective-permute-start(bf16[1,128,1024]{2,1,0:T(8,128)(2,1)} %copy-done.22), channel_id=1, source_target_pairs={{0,1},{1,0},{2,3},{3,2},{4,5},{5,4},{6,7},{7,6},{8,9},{9,8},{10,11... | collective-permute-start | bytes 786440 | tf_op jit(solution)/shard_map/ppermute | solution.py:809
  132.6 5.6 %collective-permute-start.19 = (bf16[1,2,128,1024]{3,2,1,0:T(8,128)(2,1)}, bf16[1,2,128,1024]{3,2,1,0:T(8,128)(2,1)S(1)}, u32[]{:S(2)}, u32[]{:S(2)}) collective-permute-start(bf16[1,2,128,1024]{3,2,1,0:T(8,128)(2,1)} %bitcast.214), channel_id=1, source_target_pairs={{0,1},{1,0},{2,3},{3,2},{4,5},{5,4},{6,7},{7,6},{8,9},{9,8},{10,11... | collective-permute-start | bytes 1572872 | tf_op jit(solution)/shard_map/ppermute | solution.py:809
  132.7 10.8 %collective-permute-start.21 = (bf16[2,2,128,1024]{3,2,1,0:T(8,128)(2,1)S(1)}, bf16[2,2,128,1024]{3,2,1,0:T(8,128)(2,1)}, u32[]{:S(2)}, u32[]{:S(2)}) collective-permute-start(bf16[2,2,128,1024]{3,2,1,0:T(8,128)(2,1)S(1)} %collective-permute-done.17), channel_id=1, source_target_pairs={{0,1},{1,0},{2,3},{3,2},{4,5},{5,4},{6,7},{7,6},{8,9},{9,8},{10,11... | collective-permute-start | bytes 3145736 | tf_op jit(solution)/shard_map/ppermute | solution.py:809
  134.1 118.5 %reduce-scatter.4.cloned.1.call-start = ((), (), s32[]{:S(2)}) async-start(), calls=%async_computation.5 | async-start | bytes 839680 | tf_op jit(solution)/shard_map/reduce_scatter | solution.py:999
  134.2 10.6 %collective-permute-start.23 = (bf16[328,1024]{1,0:T(8,128)(2,1)}, bf16[328,1024]{1,0:T(8,128)(2,1)S(1)}, u32[]{:S(2)}, u32[]{:S(2)}) collective-permute-start(bf16[328,1024]{1,0:T(8,128)(2,1)} %param.13), channel_id=1, source_target_pairs={{0,0},{16,1},{8,2},{24,3},{1,8},{17,9},{9,10},{25,11},{2,16},{18,1... | collective-permute-start | bytes 2015240 | tf_op jit(solution)/shard_map/ppermute | solution.py:826
  136.5 6.9 %collective-permute-start.22 = (bf16[1,2,128,1024]{3,2,1,0:T(8,128)(2,1)}, bf16[1,2,128,1024]{3,2,1,0:T(8,128)(2,1)S(1)}, u32[]{:S(2)}, u32[]{:S(2)}) collective-permute-start(bf16[1,2,128,1024]{3,2,1,0:T(8,128)(2,1)} %collective-permute-done.18), channel_id=1, source_target_pairs={{0,1},{1,0},{2,3},{3,2},{4,5},{5,4},{6,7},{7,6},{8,9},{9,8},{10,11... | collective-permute-start | bytes 1572872 | tf_op jit(solution)/shard_map/ppermute | solution.py:809
  139.5 14.9 %collective-permute-start.20 = (bf16[2,2,128,1024]{3,2,1,0:T(8,128)(2,1)S(1)}, bf16[2,2,128,1024]{3,2,1,0:T(8,128)(2,1)S(1)}, u32[]{:S(2)}, u32[]{:S(2)}) collective-permute-start(bf16[2,2,128,1024]{3,2,1,0:T(8,128)(2,1)S(1)} %pad_maximum_fusion.2), channel_id=1, source_target_pairs={{0,4},{1,3},{2,6},{3,1},{4,0},{5,7},{6,2},{7,5},{8,12},{9,11},{10,... | collective-permute-start | bytes 3145736 | tf_op jit(solution)/shard_map/ppermute | solution.py:815
  154.5 44.9 %collective-permute-start.24 = (bf16[1,2,128,1024]{3,2,1,0:T(8,128)(2,1)S(1)}, bf16[1,2,128,1024]{3,2,1,0:T(8,128)(2,1)S(1)}, u32[]{:S(2)}, u32[]{:S(2)}) collective-permute-start(bf16[1,2,128,1024]{3,2,1,0:T(8,128)(2,1)S(1)} %slice.197), channel_id=1, source_target_pairs={{0,2},{1,5},{2,0},{3,7},{4,6},{5,1},{6,4},{7,3},{8,10},{9,13},{10,... | collective-permute-start | bytes 1572872 | tf_op jit(solution)/shard_map/ppermute | solution.py:818
  175.3 32.3 %collective-permute-start.25 = (bf16[2,2,128,1024]{3,2,1,0:T(8,128)(2,1)S(1)}, bf16[2,2,128,1024]{3,2,1,0:T(8,128)(2,1)S(1)}, u32[]{:S(2)}, u32[]{:S(2)}) collective-permute-start(bf16[2,2,128,1024]{3,2,1,0:T(8,128)(2,1)S(1)} %collective-permute-done.20.refs_2_), channel_id=1, source_target_pairs={{0,1},{1,0},{2,3},{3,2},{4,5},{5,4},{6,7},{7,6},{8,9},{9,8},{10,11... | collective-permute-start | bytes 3145736 | tf_op jit(solution)/shard_map/ppermute | solution.py:809
  199.4 8.2 %collective-permute-start.26 = (bf16[1,2,128,1024]{3,2,1,0:T(8,128)(2,1)S(1)}, bf16[1,2,128,1024]{3,2,1,0:T(8,128)(2,1)S(1)}, u32[]{:S(2)}, u32[]{:S(2)}) collective-permute-start(bf16[1,2,128,1024]{3,2,1,0:T(8,128)(2,1)S(1)} %collective-permute-done.24.refs_3_), channel_id=1, source_target_pairs={{0,1},{1,0},{2,3},{3,2},{4,5},{5,4},{6,7},{7,6},{8,9},{9,8},{10,11... | collective-permute-start | bytes 1572872 | tf_op jit(solution)/shard_map/ppermute | solution.py:809
  226.3 26.3 %collective-permute-start.27 = (bf16[3,2,128,1024]{3,2,1,0:T(8,128)(2,1)}, bf16[3,2,128,1024]{3,2,1,0:T(8,128)(2,1)S(1)}, u32[]{:S(2)}, u32[]{:S(2)}) collective-permute-start(bf16[3,2,128,1024]{3,2,1,0:T(8,128)(2,1)} %get-tuple-element.115), channel_id=1, source_target_pairs={{0,1},{1,0},{2,3},{3,2},{4,5},{5,4},{6,7},{7,6},{8,9},{9,8},{10,11... | collective-permute-start | bytes 4718600 | tf_op jit(solution)/shard_map/ppermute | solution.py:809
  230.9 137.5 %reduce-scatter.8.cloned.1.call-start = ((), (), s32[]{:S(2)}) async-start(), calls=%async_computation.7 | async-start | bytes 1966080 | tf_op jit(solution)/shard_map/reduce_scatter | solution.py:999
  254.3 9.2 %collective-permute-start.28 = (bf16[2,128,1024]{2,1,0:T(8,128)(2,1)S(1)}, bf16[2,128,1024]{2,1,0:T(8,128)(2,1)S(1)}, u32[]{:S(2)}, u32[]{:S(2)}) collective-permute-start(bf16[2,128,1024]{2,1,0:T(8,128)(2,1)S(1)} %get-tuple-element.177), channel_id=1, source_target_pairs={{0,2},{1,5},{2,0},{3,7},{4,6},{5,1},{6,4},{7,3},{8,10},{9,13},{10,... | collective-permute-start | bytes 1572872 | tf_op jit(solution)/shard_map/ppermute | solution.py:818
  265.9 15.0 %collective-permute-start.30 = (bf16[2,2,128,1024]{3,2,1,0:T(8,128)(2,1)}, bf16[2,2,128,1024]{3,2,1,0:T(8,128)(2,1)S(1)}, u32[]{:S(2)}, u32[]{:S(2)}) collective-permute-start(bf16[2,2,128,1024]{3,2,1,0:T(8,128)(2,1)} %pad_maximum_fusion.3), channel_id=1, source_target_pairs={{0,4},{1,3},{2,6},{3,1},{4,0},{5,7},{6,2},{7,5},{8,12},{9,11},{10,... | collective-permute-start | bytes 3145736 | tf_op jit(solution)/shard_map/ppermute | solution.py:815
  267.4 34.2 %collective-permute-start.29 = (bf16[3,2,128,1024]{3,2,1,0:T(8,128)(2,1)}, bf16[3,2,128,1024]{3,2,1,0:T(8,128)(2,1)}, u32[]{:S(2)}, u32[]{:S(2)}) collective-permute-start(bf16[3,2,128,1024]{3,2,1,0:T(8,128)(2,1)} %bitcast.40), channel_id=1, source_target_pairs={{0,1},{1,0},{2,3},{3,2},{4,5},{5,4},{6,7},{7,6},{8,9},{9,8},{10,11... | collective-permute-start | bytes 4718600 | tf_op jit(solution)/shard_map/ppermute | solution.py:809
  282.2 2.0 collective-permute-start.31
  294.7 9.0 %collective-permute-start.32 = (bf16[3,128,1024]{2,1,0:T(8,128)(2,1)}, bf16[3,128,1024]{2,1,0:T(8,128)(2,1)S(1)}, u32[]{:S(2)}, u32[]{:S(2)}) collective-permute-start(bf16[3,128,1024]{2,1,0:T(8,128)(2,1)} %get-tuple-element.130), channel_id=1, source_target_pairs={{0,1},{1,0},{2,3},{3,2},{4,5},{5,4},{6,7},{7,6},{8,9},{9,8},{10,11... | collective-permute-start | bytes 2359304 | tf_op jit(solution)/shard_map/ppermute | solution.py:809
  297.6 12.6 %all-to-all-start.1 = ((bf16[8,2,128,128]{3,2,1,0:T(8,128)(2,1)}), bf16[8,2,128,128]{3,2,1,0:T(8,128)(2,1)S(1)}, u32[]{:S(2)}, u32[]{:S(2)}) async-start(bf16[8,2,128,128]{3,2,1,0:T(8,128)(2,1)} %get-tuple-element.125), calls=%async_computation.2 | async-start | bytes 1048576 | tf_op jit(solution)/shard_map/all_to_all | solution.py:892
  301.3 114.9 %reduce-scatter.6.cloned.1.call-start = ((), (), s32[]{:S(2)}) async-start(), calls=%async_computation.6 | async-start | bytes 983040 | tf_op jit(solution)/shard_map/reduce_scatter | solution.py:999
  310.2 17.3 %collective-permute-start.33 = (bf16[2,128,1024]{2,1,0:T(8,128)(2,1)}, bf16[2,128,1024]{2,1,0:T(8,128)(2,1)S(1)}, u32[]{:S(2)}, u32[]{:S(2)}) collective-permute-start(bf16[2,128,1024]{2,1,0:T(8,128)(2,1)} %fusion.17), channel_id=1, source_target_pairs={{0,2},{1,5},{2,0},{3,7},{4,6},{5,1},{6,4},{7,3},{8,10},{9,13},{10,... | collective-permute-start | bytes 1572872 | tf_op jit(solution)/shard_map/ppermute | solution.py:818
  311.8 15.6 %collective-permute-start.34 = (bf16[128,1024]{1,0:T(8,128)(2,1)S(1)}, bf16[128,1024]{1,0:T(8,128)(2,1)S(1)}, u32[]{:S(2)}, u32[]{:S(2)}) collective-permute-start(bf16[128,1024]{1,0:T(8,128)(2,1)S(1)} %get-tuple-element.133), channel_id=1, source_target_pairs={{0,2},{1,5},{2,0},{3,7},{4,6},{5,1},{6,4},{7,3},{8,10},{9,13},{10,... | collective-permute-start | bytes 786440 | tf_op jit(solution)/shard_map/ppermute | solution.py:818
  346.3 1.2 collective-permute-start.53
  347.6 4.8 %collective-permute-start.54 = (f32[16,128]{1,0:T(8,128)S(1)}, f32[16,128]{1,0:T(8,128)S(1)}, u32[]{:S(2)}, u32[]{:S(2)}) collective-permute-start(f32[16,128]{1,0:T(8,128)S(1)} %add.451), channel_id=1, source_target_pairs={{0,2},{1,3},{2,0},{3,1},{4,6},{5,7},{6,4},{7,5},{8,10},{9,11},{10,... | collective-permute-start | bytes 24584 | tf_op jit(solution)/shard_map/ppermute | solution.py:809
  349.3 3.7 collective-permute-start.52
  350.2 23.6 %collective-permute-start.36 = (bf16[3,1,128,1024]{3,2,1,0:T(8,128)(2,1)}, bf16[3,1,128,1024]{3,2,1,0:T(8,128)(2,1)}, u32[]{:S(2)}, u32[]{:S(2)}) collective-permute-start(bf16[3,1,128,1024]{3,2,1,0:T(8,128)(2,1)} %get-tuple-element.138), channel_id=1, source_target_pairs={{0,1},{1,0},{2,3},{3,2},{4,5},{5,4},{6,7},{7,6},{8,9},{9,8},{10,11... | collective-permute-start | bytes 2359304 | tf_op jit(solution)/shard_map/ppermute | solution.py:809
  352.4 3.7 collective-permute-start.55
  356.0 7.8 %collective-permute-start.56 = (f32[16,128]{1,0:T(8,128)S(1)}, f32[16,128]{1,0:T(8,128)S(1)}, u32[]{:S(2)}, u32[]{:S(2)}) collective-permute-start(f32[16,128]{1,0:T(8,128)S(1)} %add.453), channel_id=1, source_target_pairs={{0,8},{8,0},{16,24},{24,16},{1,9},{9,1},{17,25},{25,17},{2,10},{10... | collective-permute-start | bytes 24584 | tf_op jit(solution)/shard_map/ppermute | solution.py:837
  361.8 35.4 %collective-permute-start.35 = (bf16[2,2,128,1024]{3,2,1,0:T(8,128)(2,1)S(1)}, bf16[2,2,128,1024]{3,2,1,0:T(8,128)(2,1)}, u32[]{:S(2)}, u32[]{:S(2)}) collective-permute-start(bf16[2,2,128,1024]{3,2,1,0:T(8,128)(2,1)S(1)} %pad_maximum_fusion.4), channel_id=1, source_target_pairs={{0,4},{1,3},{2,6},{3,1},{4,0},{5,7},{6,2},{7,5},{8,12},{9,11},{10,... | collective-permute-start | bytes 3145736 | tf_op jit(solution)/shard_map/ppermute | solution.py:815
  361.8 34.1 %collective-permute-start.45 = (bf16[2,128,1024]{2,1,0:T(8,128)(2,1)}, bf16[2,128,1024]{2,1,0:T(8,128)(2,1)}, u32[]{:S(2)}, u32[]{:S(2)}) collective-permute-start(bf16[2,128,1024]{2,1,0:T(8,128)(2,1)} %pad_maximum_fusion.7), channel_id=1, source_target_pairs={{0,4},{1,3},{2,6},{3,1},{4,0},{5,7},{6,2},{7,5},{8,12},{9,11},{10,... | collective-permute-start | bytes 1572872 | tf_op jit(solution)/shard_map/ppermute | solution.py:815
  363.8 27.8 %collective-permute-start.37 = (bf16[3,1,128,1024]{3,2,1,0:T(8,128)(2,1)}, bf16[3,1,128,1024]{3,2,1,0:T(8,128)(2,1)}, u32[]{:S(2)}, u32[]{:S(2)}) collective-permute-start(bf16[3,1,128,1024]{3,2,1,0:T(8,128)(2,1)} %get-tuple-element.147), channel_id=1, source_target_pairs={{0,1},{1,0},{2,3},{3,2},{4,5},{5,4},{6,7},{7,6},{8,9},{9,8},{10,11... | collective-permute-start | bytes 2359304 | tf_op jit(solution)/shard_map/ppermute | solution.py:809
  363.8 4.6 %collective-permute-start.57 = (f32[16,128]{1,0:T(8,128)S(1)}, f32[16,128]{1,0:T(8,128)S(1)}, u32[]{:S(2)}, u32[]{:S(2)}) collective-permute-start(f32[16,128]{1,0:T(8,128)S(1)} %add.454), channel_id=1, source_target_pairs={{0,16},{8,24},{16,0},{24,8},{1,17},{9,25},{17,1},{25,9},{2,18},{10... | collective-permute-start | bytes 24584 | tf_op jit(solution)/shard_map/ppermute | solution.py:837
  372.0 15.5 %collective-permute-start.50 = (bf16[128,768]{0,1:T(8,128)(2,1)}, bf16[128,768]{0,1:T(8,128)(2,1)}, u32[]{:S(2)}, u32[]{:S(2)}) collective-permute-start(bf16[128,768]{0,1:T(8,128)(2,1)} %bitcast.234), channel_id=1, source_target_pairs={{0,4},{4,0},{1,5},{5,1},{2,6},{6,2},{3,7},{7,3},{8,12},{12,8},{9,1... | collective-permute-start | bytes 589832 | tf_op jit(solution)/shard_map/ppermute | solution.py:808
  388.8 6.2 %collective-permute-start.51 = (bf16[2,128,328]{1,2,0:T(8,128)(2,1)S(1)}, bf16[2,128,328]{1,2,0:T(8,128)(2,1)S(1)}, u32[]{:S(2)}, u32[]{:S(2)}) collective-permute-start(bf16[2,128,328]{1,2,0:T(8,128)(2,1)S(1)} %get-tuple-element.204), channel_id=1, source_target_pairs={{0,2},{1,3},{2,0},{3,1},{4,6},{5,7},{6,4},{7,5},{8,10},{9,11},{10,... | collective-permute-start | bytes 503816 | tf_op jit(solution)/shard_map/ppermute | solution.py:809
  393.1 9.6 %collective-permute-start.39 = (bf16[2,128,1024]{2,1,0:T(8,128)(2,1)S(1)}, bf16[2,128,1024]{2,1,0:T(8,128)(2,1)S(1)}, u32[]{:S(2)}, u32[]{:S(2)}) collective-permute-start(bf16[2,128,1024]{2,1,0:T(8,128)(2,1)S(1)} %pad_maximum_fusion.8), channel_id=1, source_target_pairs={{0,2},{1,5},{2,0},{3,7},{4,6},{5,1},{6,4},{7,3},{8,10},{9,13},{10,... | collective-permute-start | bytes 1572872 | tf_op jit(solution)/shard_map/ppermute | solution.py:818
  397.0 8.4 %collective-permute-start.46 = (bf16[128,1024]{1,0:T(8,128)(2,1)S(1)}, bf16[128,1024]{1,0:T(8,128)(2,1)S(1)}, u32[]{:S(2)}, u32[]{:S(2)}) collective-permute-start(bf16[128,1024]{1,0:T(8,128)(2,1)S(1)} %fusion.38), channel_id=1, source_target_pairs={{0,1},{1,0},{2,3},{3,2},{4,5},{5,4},{6,7},{7,6},{8,9},{9,8},{10,11... | collective-permute-start | bytes 786440 | tf_op jit(solution)/shard_map/ppermute | solution.py:809
  403.8 21.8 %collective-permute-start.40 = (bf16[2,2,128,1024]{3,2,1,0:T(8,128)(2,1)}, bf16[2,2,128,1024]{3,2,1,0:T(8,128)(2,1)S(1)}, u32[]{:S(2)}, u32[]{:S(2)}) collective-permute-start(bf16[2,2,128,1024]{3,2,1,0:T(8,128)(2,1)} %pad_maximum_fusion.5), channel_id=1, source_target_pairs={{0,4},{1,3},{2,6},{3,1},{4,0},{5,7},{6,2},{7,5},{8,12},{9,11},{10,... | collective-permute-start | bytes 3145736 | tf_op jit(solution)/shard_map/ppermute | solution.py:815
  407.0 5.9 %collective-permute-start.47 = (bf16[2,128,256]{2,1,0:T(8,128)(2,1)S(1)}, bf16[2,128,256]{2,1,0:T(8,128)(2,1)S(1)}, u32[]{:S(2)}, u32[]{:S(2)}) collective-permute-start(bf16[2,128,256]{2,1,0:T(8,128)(2,1)S(1)} %fusion.48), channel_id=1, source_target_pairs={{0,16},{8,24},{16,0},{24,8},{1,17},{9,25},{17,1},{25,9},{2,18},{10... | collective-permute-start | bytes 393224 | tf_op jit(solution)/shard_map/ppermute | solution.py:837
  410.0 13.8 %collective-permute-start.38 = (bf16[2,128,1024]{2,1,0:T(8,128)(2,1)}, bf16[2,128,1024]{2,1,0:T(8,128)(2,1)}, u32[]{:S(2)}, u32[]{:S(2)}) collective-permute-start(bf16[2,128,1024]{2,1,0:T(8,128)(2,1)} %fusion.13), channel_id=1, source_target_pairs={{0,1},{1,0},{2,3},{3,2},{4,5},{5,4},{6,7},{7,6},{8,9},{9,8},{10,11... | collective-permute-start | bytes 1572872 | tf_op jit(solution)/shard_map/ppermute | solution.py:809
  414.3 5.8 %collective-permute-start.48 = (bf16[1,128,256]{2,1,0:T(8,128)(2,1)}, bf16[1,128,256]{2,1,0:T(8,128)(2,1)}, u32[]{:S(2)}, u32[]{:S(2)}) collective-permute-start(bf16[1,128,256]{2,1,0:T(8,128)(2,1)} %dynamic-slice_convert_fusion.1), channel_id=1, source_target_pairs={{0,8},{8,0},{16,24},{24,16},{1,9},{9,1},{17,25},{25,17},{2,10},{10... | collective-permute-start | bytes 196616 | tf_op jit(solution)/shard_map/ppermute | solution.py:837
  419.5 5.0 %collective-permute-start.42 = (bf16[128,384]{0,1:T(8,128)(2,1)}, bf16[128,384]{0,1:T(8,128)(2,1)}, u32[]{:S(2)}, u32[]{:S(2)}) collective-permute-start(bf16[128,384]{0,1:T(8,128)(2,1)} %bitcast.237), channel_id=1, source_target_pairs={{0,4},{4,0},{1,5},{5,1},{2,6},{6,2},{3,7},{7,3},{8,12},{12,8},{9,1... | collective-permute-start | bytes 294920 | tf_op jit(solution)/shard_map/ppermute | solution.py:808
  421.7 11.4 %collective-permute-start.49 = (bf16[128,256]{1,0:T(8,128)(2,1)}, bf16[128,256]{1,0:T(8,128)(2,1)}, u32[]{:S(2)}, u32[]{:S(2)}) collective-permute-start(bf16[128,256]{1,0:T(8,128)(2,1)} %fusion.49), channel_id=1, source_target_pairs={{0,0},{1,8},{2,16},{3,24},{8,1},{9,9},{10,17},{11,25},{16,2},{17,1... | collective-permute-start | bytes 196616 | tf_op jit(solution)/shard_map/ppermute | solution.py:834
  427.6 8.0 %collective-permute-start.41 = (bf16[2,128,1024]{2,1,0:T(8,128)(2,1)}, bf16[2,128,1024]{2,1,0:T(8,128)(2,1)}, u32[]{:S(2)}, u32[]{:S(2)}) collective-permute-start(bf16[2,128,1024]{2,1,0:T(8,128)(2,1)} %fusion.10), channel_id=1, source_target_pairs={{0,1},{1,0},{2,3},{3,2},{4,5},{5,4},{6,7},{7,6},{8,9},{9,8},{10,11... | collective-permute-start | bytes 1572872 | tf_op jit(solution)/shard_map/ppermute | solution.py:809
  428.3 6.4 %collective-permute-start.43 = (bf16[2,128,128]{1,2,0:T(8,128)(2,1)S(1)}, bf16[2,128,128]{1,2,0:T(8,128)(2,1)S(1)}, u32[]{:S(2)}, u32[]{:S(2)}) collective-permute-start(bf16[2,128,128]{1,2,0:T(8,128)(2,1)S(1)} %get-tuple-element.207), channel_id=1, source_target_pairs={{0,1},{1,0},{2,3},{3,2},{4,5},{5,4},{6,7},{7,6},{8,9},{9,8},{10,11... | collective-permute-start | bytes 196616 | tf_op jit(solution)/shard_map/ppermute | solution.py:809
  428.4 6.3 %collective-permute-start.44 = (bf16[2,128,128]{1,2,0:T(8,128)(2,1)S(1)}, bf16[2,128,128]{1,2,0:T(8,128)(2,1)S(1)}, u32[]{:S(2)}, u32[]{:S(2)}) collective-permute-start(bf16[2,128,128]{1,2,0:T(8,128)(2,1)S(1)} %get-tuple-element.206), channel_id=1, source_target_pairs={{0,2},{1,3},{2,0},{3,1},{4,6},{5,7},{6,4},{7,5},{8,10},{9,11},{10,... | collective-permute-start | bytes 196616 | tf_op jit(solution)/shard_map/ppermute | solution.py:809
  (37 other events, 385.7 us)
Sparse Core Ops, SparseCore 0:
  134.2 59.5 all-gather.2
  231.1 21.5 reduce-scatter.3
  297.7 34.1 reduce-scatter.7
  366.6 23.5 reduce-scatter.5
